TPU v7x, 256 devices: a whole 4x4x8 slice. The times are simulated.
256 devices in a mesh: ctx: 64 (over z, x, core), tp: 4 (over y).
Axes of the slice: x: 4, y: 4, z: 8, core: 2. Of those that a mesh axis runs over, the one named last changes fastest.
Arguments:
- context: bfloat16 [16384, 4096], P('ctx', 'tp'), may hold values from -6 to 6
- key_weight: bfloat16 [4096, 2048], P(None, 'tp'), may hold values from -0.09375 to 0.09375
- value_weight: bfloat16 [4096, 2048], P(None, 'tp'), may hold values from -0.09375 to 0.09375
- queries: bfloat16 [2048, 2048], P('ctx', 'tp'), may hold values from -64 to 64
- latent_pos: int32 [2048], replicated, may hold values from 0 to 16383, as said below
- out_grad: bfloat16 [2048, 2048], P('ctx', 'tp'), may hold values from -6 to 6
Outputs:
- attended: bfloat16 [2048, 2048], P('ctx', 'tp')
- context_grad: bfloat16 [16384, 4096], P('ctx', 'tp')
- query_grad: bfloat16 [2048, 2048], P('ctx', 'tp')
Inputs may be any that keep to these rules, and one draw needn't show every extreme that they name: `latent_pos`: some latent sees the whole context and some latent sees only position 0.
All inputs are finite; a program needn't handle non-finite values.
Results may differ from a plain program's by a relative error of at most 0.025.
The roundings to bfloat16 on the way count: a program that leaves them out, or rounds other values in their place, can miss the bound.
Values may be sent and summed in bfloat16 or wider, within the bound.
No kernel may reach another device: no remote copies, remote signals or barrier semaphores. Data moves between devices by JAX's collectives and lax.ppermute only.
A program may use at most 128 MiB of HBM per device.

v0:
```python
import math

import jax
import jax.numpy as jnp
from jax import lax
from jax.sharding import PartitionSpec as P

DH = 128


NEG_FILL = -1e30


def shards(context, key_weight, value_weight, queries, latent_pos, out_grad):
    tok_rows = context.shape[0]
    head_cols = key_weight.shape[1]
    local_heads = head_cols // DH
    lat_rows = queries.shape[0]
    latents = lat_rows * lax.axis_size("ctx")
    score_scale = 1.0 / math.sqrt(DH)
    gathered_part = lax.all_gather(context, "tp", axis=1, tiled=True)
    key_sum = jnp.dot(gathered_part, key_weight, preferred_element_type=jnp.float32)
    value_sum = jnp.dot(gathered_part, value_weight, preferred_element_type=jnp.float32)
    key_rows = key_sum.astype(jnp.bfloat16).reshape(tok_rows, local_heads, DH)
    value_rows = value_sum.astype(jnp.bfloat16).reshape(tok_rows, local_heads, DH)
    all_queries = lax.all_gather(queries, "ctx", axis=0, tiled=True).reshape(
        latents, local_heads, DH
    )
    positions = lax.axis_index("ctx") * tok_rows + jnp.arange(tok_rows, dtype=jnp.int32)
    allowed = (positions[None, :] <= latent_pos[:, None])[None]
    scores = (
        jnp.einsum("lhd,thd->hlt", all_queries, key_rows, preferred_element_type=jnp.float32)
        * score_scale
    )
    local_peak = jnp.max(jnp.where(allowed, scores, NEG_FILL), axis=2)
    row_peak = lax.pmax(local_peak, "ctx")
    expo = jnp.where(allowed, jnp.exp(scores - row_peak[:, :, None]), 0.0)
    part_denominator = jnp.sum(expo, axis=2).T
    part_numer = jnp.einsum(
        "hlt,thd->lhd", expo.astype(jnp.bfloat16), value_rows, preferred_element_type=jnp.float32
    ).reshape(latents, head_cols)
    own_first = lax.axis_index("ctx") * lat_rows
    all_grads = lax.all_gather(out_grad, "ctx", axis=0, tiled=True)
    grads_three = all_grads.reshape(latents, local_heads, DH)
    numer_sum, denominator = lax.psum((part_numer, part_denominator), "ctx")
    attended_all = (numer_sum.reshape(latents, local_heads, DH) / denominator[:, :, None]).astype(
        jnp.bfloat16
    )
    attended = lax.dynamic_slice_in_dim(
        attended_all.reshape(latents, head_cols), own_first, lat_rows, 0
    )
    log_norm = row_peak.T + jnp.log(denominator)
    grad_dot = jnp.sum(grads_three.astype(jnp.float32) * attended_all.astype(jnp.float32), axis=2)
    probabilities = jnp.where(allowed, jnp.exp(scores - log_norm.T[:, :, None]), 0.0)
    value_grad = (
        jnp.einsum(
            "hlt,lhd->thd",
            probabilities.astype(jnp.bfloat16),
            grads_three,
            preferred_element_type=jnp.float32,
        )
        .astype(jnp.bfloat16)
        .reshape(tok_rows, head_cols)
    )
    prob_grad = jnp.einsum(
        "lhd,thd->hlt", grads_three, value_rows, preferred_element_type=jnp.float32
    )
    score_grad = (probabilities * (prob_grad - grad_dot.T[:, :, None]) * score_scale).astype(
        jnp.bfloat16
    )
    key_grad = (
        jnp.einsum("hlt,lhd->thd", score_grad, all_queries, preferred_element_type=jnp.float32)
        .astype(jnp.bfloat16)
        .reshape(tok_rows, head_cols)
    )
    query_grad = lax.psum_scatter(
        jnp.einsum(
            "hlt,thd->lhd", score_grad, key_rows, preferred_element_type=jnp.float32
        ).reshape(lax.axis_size("ctx") * lat_rows, head_cols),
        "ctx",
        scatter_dimension=0,
        tiled=True,
    ).astype(jnp.bfloat16)
    contract_cols = (((1,), (1,)), ((), ()))
    input_terms = lax.dot_general(
        key_grad, key_weight, contract_cols, preferred_element_type=jnp.float32
    ) + lax.dot_general(value_grad, value_weight, contract_cols, preferred_element_type=jnp.float32)
    context_grad = lax.psum_scatter(input_terms, "tp", scatter_dimension=1, tiled=True).astype(
        jnp.bfloat16
    )
    return (attended, context_grad, query_grad)


def solution(mesh):
    return jax.shard_map(
        shards,
        mesh=mesh,
        in_specs=(
            P("ctx", "tp"),
            P(None, "tp"),
            P(None, "tp"),
            P("ctx", "tp"),
            P(),
            P("ctx", "tp"),
        ),
        out_specs=(P("ctx", "tp"), P("ctx", "tp"), P("ctx", "tp")),
        check_vma=False,
    )
```

profile of v0, /device:TPU:1, one launch (start us, length us, event | category | flops | bytes accessed | tf_op | source)
XLA Modules:
  0.0 862.9 jit_solution(17949799306412070403)
XLA Ops:
  7.2 0.7 all-gather.4.cloned.1.call-update
  7.9 0.7 all-gather.6.cloned.1.call-update
  8.7 0.7 all-gather.8.cloned.1.call-update
  9.4 1.1 broadcast_compare_fusion
  10.5 36.5 %all-gather.4.cloned.1.call-done = bf16[256,4096]{1,0:T(8,128)(2,1)} async-done(((bf16[256,1024]{1,0:T(8,128)(2,1)}), bf16[256,4096]{1,0:T(8,128)(2,1)}) %all-gather.4.cloned.1.call-update) | async-done | bytes 2097168 | tf_op jit(solution)/shard_map/all_gather | solution.py:21
  47.1 4.1 convolution_convert_fusion.1
  51.3 4.1 fusion.22
  55.3 72.2 %all-gather.6.cloned.1.call-done = bf16[2048,512]{1,0:T(8,128)(2,1)} async-done(((bf16[32,512]{1,0:T(8,128)(2,1)}), bf16[2048,512]{1,0:T(8,128)(2,1)}) %all-gather.6.cloned.1.call-update) | async-done | bytes 2097168 | tf_op jit(solution)/shard_map/all_gather | solution.py:26
  127.5 2.9 copy.35
  130.4 5.2 fusion.2
  135.6 243.5 %pmax.7 = f32[4,2048]{1,0:T(4,128)S(1)} all-reduce(f32[4,2048]{1,0:T(4,128)S(1)} %get-tuple-element.9), channel_id=1, replica_groups=mesh['ctx'=64,'tp'=4] {'ctx'}, use_global_device_ids=true, to_apply=%region_1.2 | all-reduce | flops 8192 | bytes 65536 | tf_op jit(solution)/shard_map/pmax | solution.py:36
  379.1 7.3 fusion.10
  386.4 2.9 copy.40
  389.4 4.4 fusion.8
  393.8 246.5 %psum.15 = f32[2048,4]{0,1:T(4,128)S(1)} all-reduce(f32[2048,4]{0,1:T(4,128)S(1)} %bitcast.93), channel_id=1, replica_groups=mesh['ctx'=64,'tp'=4] {'ctx'}, use_global_device_ids=true, to_apply=%region_4.5 | all-reduce | flops 8192 | bytes 65536 | tf_op jit(solution)/shard_map/psum | solution.py:45
  640.3 2.9 multiply_reduce_fusion
  643.2 5.5 fusion.1
  648.8 3.1 fusion.34
  651.9 5.4 copy.47
  657.6 5.4 fusion.19
  663.0 1.5 convolution_convert_fusion
  664.6 0.6 copy-done.5
  665.2 1.3 fusion.33
  666.5 0.9 copy-done.4
  667.4 3.3 convolution_add_fusion
  670.7 0.5 div.13
  671.2 1.2 fusion.25
  672.4 0.7 copy.48
  673.1 125.6 %reduce-scatter.5.cloned.1.call-done = f32[32,512]{1,0:T(8,128)} async-done(((f32[2048,512]{1,0:T(8,128)}), f32[32,512]{1,0:T(8,128)}) %reduce-scatter.5.cloned.1.call-update) | async-done | bytes 65552 | tf_op jit(solution)/shard_map/reduce_scatter | solution.py:76
  798.7 1.5 convert_element_type.59
  800.1 53.8 %reduce-scatter.3.cloned.1.call-done = f32[256,1024]{1,0:T(8,128)} async-done(((f32[256,4096]{1,0:T(8,128)}), f32[256,1024]{1,0:T(8,128)}) %reduce-scatter.3.cloned.1.call-update) | async-done | bytes 1048592 | tf_op jit(solution)/shard_map/reduce_scatter | solution.py:88
  853.9 2.1 convert_element_type.58
  (24 shorter events, 0.8 us)
Async XLA Ops:
  7.2 39.9 %all-gather.4.cloned.1.call-start = ((), (), s32[]{:S(2)}) async-start(), calls=%async_computation.2 | async-start | bytes 2621440 | tf_op jit(solution)/shard_map/all_gather | solution.py:21
  7.9 119.6 %all-gather.6.cloned.1.call-start = ((), (), s32[]{:S(2)}) async-start(), calls=%async_computation.3 | async-start | bytes 2129920 | tf_op jit(solution)/shard_map/all_gather | solution.py:26
  8.6 377.8 %all-gather.8.cloned.1.call-start = ((), (), s32[]{:S(2)}) async-start(), calls=%async_computation.5 | async-start | bytes 2129920 | tf_op jit(solution)/shard_map/all_gather | solution.py:43
  9.4 630.9 %all-reduce.2.cloned.1.call-start = ((), (), s32[]{:S(2)}) async-start(), calls=%async_computation.4 | async-start | bytes 8388608 | tf_op jit(solution)/shard_map/psum | solution.py:45
  130.4 5.2 copy-start.2
  386.3 412.3 %reduce-scatter.5.cloned.1.call-start = ((), (), s32[]{:S(2)}) async-start(), calls=%async_computation.7 | async-start | bytes 4259840 | tf_op jit(solution)/shard_map/reduce_scatter | solution.py:76
  648.7 3.2 copy-start
  657.3 196.6 %reduce-scatter.3.cloned.1.call-start = ((), (), s32[]{:S(2)}) async-start(), calls=%async_computation.6 | async-start | bytes 5242880 | tf_op jit(solution)/shard_map/reduce_scatter | solution.py:88
  657.6 5.4 copy-start.1
  657.6 5.4 copy-start.3
  663.0 2.2 copy-start.5
  665.2 2.2 copy-start.4
Sparse Core Ops, SparseCore 0:
  9.8 37.2 all-gather.3
  49.8 77.6 all-gather.5
  130.3 74.9 all-gather.7
  386.5 196.7 all-reduce.1
  657.4 141.1 reduce-scatter.4
  801.1 52.8 reduce-scatter.2
where the time goes:
time: 864 us; the launch traced here: 863 us
  blocking collectives  490 us (57%)
  waiting for transfers between devices  290 us (34%)
  matrix products  40.7 us (5%)
  between operations  14.3 us (2%)
  local copies, waits for them, and re-layouts  14.2 us (2%)
  other arithmetic  13.1 us (2%)
    psum x1, blocking collectives, shards(): numer_sum, denominator = lax.psum((part_numer, part_denominator), 'ctx')  246 us
    pmax x1, blocking collectives, shards(): row_peak = lax.pmax(local_peak, 'ctx')  243 us
    reduce_scatter x1, waiting for transfers between devices, shards(): lax.psum_scatter(jnp.einsum('hlt,thd->lhd', score_grad, key_rows, preferr...  126 us
    all_gather x1, waiting for transfers between devices, shards(): lax.all_gather(queries, 'ctx', axis=0, tiled=True)  72.2 us
    reduce_scatter x1, waiting for transfers between devices, shards(): lax.psum_scatter(input_terms, 'tp', scatter_dimension=1, tiled=True)  53.8 us
    all_gather x1, waiting for transfers between devices, shards(): gathered_part = lax.all_gather(context, 'tp', axis=1, tiled=True)  36.5 us
  transfers between devices with their start and end apart: 6, of which 4 were waited for; matrix products, arithmetic and copies ran while one was open for 5% of the time, Pallas kernels for 0%

commit v1 on v0

v1 whole, which is shorter than its diff:
```python
import functools
import math

import jax
import jax.numpy as jnp
from jax import lax
from jax.experimental import pallas as pl
from jax.experimental.pallas import tpu as pltpu
from jax.sharding import PartitionSpec as P

DH = 128
NZ, NX, NC, NY = 8, 4, 2, 4
NEG_FILL = -1e30
SCORE_SCALE = 1.0 / math.sqrt(DH)
LOG2_SCALE = SCORE_SCALE * math.log2(math.e)
VMEM_LIMIT = 56 * 1024 * 1024
F32 = jnp.float32
BF16 = jnp.bfloat16
NT = (((1,), (1,)), ((), ()))


def place(z, x, c):
    return (z * NX + x) * NC + c


CORE_SWAP = [
    (place(z, x, c), place(z, x, 1 - c)) for z in range(NZ) for x in range(NX) for c in range(NC)
]
X_GROUPS = [[place(z, x, c) for x in range(NX)] for z in range(NZ) for c in range(NC)]
Z_GROUPS = [[place(z, x, c) for z in range(NZ)] for x in range(NX) for c in range(NC)]
ZX_GROUPS = [[place(z, x, c) for z in range(NZ) for x in range(NX)] for c in range(NC)]


def swap_cores(array):
    return lax.ppermute(array, "ctx", CORE_SWAP)


def shift_y(array, step):
    return lax.ppermute(array, "tp", [(i, (i + step) % NY) for i in range(NY)])


def exchange(array, groups):
    return lax.all_to_all(array, "ctx", 0, 0, tiled=True, axis_index_groups=groups)


def compiler_params(**kw):
    return pltpu.CompilerParams(vmem_limit_bytes=VMEM_LIMIT, **kw)


def project_kernel(first, last, chunk_ref, x_ref, wk_ref, wv_ref, *refs):
    if first:
        out_ref, acc_ref = refs
    else:
        sum_ref, out_ref, acc_ref = refs
    step = pl.program_id(0)
    cols = wk_ref.shape[1]

    @pl.when(step == 0)
    def _():
        acc_ref[...] = jnp.zeros_like(acc_ref) if first else sum_ref[...]

    x = x_ref[...]
    acc_ref[:, :cols] += jnp.dot(x, wk_ref[...], preferred_element_type=F32)
    acc_ref[:, cols:] += jnp.dot(x, wv_ref[...], preferred_element_type=F32)

    @pl.when(step == pl.num_programs(0) - 1)
    def _():
        if last:
            for head in range(cols // DH):
                for kind in range(2):
                    at = kind * cols + head * DH
                    out_ref[head, kind] = acc_ref[:, at : at + DH].astype(BF16)
        else:
            out_ref[...] = acc_ref[...]


def project(chunk, x, wk, wv, total, last):
    rows, depth = x.shape
    cols = wk.shape[1]
    steps = 2
    tile = depth // steps
    first = total is None
    in_specs = [
        pl.BlockSpec((rows, tile), lambda i, ch: (0, i)),
        pl.BlockSpec((tile, cols), lambda i, ch: (ch[0] * steps + i, 0)),
        pl.BlockSpec((tile, cols), lambda i, ch: (ch[0] * steps + i, 0)),
    ]
    args = [x, wk, wv]
    if not first:
        in_specs.append(pl.BlockSpec((rows, 2 * cols), lambda i, ch: (0, 0)))
        args.append(total)
    if last:
        out_shape = jax.ShapeDtypeStruct((cols // DH, 2, rows, DH), BF16)
        out_spec = pl.BlockSpec((cols // DH, 2, rows, DH), lambda i, ch: (0, 0, 0, 0))
    else:
        out_shape = jax.ShapeDtypeStruct((rows, 2 * cols), F32)
        out_spec = pl.BlockSpec((rows, 2 * cols), lambda i, ch: (0, 0))
    return pl.pallas_call(
        functools.partial(project_kernel, first, last),
        out_shape=out_shape,
        grid_spec=pltpu.PrefetchScalarGridSpec(
            num_scalar_prefetch=1,
            grid=(steps,),
            in_specs=in_specs,
            out_specs=out_spec,
            scratch_shapes=[pltpu.VMEM((rows, 2 * cols), F32)],
        ),
        compiler_params=compiler_params(),
        cost_estimate=pl.CostEstimate(
            flops=4 * rows * depth * cols, bytes_accessed=4 * depth * cols, transcendentals=0
        ),
        name="project",
    )(chunk, *args)


BLOCK = 256


def masked_scores(base, kv_ref, q, lp):
    parts, rows = kv_ref.shape[0], kv_ref.shape[2]
    out = []
    for part in range(parts):
        scores = lax.dot_general(kv_ref[part, 0], q, NT, preferred_element_type=F32) * LOG2_SCALE
        rank = lax.broadcasted_iota(jnp.int32, (rows, BLOCK), 0)
        limit = lp - (base + part * NC * rows)
        out.append(jnp.where(rank <= limit, scores, NEG_FILL))
    return out


def row_pair(ref, *index):
    *lead, row = index
    return jnp.concatenate([ref[(*lead, pl.ds(row + k, 1))] for k in range(BLOCK // 128)], axis=1)


def stats_kernel(base_ref, kv_ref, own_ref, other_ref, lp_ref, out_ref):
    base = base_ref[0]
    parts = kv_ref.shape[0]
    per = own_ref.shape[0] // BLOCK
    lanes = BLOCK // 128
    for half, src in enumerate((own_ref, other_ref)):
        for block in range(per):
            at = pl.ds(block * BLOCK, BLOCK)
            q = src[at, :DH]
            go = src[at, DH:]
            lp = row_pair(lp_ref, half, block * lanes)
            scores = masked_scores(base, kv_ref, q, lp)
            peak = functools.reduce(
                jnp.maximum, [jnp.max(s, axis=0, keepdims=True) for s in scores]
            )
            total = 0.0
            dots = 0.0
            for part in range(parts):
                expo = jnp.exp2(scores[part] - peak)
                grads = lax.dot_general(kv_ref[part, 1], go, NT, preferred_element_type=F32)
                total += jnp.sum(expo, axis=0, keepdims=True)
                dots += jnp.sum(expo * grads, axis=0, keepdims=True)
            seen = peak > 0.5 * NEG_FILL
            total = jnp.where(seen, total, 0.0)
            dots = jnp.where(seen, dots, 0.0)
            for kind, value in enumerate((peak, total, dots)):
                for k in range(lanes):
                    out_ref[kind, half, pl.ds(block * lanes + k, 1)] = value[
                        :, k * 128 : (k + 1) * 128
                    ]


def latent_stats(base, kv, own, other, lp):
    groups = own.shape[0] // 128
    whole = pl.BlockSpec(memory_space=pltpu.VMEM)
    tokens = kv.shape[0] * kv.shape[2]
    work = tokens * 2 * own.shape[0]
    return pl.pallas_call(
        stats_kernel,
        out_shape=jax.ShapeDtypeStruct((3, 2, groups, 128), F32),
        in_specs=[pl.BlockSpec(memory_space=pltpu.SMEM)] + [whole] * 4,
        out_specs=whole,
        compiler_params=compiler_params(),
        cost_estimate=pl.CostEstimate(
            flops=4 * work * DH, bytes_accessed=2 * 2**20, transcendentals=work
        ),
        name="latent_stats",
    )(base, kv, own, other, lp)


def backward_kernel(
    base_ref, kv_ref, own_ref, other_ref, lp_ref, st_ref, dkv_ref, own_out, other_out,
    kvt_ref, acc_ref, fin_ref,
):
    base = base_ref[0]
    parts, rows = kv_ref.shape[0], kv_ref.shape[2]
    per = own_ref.shape[0] // BLOCK
    lanes = BLOCK // 128
    for part in range(parts):
        at = pl.ds(part * rows, rows)
        for kind in range(2):
            kvt_ref[kind, :, at] = kv_ref[part, kind].T
    acc_ref[...] = jnp.zeros_like(acc_ref)

    peaks = [st_ref[n, 0] for n in range(NZ)]
    top = functools.reduce(jnp.maximum, peaks)
    total = 0.0
    dots = 0.0
    for n in range(NZ):
        share = jnp.exp2(peaks[n] - top)
        total += share * st_ref[n, 1]
        dots += share * st_ref[n, 2]
    fin_ref[0] = top
    fin_ref[1] = jnp.log2(total)
    fin_ref[2] = dots / total

    for half, (src, dst) in enumerate(((own_ref, own_out), (other_ref, other_out))):
        for block in range(per):
            at = pl.ds(block * BLOCK, BLOCK)
            q = src[at, :DH]
            go = src[at, DH:]
            lp = row_pair(lp_ref, half, block * lanes)
            peak = row_pair(fin_ref, 0, half, block * lanes)
            log_total = row_pair(fin_ref, 1, half, block * lanes)
            dot = row_pair(fin_ref, 2, half, block * lanes)
            scores = masked_scores(base, kv_ref, q, lp)
            attended = 0.0
            query_grad = 0.0
            for part in range(parts):
                rows_at = pl.ds(part * rows, rows)
                probs = jnp.exp2((scores[part] - peak) - log_total)
                low = probs.astype(BF16)
                grads = lax.dot_general(kv_ref[part, 1], go, NT, preferred_element_type=F32)
                score_grad = (probs * (grads - dot) * SCORE_SCALE).astype(BF16)
                acc_ref[part, 1] += jnp.dot(low, go, preferred_element_type=F32)
                acc_ref[part, 0] += jnp.dot(score_grad, q, preferred_element_type=F32)
                attended += jnp.dot(kvt_ref[1, :, rows_at], low, preferred_element_type=F32)
                query_grad += jnp.dot(kvt_ref[0, :, rows_at], score_grad, preferred_element_type=F32)
            dst[at, :DH] = attended.T.astype(dst.dtype)
            dst[at, DH:] = query_grad.T.astype(dst.dtype)
    dkv_ref[...] = acc_ref[...].astype(BF16)


def backward(base, kv, own, other, lp, stats):
    whole = pl.BlockSpec(memory_space=pltpu.VMEM)
    parts, _, rows, _ = kv.shape
    work = parts * rows * 2 * own.shape[0]
    return pl.pallas_call(
        backward_kernel,
        out_shape=(
            jax.ShapeDtypeStruct(kv.shape, BF16),
            jax.ShapeDtypeStruct(own.shape, F32),
            jax.ShapeDtypeStruct(own.shape, BF16),
        ),
        in_specs=[pl.BlockSpec(memory_space=pltpu.SMEM)] + [whole] * 5,
        out_specs=(whole, whole, whole),
        scratch_shapes=[
            pltpu.VMEM((2, DH, parts * rows), BF16),
            pltpu.VMEM(kv.shape, F32),
            pltpu.VMEM(stats.shape[1:], F32),
        ],
        compiler_params=compiler_params(),
        cost_estimate=pl.CostEstimate(
            flops=12 * work * DH, bytes_accessed=5 * 2**20, transcendentals=work
        ),
        name="backward",
    )(base, kv, own, other, lp, stats)


def context_grad_kernel(chunk_ref, dkv_ref, wk_ref, wv_ref, out_ref):
    heads = dkv_ref.shape[0]
    dk = jnp.concatenate([dkv_ref[head, 0] for head in range(heads)], axis=1)
    dv = jnp.concatenate([dkv_ref[head, 1] for head in range(heads)], axis=1)
    total = lax.dot_general(dk, wk_ref[...], NT, preferred_element_type=F32)
    total += lax.dot_general(dv, wv_ref[...], NT, preferred_element_type=F32)
    out_ref[...] = total.astype(out_ref.dtype)


def context_term(chunk, dkv, wk, wv, dtype):
    heads, _, rows, _ = dkv.shape
    depth, cols = wk.shape
    width = depth // NY
    steps = 2
    tile = width // steps
    return pl.pallas_call(
        context_grad_kernel,
        out_shape=jax.ShapeDtypeStruct((rows, width), dtype),
        grid_spec=pltpu.PrefetchScalarGridSpec(
            num_scalar_prefetch=1,
            grid=(steps,),
            in_specs=[
                pl.BlockSpec(dkv.shape, lambda i, ch: (0, 0, 0, 0)),
                pl.BlockSpec((tile, cols), lambda i, ch: (ch[0] * steps + i, 0)),
                pl.BlockSpec((tile, cols), lambda i, ch: (ch[0] * steps + i, 0)),
            ],
            out_specs=pl.BlockSpec((rows, tile), lambda i, ch: (0, i)),
        ),
        compiler_params=compiler_params(),
        cost_estimate=pl.CostEstimate(
            flops=4 * rows * width * cols, bytes_accessed=4 * width * cols, transcendentals=0
        ),
        name="context_term",
    )(chunk, dkv, wk, wv)


def shards(context, key_weight, value_weight, queries, latent_pos, out_grad):
    rows = context.shape[0]
    lat = queries.shape[0]
    heads = key_weight.shape[1] // DH
    me = lax.axis_index("ctx")
    y = lax.axis_index("tp")
    z, core = me // (NX * NC), me % NC
    own_lat = NZ * NX * lat

    ahead = shift_y(context, 1)
    behind = shift_y(context, -1)
    across = shift_y(context, 2)

    def chunk(step):
        return lax.rem(y + step + NY, NY).astype(jnp.int32).reshape(1)

    both = jnp.concatenate(
        [queries.reshape(lat, heads, DH), out_grad.reshape(lat, heads, DH)], axis=2
    ).transpose(1, 0, 2)
    own = exchange(
        jnp.broadcast_to(both[None], (NZ, heads, lat, 2 * DH)).reshape(NZ * heads, lat, 2 * DH),
        ZX_GROUPS,
    ).reshape(own_lat, 2 * DH)
    other = swap_cores(own)

    by_core = latent_pos.reshape(NZ * NX, NC, lat).transpose(1, 0, 2).reshape(NC, own_lat)
    lp = jnp.where(core == 0, by_core, by_core[::-1]).reshape(NC, own_lat // 128, 128)
    base = ((z * NX * NC + core) * rows).astype(jnp.int32).reshape(1)

    total = project(chunk(0), context, key_weight, value_weight, None, False)
    total = project(chunk(-1), ahead, key_weight, value_weight, total, False)
    total = project(chunk(1), behind, key_weight, value_weight, total, False)
    kv = project(chunk(2), across, key_weight, value_weight, total, True)
    kv = exchange(kv, X_GROUPS)

    stats = latent_stats(base, kv, own, other, lp)
    theirs = swap_cores(stats)[:, ::-1]
    peak = jnp.maximum(stats[0], theirs[0])
    mine_share = jnp.exp2(stats[0] - peak)
    their_share = jnp.exp2(theirs[0] - peak)
    joined = jnp.stack([peak] + [stats[k] * mine_share + theirs[k] * their_share for k in (1, 2)])
    every = exchange(jnp.broadcast_to(joined[None], (NZ, *joined.shape)), Z_GROUPS)

    dkv, own_part, other_part = backward(base, kv, own, other, lp, every)
    received = swap_cores(other_part)
    dkv = exchange(dkv, X_GROUPS)

    send_across = context_term(chunk(2), dkv, key_weight, value_weight, BF16)
    got_across = shift_y(send_across, 2)
    send_ahead = context_term(chunk(1), dkv, key_weight, value_weight, BF16)
    got_ahead = shift_y(send_ahead, 1)
    send_behind = context_term(chunk(-1), dkv, key_weight, value_weight, BF16)
    got_behind = shift_y(send_behind, -1)
    kept = context_term(chunk(0), dkv, key_weight, value_weight, F32)

    parts = (own_part + received.astype(F32)).astype(BF16)
    parts = exchange(parts.reshape(NZ * NX, lat, 2 * DH), ZX_GROUPS)
    sums = jnp.sum(parts.reshape(NZ, heads, lat, 2 * DH).astype(F32), axis=0)
    sums = sums.astype(BF16).transpose(1, 0, 2)
    attended = sums[:, :, :DH].reshape(lat, heads * DH)
    query_grad = sums[:, :, DH:].reshape(lat, heads * DH)

    context_grad = (
        kept + got_across.astype(F32) + got_ahead.astype(F32) + got_behind.astype(F32)
    ).astype(BF16)
    return (attended, context_grad, query_grad)


def solution(mesh):
    return jax.shard_map(
        shards,
        mesh=mesh,
        in_specs=(
            P("ctx", "tp"),
            P(None, "tp"),
            P(None, "tp"),
            P("ctx", "tp"),
            P(),
            P("ctx", "tp"),
        ),
        out_specs=(P("ctx", "tp"), P("ctx", "tp"), P("ctx", "tp")),
        check_vma=False,
    )
```

time: 864 us -> 157 us (0.18)
  blocking collectives: 490 us -> 15.7 us
  waiting for transfers between devices: 290 us -> 39 us
  starting transfers between devices: 0.42 us -> 45 us
  Pallas kernels: 0 us -> 42.4 us
  matrix products: 40.7 us -> 0 us
  between operations: 14.3 us -> 0.82 us
    psum x1 -> x0, blocking collectives: 246 us -> none  [shards(): numer_sum, denominator = lax.psum((part_numer, part_denominator), 'ctx')]
    pmax x1 -> x0, blocking collectives: 243 us -> none  [shards(): row_peak = lax.pmax(local_peak, 'ctx')]
    reduce_scatter x2 -> x0, waiting for transfers between devices: 179 us -> none  [the longest x1 126 us: shards(): lax.psum_scatter(jnp.einsum('hlt,thd->lhd', score_grad, key_rows, preferr...]
    all_gather x3 -> x0, waiting for transfers between devices: 109 us -> none  [the longest x1 72.2 us: shards(): lax.all_gather(queries, 'ctx', axis=0, tiled=True)]
    pallas_call x0 -> x10, Pallas kernels: none -> 42.4 us  [the longest x4 14.6 us: project(): pl.pallas_call(functools.partial(project_kernel, first, last), out_shape=...]
    dot_general x10 -> x0, matrix products: 40.7 us -> none  [the longest x1 7.25 us: shards(): jnp.einsum('hlt,thd->lhd', expo.astype(jnp.bfloat16), value_rows, preferr...]
    all_to_all x0 -> x4, starting transfers between devices: none -> 22.7 us  [exchange(): lax.all_to_all(array, 'ctx', 0, 0, tiled=True, axis_index_groups=groups)]
    ppermute x0 -> x9, starting transfers between devices: none -> 22.4 us  [the longest x6 12.6 us: shift_y(): return lax.ppermute(array, 'tp', [(i, (i + step) % NY) for i in range(NY)])]
  transfers between devices with their start and end apart: 6 -> 13, of which waited for: 4 -> 6; matrix products, arithmetic and copies ran while one was open for 5% -> 4% of each run, Pallas kernels for 0% -> 17%
where the time goes in v1:
time: 157 us; the launch traced here: 156 us
  starting transfers between devices  45 us (29%)
  Pallas kernels  42.4 us (27%)
  waiting for transfers between devices  39 us (25%)
  blocking collectives  15.7 us (10%)
  local copies, waits for them, and re-layouts  7.43 us (5%)
  other arithmetic  5.33 us (3%)
    all_to_all x4, starting transfers between devices, exchange(): lax.all_to_all(array, 'ctx', 0, 0, tiled=True, axis_index_groups=groups)  22.7 us
    all_to_all x4, waiting for transfers between devices, exchange(): lax.all_to_all(array, 'ctx', 0, 0, tiled=True, axis_index_groups=groups)  21.8 us
    ppermute x6, waiting for transfers between devices, shift_y(): return lax.ppermute(array, 'tp', [(i, (i + step) % NY) for i in range(NY)])  16.2 us
    all_to_all x1, blocking collectives, exchange(): lax.all_to_all(array, 'ctx', 0, 0, tiled=True, axis_index_groups=groups)  15.7 us
    pallas_call x4, Pallas kernels, project(): pl.pallas_call(functools.partial(project_kernel, first, last), out_shape=...  14.6 us
    ppermute x6, starting transfers between devices, shift_y(): return lax.ppermute(array, 'tp', [(i, (i + step) % NY) for i in range(NY)])  12.6 us
    pallas_call x4, Pallas kernels, context_term(): pl.pallas_call(context_grad_kernel, out_shape=jax.ShapeDtypeStruct((rows,...  12.4 us
    pallas_call x1, Pallas kernels, backward(): pl.pallas_call(backward_kernel, out_shape=(jax.ShapeDtypeStruct(kv.shape,...  9.86 us
  transfers between devices with their start and end apart: 13, of which 6 were waited for; matrix products, arithmetic and copies ran while one was open for 4% of the time, Pallas kernels for 17%

profile of v1, /device:TPU:1, one launch (start us, length us, event | category | flops | bytes accessed | tf_op | source)
XLA Modules:
  0.0 155.8 jit_solution(3684977278777179553)
XLA Ops:
  2.2 0.9 broadcast_in_dim.4
  3.1 11.9 %all-to-all-start.1 = ((bf16[32,32,256]{2,1,0:T(8,128)(2,1)}), bf16[32,32,256]{2,1,0:T(8,128)(2,1)S(1)}, u32[]{:S(2)}, u32[]{:S(2)}) async-start(bf16[32,32,256]{2,1,0:T(8,128)(2,1)} %bitcast.6), calls=%async_computation.1 | async-start | bytes 1048576 | tf_op jit(solution)/shard_map/all_to_all | solution.py:43
  15.0 1.4 collective-permute-start.2
  16.3 1.5 collective-permute-start.1
  17.9 1.6 collective-permute-start
  19.4 3.3 %project.4.refs_0_ = f32[256,1024]{1,0:T(8,128)} custom-call(s32[1]{0:T(128)} %bitcast.4.chunk_ref, bf16[256,1024]{1,0:T(8,128)(2,1)} %x_ref.1, bf16[4096,512]{1,0:T(8,128)(2,1)} %wk_ref.15, bf16[4096,512]{1,0:T(8,128)(2,1)} %wv_ref.15), custom_call_target="tpu_custom_call" | custom-call | flops 536870912 | bytes 2097152 | tf_op jit(solution)/shard_map/project/pallas_call | solution.py:98
  22.8 8.5 %all-to-all-done.1 = bf16[32,32,256]{2,1,0:T(8,128)(2,1)S(1)} async-done(((bf16[32,32,256]{2,1,0:T(8,128)(2,1)}), bf16[32,32,256]{2,1,0:T(8,128)(2,1)S(1)}, u32[]{:S(2)}, u32[]{:S(2)}) %all-to-all-start.1) | async-done | bytes 524320 | tf_op jit(solution)/shard_map/all_to_all | solution.py:43
  31.2 2.4 %collective-permute-start.3 = (bf16[1024,256]{1,0:T(8,128)(2,1)S(1)}, bf16[1024,256]{1,0:T(8,128)(2,1)S(1)}, u32[]{:S(2)}, u32[]{:S(2)}) collective-permute-start(bf16[1024,256]{1,0:T(8,128)(2,1)S(1)} %bitcast.27), channel_id=1, source_target_pairs={{0,4},{4,0},{8,12},{12,8},{16,20},{20,16},{24,28},{28,24},{32,36},... | collective-permute-start | bytes 1572872 | tf_op jit(solution)/shard_map/ppermute | solution.py:35
  34.4 3.8 %project.5.refs_0_ = f32[256,1024]{1,0:T(8,128)} custom-call(s32[1]{0:T(128)} %bitcast.3.chunk_ref, bf16[256,1024]{1,0:T(8,128)(2,1)} %copy-done.2, bf16[4096,512]{1,0:T(8,128)(2,1)} %wk_ref.15, bf16[4096,512]{1,0:T(8,128)(2,1)} %wv_ref.15, f32[256,1024]{1,0:T(8,128)} %project.4.refs_0_), custom_call_target="tpu_custom_call" | custom-call | flops 536870912 | bytes 2097152 | tf_op jit(solution)/shard_map/project/pallas_call | solution.py:98
  39.0 3.8 %project.6.refs_0_ = f32[256,1024]{1,0:T(8,128)} custom-call(s32[1]{0:T(128)} %bitcast.2.chunk_ref, bf16[256,1024]{1,0:T(8,128)(2,1)} %copy-done.1, bf16[4096,512]{1,0:T(8,128)(2,1)} %wk_ref.15, bf16[4096,512]{1,0:T(8,128)(2,1)} %wv_ref.15, f32[256,1024]{1,0:T(8,128)} %project.5.refs_0_), custom_call_target="tpu_custom_call" | custom-call | flops 536870912 | bytes 2097152 | tf_op jit(solution)/shard_map/project/pallas_call | solution.py:98
  43.7 3.7 %project.7 = bf16[4,2,256,128]{3,2,1,0:T(8,128)(2,1)} custom-call(s32[1]{0:T(128)} %bitcast.1.chunk_ref, bf16[256,1024]{1,0:T(8,128)(2,1)} %copy-done.5, bf16[4096,512]{1,0:T(8,128)(2,1)} %wk_ref.15, bf16[4096,512]{1,0:T(8,128)(2,1)} %wv_ref.15, f32[256,1024]{1,0:T(8,128)} %project.6.refs_0_), custom_call_target="tpu_custom_call" | custom-call | flops 536870912 | bytes 2097152 | tf_op jit(solution)/shard_map/project/pallas_call | solution.py:98
  47.3 3.5 %all-to-all-start = ((bf16[4,2,256,128]{3,2,1,0:T(8,128)(2,1)}), bf16[4,2,256,128]{3,2,1,0:T(8,128)(2,1)S(1)}, u32[]{:S(2)}, u32[]{:S(2)}) async-start(bf16[4,2,256,128]{3,2,1,0:T(8,128)(2,1)} %project.7), calls=%async_computation | async-start | bytes 1048576 | tf_op jit(solution)/shard_map/all_to_all | solution.py:43
  51.9 5.8 %all-to-all-done.kv_ref = bf16[4,2,256,128]{3,2,1,0:T(8,128)(2,1)S(1)} async-done(((bf16[4,2,256,128]{3,2,1,0:T(8,128)(2,1)}), bf16[4,2,256,128]{3,2,1,0:T(8,128)(2,1)S(1)}, u32[]{:S(2)}, u32[]{:S(2)}) %all-to-all-start) | async-done | bytes 524320 | tf_op jit(solution)/shard_map/all_to_all | solution.py:43
  58.7 5.6 %latent_stats.1 = f32[3,2,8,128]{3,2,1,0:T(8,128)} custom-call(s32[1]{0:T(128)} %bitcast.base_ref, bf16[4,2,256,128]{3,2,1,0:T(8,128)(2,1)} %copy-done.4, bf16[1024,256]{1,0:T(8,128)(2,1)} %bitcast.28, bf16[1024,256]{1,0:T(8,128)(2,1)} %copy-done.7, s32[2,8,128]{2,1,0:T(8,128)} %bitcast.32), custom_call_target="tpu_custom_call" | custom-call | flops 1073741824 | bytes 2097152 | tf_op jit(solution)/shard_map/latent_stats/pallas_call | solution.py:172
  64.3 5.4 %collective-permute-start.4 = (f32[3,2,8,128]{3,2,1,0:T(8,128)}, f32[3,2,8,128]{3,2,1,0:T(8,128)S(1)}, u32[]{:S(2)}, u32[]{:S(2)}) collective-permute-start(f32[3,2,8,128]{3,2,1,0:T(8,128)} %latent_stats.1), channel_id=1, source_target_pairs={{0,4},{4,0},{8,12},{12,8},{16,20},{20,16},{24,28},{28,24},{32,36},... | collective-permute-start | bytes 73736 | tf_op jit(solution)/shard_map/ppermute | solution.py:35
  69.6 1.1 collective-permute-done.4
  71.5 15.7 %all_to_all.25.st_ref = f32[8,3,2,8,128]{4,3,2,1,0:T(8,128)} all-to-all(f32[8,3,2,8,128]{4,3,2,1,0:T(8,128)S(1)} %broadcast_in_dim.5), channel_id=1, replica_groups={{0,32,64,96,128,160,192,224},{4,36,68,100,132,164,196,228},{8,40,72,104..., dimensions={0} | all-to-all | bytes 393216 | tf_op jit(solution)/shard_map/all_to_all | solution.py:43
  87.2 9.9 %backward.1 = (bf16[4,2,256,128]{3,2,1,0:T(8,128)(2,1)}, f32[1024,256]{1,0:T(8,128)}, bf16[1024,256]{1,0:T(8,128)(2,1)}) custom-call(s32[1]{0:T(128)} %bitcast.base_ref, bf16[4,2,256,128]{3,2,1,0:T(8,128)(2,1)} %copy-done.4, bf16[1024,256]{1,0:T(8,128)(2,1)} %bitcast.29, bf16[1024,256]{1,0:T(8,128)(2,1)} %copy-done.7, s32[2,8,128]{2,1,0:T(8,128)} %bitcast.33, ...), custom_call_target="tpu_custom_call" | custom-call | flops 3221225472 | bytes 5242880 | tf_op jit(solution)/shard_map/backward/pallas_call | solution.py:242
  97.1 2.0 %collective-permute-start.5 = (bf16[1024,256]{1,0:T(8,128)(2,1)}, bf16[1024,256]{1,0:T(8,128)(2,1)S(1)}, u32[]{:S(2)}, u32[]{:S(2)}) collective-permute-start(bf16[1024,256]{1,0:T(8,128)(2,1)} %get-tuple-element.7), channel_id=1, source_target_pairs={{0,4},{4,0},{8,12},{12,8},{16,20},{20,16},{24,28},{28,24},{32,36},... | collective-permute-start | bytes 1572872 | tf_op jit(solution)/shard_map/ppermute | solution.py:35
  99.0 3.5 %all-to-all-start.4 = ((bf16[4,2,256,128]{3,2,1,0:T(8,128)(2,1)}), bf16[4,2,256,128]{3,2,1,0:T(8,128)(2,1)S(1)}, u32[]{:S(2)}, u32[]{:S(2)}) async-start(bf16[4,2,256,128]{3,2,1,0:T(8,128)(2,1)} %get-tuple-element.8), calls=%async_computation.4 | async-start | bytes 1048576 | tf_op jit(solution)/shard_map/all_to_all | solution.py:43
  102.5 2.1 %add_convert_fusion.1 = bf16[1024,256]{1,0:T(8,128)(2,1)} fusion(f32[1024,256]{1,0:T(8,128)} %get-tuple-element.6, bf16[1024,256]{1,0:T(8,128)(2,1)S(1)} %collective-permute-done.5), kind=kLoop, calls=%fused_computation.1 | loop fusion | flops 786432 | bytes 2097152 | tf_op jit(solution)/shard_map/convert_element_type | solution.py:355
  104.6 7.5 %all-to-all-done.4.dkv_ref = bf16[4,2,256,128]{3,2,1,0:T(8,128)(2,1)S(1)} async-done(((bf16[4,2,256,128]{3,2,1,0:T(8,128)(2,1)}), bf16[4,2,256,128]{3,2,1,0:T(8,128)(2,1)S(1)}, u32[]{:S(2)}, u32[]{:S(2)}) %all-to-all-start.4) | async-done | bytes 524320 | tf_op jit(solution)/shard_map/all_to_all | solution.py:43
  112.1 3.9 %all-to-all-start.3 = ((bf16[32,32,256]{2,1,0:T(8,128)(2,1)}), bf16[32,32,256]{2,1,0:T(8,128)(2,1)S(1)}, u32[]{:S(2)}, u32[]{:S(2)}) async-start(bf16[32,32,256]{2,1,0:T(8,128)(2,1)} %bitcast.9), calls=%async_computation.3 | async-start | bytes 1048576 | tf_op jit(solution)/shard_map/all_to_all | solution.py:43
  116.0 3.1 %context_term.7 = bf16[256,1024]{1,0:T(8,128)(2,1)} custom-call(s32[1]{0:T(128)} %bitcast.3.chunk_ref, bf16[4,2,256,128]{3,2,1,0:T(8,128)(2,1)} %copy-done, bf16[4096,512]{1,0:T(8,128)(2,1)} %wk_ref.15, bf16[4096,512]{1,0:T(8,128)(2,1)} %wv_ref.15), custom_call_target="tpu_custom_call" | custom-call | flops 536870912 | bytes 2097152 | tf_op jit(solution)/shard_map/context_term/pallas_call | solution.py:279
  119.1 3.3 %collective-permute-start.8 = (bf16[256,1024]{1,0:T(8,128)(2,1)}, bf16[256,1024]{1,0:T(8,128)(2,1)S(1)}, u32[]{:S(2)}, u32[]{:S(2)}) collective-permute-start(bf16[256,1024]{1,0:T(8,128)(2,1)} %context_term.7), channel_id=1, source_target_pairs={{0,3},{1,0},{2,1},{3,2},{4,7},{5,4},{6,5},{7,6},{8,11},{9,8},{10,9... | collective-permute-start | bytes 1572872 | tf_op jit(solution)/shard_map/ppermute | solution.py:39
  122.4 3.1 %context_term.6 = bf16[256,1024]{1,0:T(8,128)(2,1)} custom-call(s32[1]{0:T(128)} %bitcast.2.chunk_ref, bf16[4,2,256,128]{3,2,1,0:T(8,128)(2,1)} %copy-done, bf16[4096,512]{1,0:T(8,128)(2,1)} %wk_ref.15, bf16[4096,512]{1,0:T(8,128)(2,1)} %wv_ref.15), custom_call_target="tpu_custom_call" | custom-call | flops 536870912 | bytes 2097152 | tf_op jit(solution)/shard_map/context_term/pallas_call | solution.py:279
  125.5 3.1 %context_term.5 = bf16[256,1024]{1,0:T(8,128)(2,1)} custom-call(s32[1]{0:T(128)} %bitcast.1.chunk_ref, bf16[4,2,256,128]{3,2,1,0:T(8,128)(2,1)} %copy-done, bf16[4096,512]{1,0:T(8,128)(2,1)} %wk_ref.15, bf16[4096,512]{1,0:T(8,128)(2,1)} %wv_ref.15), custom_call_target="tpu_custom_call" | custom-call | flops 536870912 | bytes 2097152 | tf_op jit(solution)/shard_map/context_term/pallas_call | solution.py:279
  128.5 4.9 %collective-permute-start.6 = (bf16[256,1024]{1,0:T(8,128)(2,1)}, bf16[256,1024]{1,0:T(8,128)(2,1)S(1)}, u32[]{:S(2)}, u32[]{:S(2)}) collective-permute-start(bf16[256,1024]{1,0:T(8,128)(2,1)} %context_term.5), channel_id=1, source_target_pairs={{0,2},{1,3},{2,0},{3,1},{4,6},{5,7},{6,4},{7,5},{8,10},{9,11},{10,... | collective-permute-start | bytes 1572872 | tf_op jit(solution)/shard_map/ppermute | solution.py:39
  133.4 3.1 %context_term.4 = f32[256,1024]{1,0:T(8,128)} custom-call(s32[1]{0:T(128)} %bitcast.4.chunk_ref, bf16[4,2,256,128]{3,2,1,0:T(8,128)(2,1)} %copy-done, bf16[4096,512]{1,0:T(8,128)(2,1)} %wk_ref.15, bf16[4096,512]{1,0:T(8,128)(2,1)} %wv_ref.15), custom_call_target="tpu_custom_call" | custom-call | flops 536870912 | bytes 2097152 | tf_op jit(solution)/shard_map/context_term/pallas_call | solution.py:279
  136.6 4.0 %collective-permute-done.7 = bf16[256,1024]{1,0:T(8,128)(2,1)S(1)} collective-permute-done((bf16[256,1024]{1,0:T(8,128)(2,1)}, bf16[256,1024]{1,0:T(8,128)(2,1)S(1)}, u32[]{:S(2)}, u32[]{:S(2)}) %collective-permute-start.7) | collective-permute-done | bytes 524320 | tf_op jit(solution)/shard_map/ppermute | solution.py:39
  140.6 12.1 %collective-permute-done.6 = bf16[256,1024]{1,0:T(8,128)(2,1)S(1)} collective-permute-done((bf16[256,1024]{1,0:T(8,128)(2,1)}, bf16[256,1024]{1,0:T(8,128)(2,1)S(1)}, u32[]{:S(2)}, u32[]{:S(2)}) %collective-permute-start.6) | collective-permute-done | bytes 524320 | tf_op jit(solution)/shard_map/ppermute | solution.py:39
  152.7 2.3 %add_convert_fusion = bf16[256,1024]{1,0:T(8,128)(2,1)} fusion(bf16[256,1024]{1,0:T(8,128)(2,1)S(1)} %collective-permute-done.8, bf16[256,1024]{1,0:T(8,128)(2,1)S(1)} %collective-permute-done.7, f32[256,1024]{1,0:T(8,128)} %context_term.4, bf16[256,1024]{1,0:T(8,128)(2,1)S(1)} %collective-permute-done.6), kind=kLoop, calls=%fused_computation | loop fusion | flops 1835008 | bytes 3145728 | tf_op jit(solution)/shard_map/convert_element_type | solution.py:364
  (41 shorter events, 7.5 us)
Async XLA Ops:
  3.1 28.1 %all-to-all-start.1 = ((bf16[32,32,256]{2,1,0:T(8,128)(2,1)}), bf16[32,32,256]{2,1,0:T(8,128)(2,1)S(1)}, u32[]{:S(2)}, u32[]{:S(2)}) async-start(bf16[32,32,256]{2,1,0:T(8,128)(2,1)} %bitcast.6), calls=%async_computation.1 | async-start | bytes 1048576 | tf_op jit(solution)/shard_map/all_to_all | solution.py:43
  15.0 18.7 %collective-permute-start.2 = (bf16[256,1024]{1,0:T(8,128)(2,1)}, bf16[256,1024]{1,0:T(8,128)(2,1)S(1)}, u32[]{:S(2)}, u32[]{:S(2)}) collective-permute-start(bf16[256,1024]{1,0:T(8,128)(2,1)} %x_ref.1), channel_id=1, source_target_pairs={{0,1},{1,2},{2,3},{3,0},{4,5},{5,6},{6,7},{7,4},{8,9},{9,10},{10,1... | collective-permute-start | bytes 1572872 | tf_op jit(solution)/shard_map/ppermute | solution.py:39
  16.3 21.9 %collective-permute-start.1 = (bf16[256,1024]{1,0:T(8,128)(2,1)}, bf16[256,1024]{1,0:T(8,128)(2,1)S(1)}, u32[]{:S(2)}, u32[]{:S(2)}) collective-permute-start(bf16[256,1024]{1,0:T(8,128)(2,1)} %x_ref.1), channel_id=1, source_target_pairs={{0,3},{1,0},{2,1},{3,2},{4,7},{5,4},{6,5},{7,6},{8,11},{9,8},{10,9... | collective-permute-start | bytes 1572872 | tf_op jit(solution)/shard_map/ppermute | solution.py:39
  17.9 25.0 %collective-permute-start = (bf16[256,1024]{1,0:T(8,128)(2,1)}, bf16[256,1024]{1,0:T(8,128)(2,1)S(1)}, u32[]{:S(2)}, u32[]{:S(2)}) collective-permute-start(bf16[256,1024]{1,0:T(8,128)(2,1)} %x_ref.1), channel_id=1, source_target_pairs={{0,2},{1,3},{2,0},{3,1},{4,6},{5,7},{6,4},{7,5},{8,10},{9,11},{10,... | collective-permute-start | bytes 1572872 | tf_op jit(solution)/shard_map/ppermute | solution.py:39
  31.2 16.1 %copy-start.3 = (bf16[32,32,256]{2,1,0:T(8,128)(2,1)}, bf16[32,32,256]{2,1,0:T(8,128)(2,1)S(1)}, u32[]{:S(2)}) copy-start(bf16[32,32,256]{2,1,0:T(8,128)(2,1)S(1)} %all-to-all-done.1) | copy-start | bytes 1572868
  31.2 26.4 %collective-permute-start.3 = (bf16[1024,256]{1,0:T(8,128)(2,1)S(1)}, bf16[1024,256]{1,0:T(8,128)(2,1)S(1)}, u32[]{:S(2)}, u32[]{:S(2)}) collective-permute-start(bf16[1024,256]{1,0:T(8,128)(2,1)S(1)} %bitcast.27), channel_id=1, source_target_pairs={{0,4},{4,0},{8,12},{12,8},{16,20},{20,16},{24,28},{28,24},{32,36},... | collective-permute-start | bytes 1572872 | tf_op jit(solution)/shard_map/ppermute | solution.py:35
  33.6 0.8 copy-start.2
  38.2 0.8 copy-start.1
  42.9 0.8 copy-start.5
  43.6 7.2 %copy-start.6 = (s32[2048]{0:T(1024)S(1)}, s32[2048]{0:T(1024)}, u32[]{:S(2)}) copy-start(s32[2048]{0:T(1024)} %param.10) | copy-start | bytes 24580
  47.3 10.4 %all-to-all-start = ((bf16[4,2,256,128]{3,2,1,0:T(8,128)(2,1)}), bf16[4,2,256,128]{3,2,1,0:T(8,128)(2,1)S(1)}, u32[]{:S(2)}, u32[]{:S(2)}) async-start(bf16[4,2,256,128]{3,2,1,0:T(8,128)(2,1)} %project.7), calls=%async_computation | async-start | bytes 1048576 | tf_op jit(solution)/shard_map/all_to_all | solution.py:43
  57.7 0.8 copy-start.4
  57.7 1.0 copy-start.7
  64.3 6.4 %collective-permute-start.4 = (f32[3,2,8,128]{3,2,1,0:T(8,128)}, f32[3,2,8,128]{3,2,1,0:T(8,128)S(1)}, u32[]{:S(2)}, u32[]{:S(2)}) collective-permute-start(f32[3,2,8,128]{3,2,1,0:T(8,128)} %latent_stats.1), channel_id=1, source_target_pairs={{0,4},{4,0},{8,12},{12,8},{16,20},{20,16},{24,28},{28,24},{32,36},... | collective-permute-start | bytes 73736 | tf_op jit(solution)/shard_map/ppermute | solution.py:35
  97.1 5.4 %collective-permute-start.5 = (bf16[1024,256]{1,0:T(8,128)(2,1)}, bf16[1024,256]{1,0:T(8,128)(2,1)S(1)}, u32[]{:S(2)}, u32[]{:S(2)}) collective-permute-start(bf16[1024,256]{1,0:T(8,128)(2,1)} %get-tuple-element.7), channel_id=1, source_target_pairs={{0,4},{4,0},{8,12},{12,8},{16,20},{20,16},{24,28},{28,24},{32,36},... | collective-permute-start | bytes 1572872 | tf_op jit(solution)/shard_map/ppermute | solution.py:35
  99.0 13.1 %all-to-all-start.4 = ((bf16[4,2,256,128]{3,2,1,0:T(8,128)(2,1)}), bf16[4,2,256,128]{3,2,1,0:T(8,128)(2,1)S(1)}, u32[]{:S(2)}, u32[]{:S(2)}) async-start(bf16[4,2,256,128]{3,2,1,0:T(8,128)(2,1)} %get-tuple-element.8), calls=%async_computation.4 | async-start | bytes 1048576 | tf_op jit(solution)/shard_map/all_to_all | solution.py:43
  112.1 3.9 %copy-start = (bf16[4,2,256,128]{3,2,1,0:T(8,128)(2,1)}, bf16[4,2,256,128]{3,2,1,0:T(8,128)(2,1)S(1)}, u32[]{:S(2)}) copy-start(bf16[4,2,256,128]{3,2,1,0:T(8,128)(2,1)S(1)} %all-to-all-done.4.dkv_ref) | copy-start | bytes 1572868
  112.1 42.9 %all-to-all-start.3 = ((bf16[32,32,256]{2,1,0:T(8,128)(2,1)}), bf16[32,32,256]{2,1,0:T(8,128)(2,1)S(1)}, u32[]{:S(2)}, u32[]{:S(2)}) async-start(bf16[32,32,256]{2,1,0:T(8,128)(2,1)} %bitcast.9), calls=%async_computation.3 | async-start | bytes 1048576 | tf_op jit(solution)/shard_map/all_to_all | solution.py:43
  119.1 17.4 %collective-permute-start.8 = (bf16[256,1024]{1,0:T(8,128)(2,1)}, bf16[256,1024]{1,0:T(8,128)(2,1)S(1)}, u32[]{:S(2)}, u32[]{:S(2)}) collective-permute-start(bf16[256,1024]{1,0:T(8,128)(2,1)} %context_term.7), channel_id=1, source_target_pairs={{0,3},{1,0},{2,1},{3,2},{4,7},{5,4},{6,5},{7,6},{8,11},{9,8},{10,9... | collective-permute-start | bytes 1572872 | tf_op jit(solution)/shard_map/ppermute | solution.py:39
  125.5 15.1 %collective-permute-start.7 = (bf16[256,1024]{1,0:T(8,128)(2,1)}, bf16[256,1024]{1,0:T(8,128)(2,1)S(1)}, u32[]{:S(2)}, u32[]{:S(2)}) collective-permute-start(bf16[256,1024]{1,0:T(8,128)(2,1)} %context_term.6), channel_id=1, source_target_pairs={{0,1},{1,2},{2,3},{3,0},{4,5},{5,6},{6,7},{7,4},{8,9},{9,10},{10,1... | collective-permute-start | bytes 1572872 | tf_op jit(solution)/shard_map/ppermute | solution.py:39
  128.5 24.2 %collective-permute-start.6 = (bf16[256,1024]{1,0:T(8,128)(2,1)}, bf16[256,1024]{1,0:T(8,128)(2,1)S(1)}, u32[]{:S(2)}, u32[]{:S(2)}) collective-permute-start(bf16[256,1024]{1,0:T(8,128)(2,1)} %context_term.5), channel_id=1, source_target_pairs={{0,2},{1,3},{2,0},{3,1},{4,6},{5,7},{6,4},{7,5},{8,10},{9,11},{10,... | collective-permute-start | bytes 1572872 | tf_op jit(solution)/shard_map/ppermute | solution.py:39

commit v2 on v0

v2 whole, which is shorter than its diff:
```python
import functools
import math

import jax
import jax.numpy as jnp
from jax import lax
from jax.experimental import pallas as pl
from jax.experimental.pallas import tpu as pltpu
from jax.sharding import PartitionSpec as P

DH = 128
NZ, NX, NC, NY = 8, 4, 2, 4
NEG_FILL = -1e30
SCORE_SCALE = 1.0 / math.sqrt(DH)
LOG2_SCALE = SCORE_SCALE * math.log2(math.e)
VMEM_LIMIT = 16 * 1024 * 1024
F32 = jnp.float32
BF16 = jnp.bfloat16
NT = (((1,), (1,)), ((), ()))


def place(z, x, c):
    return (z * NX + x) * NC + c


CORE_SWAP = [
    (place(z, x, c), place(z, x, 1 - c)) for z in range(NZ) for x in range(NX) for c in range(NC)
]
Z_GROUPS = [[place(z, x, c) for z in range(NZ)] for x in range(NX) for c in range(NC)]


def swap_cores(array):
    return lax.ppermute(array, "ctx", CORE_SWAP)


def shift_y(array, step):
    return lax.ppermute(array, "tp", [(i, (i + step) % NY) for i in range(NY)])


def shift_x(array, step):
    pairs = [
        (place(z, x, c), place(z, (x + step) % NX, c))
        for z in range(NZ)
        for x in range(NX)
        for c in range(NC)
    ]
    return lax.ppermute(array, "ctx", pairs)


def flip_z(array, bit):
    pairs = [
        (place(z, x, c), place(z ^ bit, x, c))
        for z in range(NZ)
        for x in range(NX)
        for c in range(NC)
    ]
    return lax.ppermute(array, "ctx", pairs)


def exchange(array, groups):
    return lax.all_to_all(array, "ctx", 0, 0, tiled=True, axis_index_groups=groups)


FLIPS = (0, 4, 2, 6, 1, 5, 3, 7)


def compiler_params(limit=VMEM_LIMIT):
    return pltpu.CompilerParams(vmem_limit_bytes=limit)


def chunk_rows(at_ref, step, depth):
    return pl.ds(pl.multiple_of(lax.rem(at_ref[0] + step, NY) * depth, depth), depth)


def head_columns(at_ref, turn, heads):
    return pl.ds(pl.multiple_of(lax.rem(at_ref[1] + turn, heads) * DH, DH), DH)


def cost(flops, size, exponentials):
    return pl.CostEstimate(flops=0, bytes_accessed=0, transcendentals=0)


def load_weights_kernel(*refs):
    sources, targets, sem = refs[:2], refs[2:4], refs[4]
    copies = [pltpu.make_async_copy(*pair, sem.at[n]) for n, pair in enumerate(zip(sources, targets))]
    for copy in copies:
        copy.start()
    for copy in copies:
        copy.wait()


def load_weights(wk, wv):
    return pl.pallas_call(
        load_weights_kernel,
        out_shape=[jax.ShapeDtypeStruct(w.shape, w.dtype) for w in (wk, wv)],
        in_specs=[pl.BlockSpec(memory_space=pltpu.HBM)] * 2,
        out_specs=[pl.BlockSpec(memory_space=pltpu.VMEM)] * 2,
        scratch_shapes=[pltpu.SemaphoreType.DMA((2,))],
        compiler_params=compiler_params(),
        cost_estimate=cost(0, 4 * wk.size, 0),
        name="load_weights",
    )(wk, wv)


def project_kernel(steps, first, last, at_ref, *refs):
    wk_ref, wv_ref, refs = refs[0], refs[1], refs[2:]
    depth, cols = refs[0].shape[1], wk_ref.shape[1]
    total = [0.0, 0.0]
    refs = list(refs)
    pieces = []
    for step, count in steps:
        pieces.append(jnp.concatenate([refs.pop(0)[...] for _ in range(count)]))
    if not first:
        before = refs.pop(0)
        total = [before[kind] for kind in range(2)]
    for (step, _), piece in zip(steps, pieces):
        at = chunk_rows(at_ref, step, depth)
        for kind, weight in enumerate((wk_ref, wv_ref)):
            total[kind] += jnp.dot(piece, weight[at, :], preferred_element_type=F32)
    if last:
        heads = cols // DH
        outs, low_ref = refs[-heads - 1 : -1], refs[-1]
        for kind in range(2):
            low_ref[kind] = total[kind].astype(BF16)
        for turn, out in enumerate(outs):
            for kind in range(2):
                out[kind] = low_ref[kind, :, head_columns(at_ref, turn, heads)]
    else:
        for kind in range(2):
            refs[-1][kind] = total[kind]


def project(at, wk, wv, pieces, total, last):
    arrays = [array for group in pieces.values() for array in group]
    steps = tuple((step, len(group)) for step, group in pieces.items())
    depth = arrays[0].shape[1]
    rows = sum(array.shape[0] for array in arrays) // len(pieces)
    cols = wk.shape[1]
    first = total is None
    args = [wk, wv, *arrays] + ([] if first else [total])
    if last:
        out_shape = [jax.ShapeDtypeStruct((2, rows, DH), BF16)] * (cols // DH)
    else:
        out_shape = [jax.ShapeDtypeStruct((2, rows, cols), F32)]
    whole = pl.BlockSpec(memory_space=pltpu.VMEM)
    return pl.pallas_call(
        functools.partial(project_kernel, steps, first, last),
        out_shape=out_shape,
        in_specs=[pl.BlockSpec(memory_space=pltpu.SMEM)] + [whole] * len(args),
        out_specs=[whole] * len(out_shape),
        scratch_shapes=[pltpu.VMEM((2, rows, cols), BF16)] if last else [],
        compiler_params=compiler_params(),
        cost_estimate=cost(4 * len(pieces) * rows * depth * cols, 2**20, 0),
        name="project",
    )(at, *args)


BLOCK = 256
LANES = BLOCK // 128


def masked_scores(first, keys, q, lp):
    scores = lax.dot_general(keys, q, NT, preferred_element_type=F32) * LOG2_SCALE
    rank = lax.broadcasted_iota(jnp.int32, scores.shape, 0)
    return jnp.where(rank <= lp - first, scores, NEG_FILL)


def first_position(at_ref, turn, rows):
    return place(at_ref[2], lax.rem(at_ref[1] - turn + NX, NX), at_ref[3]) * rows


def row_of(at_ref, ref, *index):
    *lead, block = index
    parts = [
        ref[(*lead, pl.ds(at_ref[2] ^ FLIPS[block * LANES + k], 1))] for k in range(LANES)
    ]
    return jnp.concatenate(parts, axis=1)


def stats_kernel(at_ref, *refs):
    kv_refs, (own_ref, other_ref, lp_ref, out_ref) = refs[:NX], refs[NX:]
    rows = kv_refs[0].shape[1]
    for half, src in enumerate((own_ref, other_ref)):
        for block in range(src.shape[0] // BLOCK):
            at = pl.ds(block * BLOCK, BLOCK)
            q = src[at, :DH]
            go = src[at, DH:]
            lp = row_of(at_ref, lp_ref, half, block)
            scores = [masked_scores(first_position(at_ref, n, rows), kv_refs[n][0], q, lp) for n in range(NX)]
            peak = functools.reduce(
                jnp.maximum, [jnp.max(s, axis=0, keepdims=True) for s in scores]
            )
            total = 0.0
            dots = 0.0
            for n in range(NX):
                expo = jnp.exp2(scores[n] - peak)
                grads = lax.dot_general(kv_refs[n][1], go, NT, preferred_element_type=F32)
                total += jnp.sum(expo, axis=0, keepdims=True)
                dots += jnp.sum(expo * grads, axis=0, keepdims=True)
            seen = peak > 0.5 * NEG_FILL
            total = jnp.where(seen, total, 0.0)
            dots = jnp.where(seen, dots, 0.0)
            for kind, value in enumerate((peak, total, dots)):
                for k in range(LANES):
                    out_ref[kind, half, pl.ds(at_ref[2] ^ FLIPS[block * LANES + k], 1)] = value[
                        :, k * 128 : (k + 1) * 128
                    ]


def latent_stats(at, kv, own, other, lp):
    whole = pl.BlockSpec(memory_space=pltpu.VMEM)
    work = NX * kv[0].shape[1] * 2 * own.shape[0]
    return pl.pallas_call(
        stats_kernel,
        out_shape=jax.ShapeDtypeStruct((3, 2, own.shape[0] // 128, 128), F32),
        in_specs=[pl.BlockSpec(memory_space=pltpu.SMEM)] + [whole] * (NX + 3),
        out_specs=whole,
        compiler_params=compiler_params(),
        cost_estimate=cost(4 * work * DH, 2 * 2**20, work),
        name="latent_stats",
    )(at, *kv, own, other, lp)


def backward_kernel(at_ref, *refs):
    kv_refs, refs = refs[:NX], refs[NX:]
    rows = kv_refs[0].shape[1]
    (own_ref, other_ref, lp_ref, st_ref), refs = refs[:4], refs[4:]
    dkv_refs, (own_out, other_out, kvt_ref, acc_ref, fin_ref) = refs[:NX], refs[NX:]
    for n in range(NX):
        for kind in range(2):
            kvt_ref[n, kind] = kv_refs[n][kind].T
    acc_ref[...] = jnp.zeros_like(acc_ref)

    peaks = [st_ref[n, 0] for n in range(NZ)]
    top = functools.reduce(jnp.maximum, peaks)
    total = 0.0
    dots = 0.0
    for n in range(NZ):
        share = jnp.exp2(peaks[n] - top)
        total += share * st_ref[n, 1]
        dots += share * st_ref[n, 2]
    fin_ref[0] = top
    fin_ref[1] = jnp.log2(total)
    fin_ref[2] = dots / total

    for half, (src, dst) in enumerate(((own_ref, own_out), (other_ref, other_out))):
        for block in range(src.shape[0] // BLOCK):
            at = pl.ds(block * BLOCK, BLOCK)
            q = src[at, :DH]
            go = src[at, DH:]
            lp = row_of(at_ref, lp_ref, half, block)
            peak, log_total, dot = (row_of(at_ref, fin_ref, k, half, block) for k in range(3))
            attended = 0.0
            query_grad = 0.0
            for n in range(NX):
                scores = masked_scores(first_position(at_ref, n, rows), kv_refs[n][0], q, lp)
                probs = jnp.exp2((scores - peak) - log_total)
                low = probs.astype(BF16)
                grads = lax.dot_general(kv_refs[n][1], go, NT, preferred_element_type=F32)
                score_grad = (probs * (grads - dot) * SCORE_SCALE).astype(BF16)
                acc_ref[n, 1] += jnp.dot(low, go, preferred_element_type=F32)
                acc_ref[n, 0] += jnp.dot(score_grad, q, preferred_element_type=F32)
                attended += jnp.dot(kvt_ref[n, 1], low, preferred_element_type=F32)
                query_grad += jnp.dot(kvt_ref[n, 0], score_grad, preferred_element_type=F32)
            dst[at, :DH] = attended.T.astype(dst.dtype)
            dst[at, DH:] = query_grad.T.astype(dst.dtype)
    for n in range(NX):
        dkv_refs[n][...] = acc_ref[n].astype(BF16)


def backward(at, kv, own, other, lp, stats):
    whole = pl.BlockSpec(memory_space=pltpu.VMEM)
    rows = kv[0].shape[1]
    work = NX * rows * 2 * own.shape[0]
    out = pl.pallas_call(
        backward_kernel,
        out_shape=[jax.ShapeDtypeStruct(kv[0].shape, BF16)] * NX
        + [jax.ShapeDtypeStruct(own.shape, F32), jax.ShapeDtypeStruct(own.shape, BF16)],
        in_specs=[pl.BlockSpec(memory_space=pltpu.SMEM)] + [whole] * (NX + 4),
        out_specs=[whole] * (NX + 2),
        scratch_shapes=[
            pltpu.VMEM((NX, 2, DH, rows), BF16),
            pltpu.VMEM((NX, *kv[0].shape), F32),
            pltpu.VMEM(stats.shape[1:], F32),
        ],
        compiler_params=compiler_params(),
        cost_estimate=cost(12 * work * DH, 5 * 2**20, work),
        name="backward",
    )(at, *kv, own, other, lp, stats)
    return out[:NX], out[NX], out[NX + 1]


def context_grad_kernel(steps, halves, at_ref, wk_ref, wv_ref, *refs):
    dkv_refs, out_refs, grads_ref = refs[:NX], refs[NX:-1], refs[-1]
    for turn, ref in enumerate(dkv_refs):
        for kind in range(2):
            grads_ref[kind, :, head_columns(at_ref, turn, NX)] = ref[kind]
    for n, step in enumerate(steps):
        at = chunk_rows(at_ref, step, out_refs[0].shape[1])
        total = lax.dot_general(grads_ref[0], wk_ref[at, :], NT, preferred_element_type=F32)
        total += lax.dot_general(grads_ref[1], wv_ref[at, :], NT, preferred_element_type=F32)
        size = out_refs[0].shape[0]
        for k in range(halves):
            out = out_refs[n * halves + k]
            out[...] = total[k * size : (k + 1) * size].astype(out.dtype)


def context_terms(at, wk, wv, dkv, steps, halves, dtype):
    rows = dkv[0].shape[1]
    width, cols = wk.shape[0] // NY, wk.shape[1]
    whole = pl.BlockSpec(memory_space=pltpu.VMEM)
    count = len(steps) * halves
    return pl.pallas_call(
        functools.partial(context_grad_kernel, steps, halves),
        out_shape=[jax.ShapeDtypeStruct((rows // halves, width), dtype)] * count,
        in_specs=[pl.BlockSpec(memory_space=pltpu.SMEM)] + [whole] * (NX + 2),
        out_specs=[whole] * count,
        scratch_shapes=[pltpu.VMEM((2, rows, cols), BF16)],
        compiler_params=compiler_params(),
        cost_estimate=cost(4 * rows * width * cols * len(steps), 2**20, 0),
        name="context_terms",
    )(at, wk, wv, *dkv)


def join_kernel(up_ref, down_ref, upper_ref, lower_ref, up_out, down_out):
    half = upper_ref.shape[0]
    up_out[:half] = (up_ref[:half] + upper_ref[...].astype(F32)).astype(up_out.dtype)
    up_out[half:] = up_ref[half:].astype(up_out.dtype)
    down_out[:half] = down_ref[:half].astype(down_out.dtype)
    down_out[half:] = (down_ref[half:] + lower_ref[...].astype(F32)).astype(down_out.dtype)


def join_terms(up, down, upper, lower):
    whole = pl.BlockSpec(memory_space=pltpu.VMEM)
    return pl.pallas_call(
        join_kernel,
        out_shape=[jax.ShapeDtypeStruct(up.shape, BF16)] * 2,
        in_specs=[whole] * 4,
        out_specs=[whole] * 2,
        compiler_params=compiler_params(),
        cost_estimate=cost(0, 2**20, 0),
        name="join_terms",
    )(up, down, upper, lower)


def finish_kernel(kept_ref, up_ref, down_ref, out_ref):
    total = kept_ref[...] + up_ref[...].astype(F32) + down_ref[...].astype(F32)
    out_ref[...] = total.astype(out_ref.dtype)


def finish(kept, up, down):
    whole = pl.BlockSpec(memory_space=pltpu.VMEM)
    return pl.pallas_call(
        finish_kernel,
        out_shape=jax.ShapeDtypeStruct(kept.shape, BF16),
        in_specs=[whole] * 3,
        out_specs=whole,
        compiler_params=compiler_params(),
        cost_estimate=cost(0, 2**20, 0),
        name="finish",
    )(kept, up, down)


def shards(context, key_weight, value_weight, queries, latent_pos, out_grad):
    lat = queries.shape[0]
    heads = key_weight.shape[1] // DH
    me = lax.axis_index("ctx").astype(jnp.int32)
    y = lax.axis_index("tp").astype(jnp.int32)
    z, x, core = me >> 3, (me >> 1) & 3, me & 1
    at = jnp.stack([y, x, z, core])

    lp = latent_pos.reshape(NZ, NX, NC, lat)[:, ::-1]
    lp = lax.dynamic_slice_in_dim(jnp.concatenate([lp, lp], axis=1), NX - 1 - x, NX, 1)
    lp = lp.transpose(2, 0, 1, 3).reshape(NC, NZ, NX * lat)
    lp = jnp.where(core == 0, lp, lp[::-1])
    at, lp = lax.optimization_barrier((at, lp))

    rows = context.shape[0]
    ahead, behind = shift_y(context, 1), shift_y(context, -1)
    weights = load_weights(key_weight, value_weight)
    (total,) = project(at, *weights, {0: [context]}, None, False)

    both = jnp.concatenate(
        [queries.reshape(lat, heads, DH), out_grad.reshape(lat, heads, DH)], axis=2
    ).transpose(1, 0, 2)
    both = jnp.concatenate([both, both])
    by_turn = [lax.dynamic_slice_in_dim(both, x + turn, 1, 0)[0] for turn in range(NX)]
    own = jnp.concatenate([by_turn[0]] + [shift_x(by_turn[n], n) for n in range(1, NX)])
    own = jnp.concatenate([own, flip_z(own, 4)])
    own, total, ahead, behind = lax.optimization_barrier((own, total, ahead, behind))
    far_upper, far_lower = shift_y(ahead[: rows // 2], 1), shift_y(behind[rows // 2 :], -1)
    own = jnp.concatenate([own, flip_z(own, 2)])
    (total,) = project(at, *weights, {3: [ahead], 1: [behind]}, total, False)
    own, total, far_upper, far_lower = lax.optimization_barrier((own, total, far_upper, far_lower))
    own = jnp.concatenate([own, flip_z(own, 1)])
    kv = project(at, *weights, {2: [far_upper, far_lower]}, total, True)
    own, kv = lax.optimization_barrier((own, kv))
    kv = [kv[0]] + [shift_x(kv[n], n) for n in range(1, NX)]
    other = swap_cores(own)

    stats = latent_stats(at, kv, own, other, lp)
    theirs = swap_cores(stats)[:, ::-1]
    peak = jnp.maximum(stats[0], theirs[0])
    mine_share = jnp.exp2(stats[0] - peak)
    their_share = jnp.exp2(theirs[0] - peak)
    joined = jnp.stack([peak] + [stats[k] * mine_share + theirs[k] * their_share for k in (1, 2)])
    every = exchange(jnp.broadcast_to(joined[None], (NZ, *joined.shape)), Z_GROUPS)

    dkv, own_part, other_part = backward(at, kv, own, other, lp, every)
    received = swap_cores(other_part)
    dkv = [dkv[0]] + [shift_x(dkv[n], -n) for n in range(1, NX)]

    def terms(steps, halves, dtype):
        return context_terms(at, *weights, dkv, steps, halves, dtype)

    def halve(part, bit):
        half = part.shape[0] // 2
        return part[:half] + flip_z(part[half:].astype(BF16), bit).astype(F32)

    far_upper, far_lower = terms((2,), 2, BF16)
    add_upper, add_lower = shift_y(far_upper, 1), shift_y(far_lower, -1)
    part = own_part + received.astype(F32)
    part = halve(part, 1)
    part, far_upper = lax.optimization_barrier((part, far_upper))
    part = halve(part, 2)

    up, down, kept = terms((1, 3, 0), 1, F32)
    part, up, down, kept = lax.optimization_barrier((part, up, down, kept))
    part = halve(part, 4)
    up, down = join_terms(up, down, add_upper, add_lower)
    from_below, from_above = shift_y(up, 1), shift_y(down, -1)
    part, up = lax.optimization_barrier((part, up))

    part = part.astype(BF16).reshape(NX, lat, 2 * DH)
    part = jnp.stack([part[0]] + [shift_x(part[n], -n) for n in range(1, NX)])
    part = lax.dynamic_slice_in_dim(jnp.concatenate([part, part]), (heads - x) & 3, heads, 0)
    part, kept = lax.optimization_barrier((part.transpose(1, 0, 2), kept))
    attended = part[:, :, :DH].reshape(lat, heads * DH)
    query_grad = part[:, :, DH:].reshape(lat, heads * DH)

    return (attended, finish(kept, from_below, from_above), query_grad)


def solution(mesh):
    return jax.shard_map(
        shards,
        mesh=mesh,
        in_specs=(
            P("ctx", "tp"),
            P(None, "tp"),
            P(None, "tp"),
            P("ctx", "tp"),
            P(),
            P("ctx", "tp"),
        ),
        out_specs=(P("ctx", "tp"), P("ctx", "tp"), P("ctx", "tp")),
        check_vma=False,
    )
```

time: 864 us -> 133 us (0.15)
  blocking collectives: 490 us -> 16.3 us
  waiting for transfers between devices: 290 us -> 36.1 us
  starting transfers between devices: 0.42 us -> 42.9 us
  matrix products: 40.7 us -> 0 us
  Pallas kernels: 0 us -> 25 us
  between operations: 14.3 us -> 1 us
  other arithmetic: 13.1 us -> 1.49 us
    psum x1 -> x0, blocking collectives: 246 us -> none  [shards(): numer_sum, denominator = lax.psum((part_numer, part_denominator), 'ctx')]
    pmax x1 -> x0, blocking collectives: 243 us -> none  [shards(): row_peak = lax.pmax(local_peak, 'ctx')]
    reduce_scatter x2 -> x0, waiting for transfers between devices: 179 us -> none  [the longest x1 126 us: shards(): lax.psum_scatter(jnp.einsum('hlt,thd->lhd', score_grad, key_rows, preferr...]
    all_gather x3 -> x0, waiting for transfers between devices: 109 us -> none  [the longest x1 72.2 us: shards(): lax.all_gather(queries, 'ctx', axis=0, tiled=True)]
    ppermute x0 -> x29, starting transfers between devices: none -> 42.9 us  [the longest x8 12 us: shift_y(): return lax.ppermute(array, 'tp', [(i, (i + step) % NY) for i in range(NY)])]
    dot_general x10 -> x0, matrix products: 40.7 us -> none  [the longest x1 7.25 us: shards(): jnp.einsum('hlt,thd->lhd', expo.astype(jnp.bfloat16), value_rows, preferr...]
    ppermute x0 -> x29, waiting for transfers between devices: none -> 36.1 us  [the longest x12 19 us: shift_x(): return lax.ppermute(array, 'ctx', pairs)]
    pallas_call x0 -> x10, Pallas kernels: none -> 25 us  [the longest x1 9.14 us: backward(): pl.pallas_call(backward_kernel, out_shape=[jax.ShapeDtypeStruct(kv[0].sha...]
  transfers between devices with their start and end apart: 6 -> 29, of which waited for: 4 -> 16; matrix products, arithmetic and copies ran while one was open for 5% -> 3% of each run, Pallas kernels for 0% -> 8%
where the time goes in v2:
time: 133 us; the launch traced here: 131 us
  starting transfers between devices  42.9 us (32%)
  waiting for transfers between devices  36.1 us (27%)
  Pallas kernels  25 us (19%)
  blocking collectives  16.3 us (12%)
  local copies, waits for them, and re-layouts  8.61 us (6%)
  other arithmetic  1.49 us (1%)
    ppermute x12, waiting for transfers between devices, shift_x(): return lax.ppermute(array, 'ctx', pairs)  19 us
    all_to_all x1, blocking collectives, exchange(): lax.all_to_all(array, 'ctx', 0, 0, tiled=True, axis_index_groups=groups)  16.3 us
    ppermute x6, waiting for transfers between devices, flip_z(): return lax.ppermute(array, 'ctx', pairs)  14.5 us
    ppermute x8, starting transfers between devices, shift_y(): return lax.ppermute(array, 'tp', [(i, (i + step) % NY) for i in range(NY)])  12 us
    ppermute x12, starting transfers between devices, shift_x(): return lax.ppermute(array, 'ctx', pairs)  11.8 us
    ppermute x6, starting transfers between devices, flip_z(): return lax.ppermute(array, 'ctx', pairs)  10.3 us
    pallas_call x1, Pallas kernels, backward(): pl.pallas_call(backward_kernel, out_shape=[jax.ShapeDtypeStruct(kv[0].sha...  9.14 us
    ppermute x3, starting transfers between devices, swap_cores(): return lax.ppermute(array, 'ctx', CORE_SWAP)  8.84 us
  transfers between devices with their start and end apart: 29, of which 16 were waited for; matrix products, arithmetic and copies ran while one was open for 3% of the time, Pallas kernels for 8%

profile of v2, /device:TPU:1, one launch (start us, length us, event | category | flops | bytes accessed | tf_op | source)
XLA Modules:
  0.0 131.5 jit_solution(7719183292666713896)
XLA Ops:
  0.6 2.2 %collective-permute-start.4 = (bf16[256,1024]{1,0:T(8,128)(2,1)}, bf16[256,1024]{1,0:T(8,128)(2,1)S(1)}, u32[]{:S(2)}, u32[]{:S(2)}) collective-permute-start(bf16[256,1024]{1,0:T(8,128)(2,1)} %refs_2_.1), channel_id=1, source_target_pairs={{0,1},{1,2},{2,3},{3,0},{4,5},{5,6},{6,7},{7,4},{8,9},{9,10},{10,1... | collective-permute-start | bytes 1572872 | tf_op jit(solution)/shard_map/ppermute | solution.py:37
  2.8 1.5 %collective-permute-start.5 = (bf16[256,1024]{1,0:T(8,128)(2,1)}, bf16[256,1024]{1,0:T(8,128)(2,1)S(1)}, u32[]{:S(2)}, u32[]{:S(2)}) collective-permute-start(bf16[256,1024]{1,0:T(8,128)(2,1)} %refs_2_.1), channel_id=1, source_target_pairs={{0,3},{1,0},{2,1},{3,2},{4,7},{5,4},{6,5},{7,6},{8,11},{9,8},{10,9... | collective-permute-start | bytes 1572872 | tf_op jit(solution)/shard_map/ppermute | solution.py:37
  6.5 2.5 %collective-permute-start.1 = (bf16[32,256]{1,0:T(8,128)(2,1)S(1)}, bf16[32,256]{1,0:T(8,128)(2,1)S(1)}, u32[]{:S(2)}, u32[]{:S(2)}) collective-permute-start(bf16[32,256]{1,0:T(8,128)(2,1)S(1)} %get-tuple-element.95), channel_id=1, source_target_pairs={{0,16},{4,20},{8,24},{12,28},{16,0},{20,4},{24,8},{28,12},{32,48},... | collective-permute-start | bytes 49160 | tf_op jit(solution)/shard_map/ppermute | solution.py:47
  11.2 2.2 %copy-done.1 = bf16[4096,512]{1,0:T(8,128)(2,1)S(1)} copy-done((bf16[4096,512]{1,0:T(8,128)(2,1)S(1)}, bf16[4096,512]{1,0:T(8,128)(2,1)}, u32[]{:S(2)}) %copy-start.1) | copy-done | bytes 4194328
  13.4 2.2 %copy-done.2 = bf16[4096,512]{1,0:T(8,128)(2,1)S(1)} copy-done((bf16[4096,512]{1,0:T(8,128)(2,1)S(1)}, bf16[4096,512]{1,0:T(8,128)(2,1)}, u32[]{:S(2)}) %copy-start.2) | copy-done | bytes 4194328
  17.9 7.0 %collective-permute-start.3 = (bf16[128,256]{1,0:T(8,128)(2,1)S(1)}, bf16[128,256]{1,0:T(8,128)(2,1)S(1)}, u32[]{:S(2)}, u32[]{:S(2)}) collective-permute-start(bf16[128,256]{1,0:T(8,128)(2,1)S(1)} %pad_maximum_fusion.2), channel_id=1, source_target_pairs={{0,128},{4,132},{8,136},{12,140},{16,144},{20,148},{24,152},{28,15... | collective-permute-start | bytes 196616 | tf_op jit(solution)/shard_map/ppermute | solution.py:57
  24.9 1.7 %collective-permute-done.3 = bf16[128,256]{1,0:T(8,128)(2,1)S(1)} collective-permute-done((bf16[128,256]{1,0:T(8,128)(2,1)S(1)}, bf16[128,256]{1,0:T(8,128)(2,1)S(1)}, u32[]{:S(2)}, u32[]{:S(2)}) %collective-permute-start.3) | collective-permute-done | bytes 65568 | tf_op jit(solution)/shard_map/ppermute | solution.py:57
  26.8 2.7 %collective-permute-start.8 = (bf16[128,1024]{1,0:T(8,128)(2,1)S(1)}, bf16[128,1024]{1,0:T(8,128)(2,1)S(1)}, u32[]{:S(2)}, u32[]{:S(2)}) collective-permute-start(bf16[128,1024]{1,0:T(8,128)(2,1)S(1)} %slice.81), channel_id=1, source_target_pairs={{0,3},{1,0},{2,1},{3,2},{4,7},{5,4},{6,5},{7,6},{8,11},{9,8},{10,9... | collective-permute-start | bytes 786440 | tf_op jit(solution)/shard_map/ppermute | solution.py:37
  29.6 1.4 %collective-permute-start.6 = (bf16[256,256]{1,0:T(8,128)(2,1)S(1)}, bf16[256,256]{1,0:T(8,128)(2,1)S(1)}, u32[]{:S(2)}, u32[]{:S(2)}) collective-permute-start(bf16[256,256]{1,0:T(8,128)(2,1)S(1)} %constant_dynamic-update-slice_fusion), channel_id=1, source_target_pairs={{0,64},{4,68},{8,72},{12,76},{16,80},{20,84},{24,88},{28,92},{32,9... | collective-permute-start | bytes 393224 | tf_op jit(solution)/shard_map/ppermute | solution.py:57
  30.9 1.8 %project.4.refs_4_ = f32[2,256,512]{2,1,0:T(8,128)S(1)} custom-call(s32[4]{0:T(128)S(1)} %pad_add_fusion.at_ref, bf16[4096,512]{1,0:T(8,128)(2,1)S(1)} %get-tuple-element.46.refs_0_.wk_ref, bf16[4096,512]{1,0:T(8,128)(2,1)S(1)} %get-tuple-element.47.refs_1_.wv_ref, bf16[256,1024]{1,0:T(8,128)(2,1)S(1)} %collective-permute-done.4.refs_2_, ...), custom_call_target="tpu_custom_call" | custom-call | tf_op jit(solution)/shard_map/project/pallas_call | solution.py:146
  32.8 3.2 %collective-permute-done.6 = bf16[256,256]{1,0:T(8,128)(2,1)S(1)} collective-permute-done((bf16[256,256]{1,0:T(8,128)(2,1)S(1)}, bf16[256,256]{1,0:T(8,128)(2,1)S(1)}, u32[]{:S(2)}, u32[]{:S(2)}) %collective-permute-start.6) | collective-permute-done | bytes 131104 | tf_op jit(solution)/shard_map/ppermute | solution.py:57
  36.1 1.4 %project.5 = (bf16[2,256,128]{2,1,0:T(8,128)(2,1)S(1)}, bf16[2,256,128]{2,1,0:T(8,128)(2,1)S(1)}, bf16[2,256,128]{2,1,0:T(8,128)(2,1)S(1)}, bf16[2,256,128]{2,1,0:T(8,128)(2,1)S(1)}) custom-call(s32[4]{0:T(128)S(1)} %pad_add_fusion.at_ref, bf16[4096,512]{1,0:T(8,128)(2,1)S(1)} %get-tuple-element.46.refs_0_.wk_ref, ...), custom_call_target="tpu_custom_call" | custom-call | tf_op jit(solution)/shard_map/project/pallas_call | solution.py:146
  37.6 4.1 %collective-permute-done.9 = bf16[512,256]{1,0:T(8,128)(2,1)S(1)} collective-permute-done((bf16[512,256]{1,0:T(8,128)(2,1)S(1)}, bf16[512,256]{1,0:T(8,128)(2,1)S(1)}, u32[]{:S(2)}, u32[]{:S(2)}) %collective-permute-start.9) | collective-permute-done | bytes 262176 | tf_op jit(solution)/shard_map/ppermute | solution.py:57
  41.7 5.3 %collective-permute-start.13 = (bf16[1024,256]{1,0:T(8,128)(2,1)S(1)}, bf16[1024,256]{1,0:T(8,128)(2,1)S(1)}, u32[]{:S(2)}, u32[]{:S(2)}) collective-permute-start(bf16[1024,256]{1,0:T(8,128)(2,1)S(1)} %pad_maximum_fusion.refs_4_), channel_id=1, source_target_pairs={{0,4},{4,0},{8,12},{12,8},{16,20},{20,16},{24,28},{28,24},{32,36},... | collective-permute-start | bytes 1572872 | tf_op jit(solution)/shard_map/ppermute | solution.py:33
  47.9 1.8 %collective-permute-start.12 = (bf16[2,256,128]{2,1,0:T(8,128)(2,1)S(1)}, bf16[2,256,128]{2,1,0:T(8,128)(2,1)S(1)}, u32[]{:S(2)}, u32[]{:S(2)}) collective-permute-start(bf16[2,256,128]{2,1,0:T(8,128)(2,1)S(1)} %get-tuple-element.63), channel_id=1, source_target_pairs={{0,24},{4,28},{8,0},{12,4},{16,8},{20,12},{24,16},{28,20},{32,56},... | collective-permute-start | bytes 393224 | tf_op jit(solution)/shard_map/ppermute | solution.py:47
  49.7 6.4 %collective-permute-done.10.refs_1_ = bf16[2,256,128]{2,1,0:T(8,128)(2,1)S(1)} collective-permute-done((bf16[2,256,128]{2,1,0:T(8,128)(2,1)S(1)}, bf16[2,256,128]{2,1,0:T(8,128)(2,1)S(1)}, u32[]{:S(2)}, u32[]{:S(2)}) %collective-permute-start.10) | collective-permute-done | bytes 131104 | tf_op jit(solution)/shard_map/ppermute | solution.py:47
  56.3 4.2 %latent_stats.1 = f32[3,2,8,128]{3,2,1,0:T(8,128)S(1)} custom-call(s32[4]{0:T(128)S(1)} %pad_add_fusion.at_ref, bf16[2,256,128]{2,1,0:T(8,128)(2,1)S(1)} %get-tuple-element.60.refs_0_, bf16[2,256,128]{2,1,0:T(8,128)(2,1)S(1)} %collective-permute-done.10.refs_1_, bf16[2,256,128]{2,1,0:T(8,128)(2,1)S(1)} %collective-permute-done.11.refs_2_, ...), custom_call_target="tpu_custom_call" | custom-call | tf_op jit(solution)/shard_map/latent_stats/pallas_call | solution.py:213
  62.7 16.3 %all_to_all.5.refs_7_ = f32[8,3,2,8,128]{4,3,2,1,0:T(8,128)S(1)} all-to-all(f32[8,3,2,8,128]{4,3,2,1,0:T(8,128)S(1)} %broadcast_in_dim.2), channel_id=1, replica_groups={{0,32,64,96,128,160,192,224},{4,36,68,100,132,164,196,228},{8,40,72,104..., dimensions={0} | all-to-all | bytes 393216 | tf_op jit(solution)/shard_map/all_to_all | solution.py:61
  79.0 9.1 %backward.1 = (bf16[2,256,128]{2,1,0:T(8,128)(2,1)S(1)}, bf16[2,256,128]{2,1,0:T(8,128)(2,1)S(1)}, bf16[2,256,128]{2,1,0:T(8,128)(2,1)S(1)}, bf16[2,256,128]{2,1...) custom-call(s32[4]{0:T(128)S(1)} %pad_add_fusion.at_ref, ...), custom_call_target="tpu_custom_call" | custom-call | tf_op jit(solution)/shard_map/backward/pallas_call | solution.py:275
  88.2 2.3 %collective-permute-start.15 = (bf16[1024,256]{1,0:T(8,128)(2,1)S(1)}, bf16[1024,256]{1,0:T(8,128)(2,1)S(1)}, u32[]{:S(2)}, u32[]{:S(2)}) collective-permute-start(bf16[1024,256]{1,0:T(8,128)(2,1)S(1)} %get-tuple-element.67), channel_id=1, source_target_pairs={{0,4},{4,0},{8,12},{12,8},{16,20},{20,16},{24,28},{28,24},{32,36},... | collective-permute-start | bytes 1572872 | tf_op jit(solution)/shard_map/ppermute | solution.py:33
  90.4 1.5 %collective-permute-done.15 = bf16[1024,256]{1,0:T(8,128)(2,1)S(1)} collective-permute-done((bf16[1024,256]{1,0:T(8,128)(2,1)S(1)}, bf16[1024,256]{1,0:T(8,128)(2,1)S(1)}, u32[]{:S(2)}, u32[]{:S(2)}) %collective-permute-start.15) | collective-permute-done | bytes 524320 | tf_op jit(solution)/shard_map/ppermute | solution.py:33
  92.6 2.1 %collective-permute-start.17 = (bf16[2,256,128]{2,1,0:T(8,128)(2,1)S(1)}, bf16[2,256,128]{2,1,0:T(8,128)(2,1)S(1)}, u32[]{:S(2)}, u32[]{:S(2)}) collective-permute-start(bf16[2,256,128]{2,1,0:T(8,128)(2,1)S(1)} %get-tuple-element.69), channel_id=1, source_target_pairs={{0,24},{4,28},{8,0},{12,4},{16,8},{20,12},{24,16},{28,20},{32,56},... | collective-permute-start | bytes 393224 | tf_op jit(solution)/shard_map/ppermute | solution.py:47
  95.2 2.3 %collective-permute-done.17.refs_1_ = bf16[2,256,128]{2,1,0:T(8,128)(2,1)S(1)} collective-permute-done((bf16[2,256,128]{2,1,0:T(8,128)(2,1)S(1)}, bf16[2,256,128]{2,1,0:T(8,128)(2,1)S(1)}, u32[]{:S(2)}, u32[]{:S(2)}) %collective-permute-start.17) | collective-permute-done | bytes 131104 | tf_op jit(solution)/shard_map/ppermute | solution.py:47
  97.5 2.5 %collective-permute-done.18.refs_2_ = bf16[2,256,128]{2,1,0:T(8,128)(2,1)S(1)} collective-permute-done((bf16[2,256,128]{2,1,0:T(8,128)(2,1)S(1)}, bf16[2,256,128]{2,1,0:T(8,128)(2,1)S(1)}, u32[]{:S(2)}, u32[]{:S(2)}) %collective-permute-start.18) | collective-permute-done | bytes 131104 | tf_op jit(solution)/shard_map/ppermute | solution.py:47
  100.0 3.7 %collective-permute-done.19.refs_3_ = bf16[2,256,128]{2,1,0:T(8,128)(2,1)S(1)} collective-permute-done((bf16[2,256,128]{2,1,0:T(8,128)(2,1)S(1)}, bf16[2,256,128]{2,1,0:T(8,128)(2,1)S(1)}, u32[]{:S(2)}, u32[]{:S(2)}) %collective-permute-start.19) | collective-permute-done | bytes 131104 | tf_op jit(solution)/shard_map/ppermute | solution.py:47
  103.7 2.1 %context_terms.2 = (bf16[128,1024]{1,0:T(8,128)(2,1)}, bf16[128,1024]{1,0:T(8,128)(2,1)}) custom-call(s32[4]{0:T(128)S(1)} %pad_add_fusion.at_ref, bf16[4096,512]{1,0:T(8,128)(2,1)S(1)} %get-tuple-element.46.refs_0_.wk_ref, bf16[4096,512]{1,0:T(8,128)(2,1)S(1)} %get-tuple-element.47.refs_1_.wv_ref, bf16[2,256,128]{2,1,0:T(8,128)(2,1)S(1)} %get-tuple-element.68.refs_0_, ...), custom_call_target="tpu_custom_call" | custom-call | tf_op jit(solution)/shard_map/context_terms/pallas_call | solution.py:313
  106.3 2.7 %collective-permute-start.23 = (bf16[128,1024]{1,0:T(8,128)(2,1)}, bf16[128,1024]{1,0:T(8,128)(2,1)}, u32[]{:S(2)}, u32[]{:S(2)}) collective-permute-start(bf16[128,1024]{1,0:T(8,128)(2,1)} %get-tuple-element.80), channel_id=1, source_target_pairs={{0,3},{1,0},{2,1},{3,2},{4,7},{5,4},{6,5},{7,6},{8,11},{9,8},{10,9... | collective-permute-start | bytes 786440 | tf_op jit(solution)/shard_map/ppermute | solution.py:37
  109.0 2.5 %context_terms.3 = (f32[256,1024]{1,0:T(8,128)S(1)}, f32[256,1024]{1,0:T(8,128)S(1)}, f32[256,1024]{1,0:T(8,128)S(1)}) custom-call(s32[4]{0:T(128)S(1)} %pad_add_fusion.at_ref, bf16[4096,512]{1,0:T(8,128)(2,1)S(1)} %get-tuple-element.46.refs_0_.wk_ref, bf16[4096,512]{1,0:T(8,128)(2,1)S(1)} %get-tuple-element.47.refs_1_.wv_ref, ...), custom_call_target="tpu_custom_call" | custom-call | tf_op jit(solution)/shard_map/context_terms/pallas_call | solution.py:313
  111.4 2.8 %collective-permute-done.20 = bf16[256,256]{1,0:T(8,128)(2,1)S(1)} collective-permute-done((bf16[256,256]{1,0:T(8,128)(2,1)S(1)}, bf16[256,256]{1,0:T(8,128)(2,1)S(1)}, u32[]{:S(2)}, u32[]{:S(2)}) %collective-permute-start.20) | collective-permute-done | bytes 131104 | tf_op jit(solution)/shard_map/ppermute | solution.py:57
  117.2 2.7 %collective-permute-start.28 = (bf16[256,1024]{1,0:T(8,128)(2,1)S(1)}, bf16[256,1024]{1,0:T(8,128)(2,1)S(1)}, u32[]{:S(2)}, u32[]{:S(2)}) collective-permute-start(bf16[256,1024]{1,0:T(8,128)(2,1)S(1)} %get-tuple-element.86), channel_id=1, source_target_pairs={{0,3},{1,0},{2,1},{3,2},{4,7},{5,4},{6,5},{7,6},{8,11},{9,8},{10,9... | collective-permute-start | bytes 1572872 | tf_op jit(solution)/shard_map/ppermute | solution.py:37
  119.9 2.7 %collective-permute-done.21 = bf16[128,256]{1,0:T(8,128)(2,1)} collective-permute-done((bf16[128,256]{1,0:T(8,128)(2,1)S(1)}, bf16[128,256]{1,0:T(8,128)(2,1)}, u32[]{:S(2)}, u32[]{:S(2)}) %collective-permute-start.21) | collective-permute-done | bytes 65568 | tf_op jit(solution)/shard_map/ppermute | solution.py:57
  125.1 1.4 %collective-permute-done.24 = bf16[32,256]{1,0:T(8,128)(2,1)S(1)} collective-permute-done((bf16[32,256]{1,0:T(8,128)(2,1)S(1)}, bf16[32,256]{1,0:T(8,128)(2,1)S(1)}, u32[]{:S(2)}, u32[]{:S(2)}) %collective-permute-start.24) | collective-permute-done | bytes 16416 | tf_op jit(solution)/shard_map/ppermute | solution.py:47
  (91 shorter events, 22.3 us)
Async XLA Ops:
  0.6 3.8 %copy-start = (bf16[32,512]{1,0:T(8,128)(2,1)S(1)}, bf16[32,512]{1,0:T(8,128)(2,1)}, u32[]{:S(2)}) copy-start(bf16[32,512]{1,0:T(8,128)(2,1)} %param.9) | copy-start | bytes 98308
  0.6 26.0 %collective-permute-start.4 = (bf16[256,1024]{1,0:T(8,128)(2,1)}, bf16[256,1024]{1,0:T(8,128)(2,1)S(1)}, u32[]{:S(2)}, u32[]{:S(2)}) collective-permute-start(bf16[256,1024]{1,0:T(8,128)(2,1)} %refs_2_.1), channel_id=1, source_target_pairs={{0,1},{1,2},{2,3},{3,0},{4,5},{5,6},{6,7},{7,4},{8,9},{9,10},{10,1... | collective-permute-start | bytes 1572872 | tf_op jit(solution)/shard_map/ppermute | solution.py:37
  2.8 23.8 %collective-permute-start.5 = (bf16[256,1024]{1,0:T(8,128)(2,1)}, bf16[256,1024]{1,0:T(8,128)(2,1)S(1)}, u32[]{:S(2)}, u32[]{:S(2)}) collective-permute-start(bf16[256,1024]{1,0:T(8,128)(2,1)} %refs_2_.1), channel_id=1, source_target_pairs={{0,3},{1,0},{2,1},{3,2},{4,7},{5,4},{6,5},{7,6},{8,11},{9,8},{10,9... | collective-permute-start | bytes 1572872 | tf_op jit(solution)/shard_map/ppermute | solution.py:37
  5.2 12.7 %collective-permute-start = (bf16[32,256]{1,0:T(8,128)(2,1)S(1)}, bf16[32,256]{1,0:T(8,128)(2,1)S(1)}, u32[]{:S(2)}, u32[]{:S(2)}) collective-permute-start(bf16[32,256]{1,0:T(8,128)(2,1)S(1)} %get-tuple-element.96), channel_id=1, source_target_pairs={{0,8},{4,12},{8,16},{12,20},{16,24},{20,28},{24,0},{28,4},{32,40},... | collective-permute-start | bytes 49160 | tf_op jit(solution)/shard_map/ppermute | solution.py:47
  6.5 11.4 %collective-permute-start.1 = (bf16[32,256]{1,0:T(8,128)(2,1)S(1)}, bf16[32,256]{1,0:T(8,128)(2,1)S(1)}, u32[]{:S(2)}, u32[]{:S(2)}) collective-permute-start(bf16[32,256]{1,0:T(8,128)(2,1)S(1)} %get-tuple-element.95), channel_id=1, source_target_pairs={{0,16},{4,20},{8,24},{12,28},{16,0},{20,4},{24,8},{28,12},{32,48},... | collective-permute-start | bytes 49160 | tf_op jit(solution)/shard_map/ppermute | solution.py:47
  9.0 8.9 %collective-permute-start.2 = (bf16[32,256]{1,0:T(8,128)(2,1)S(1)}, bf16[32,256]{1,0:T(8,128)(2,1)S(1)}, u32[]{:S(2)}, u32[]{:S(2)}) collective-permute-start(bf16[32,256]{1,0:T(8,128)(2,1)S(1)} %get-tuple-element.94), channel_id=1, source_target_pairs={{0,24},{4,28},{8,0},{12,4},{16,8},{20,12},{24,16},{28,20},{32,56},... | collective-permute-start | bytes 49160 | tf_op jit(solution)/shard_map/ppermute | solution.py:47
  11.2 2.2 %copy-start.1 = (bf16[4096,512]{1,0:T(8,128)(2,1)S(1)}, bf16[4096,512]{1,0:T(8,128)(2,1)}, u32[]{:S(2)}) copy-start(bf16[4096,512]{1,0:T(8,128)(2,1)} %refs_0_.1) | copy-start | bytes 12582916
  13.4 2.2 %copy-start.2 = (bf16[4096,512]{1,0:T(8,128)(2,1)S(1)}, bf16[4096,512]{1,0:T(8,128)(2,1)}, u32[]{:S(2)}) copy-start(bf16[4096,512]{1,0:T(8,128)(2,1)} %refs_1_.1) | copy-start | bytes 12582916
  17.9 8.7 %collective-permute-start.3 = (bf16[128,256]{1,0:T(8,128)(2,1)S(1)}, bf16[128,256]{1,0:T(8,128)(2,1)S(1)}, u32[]{:S(2)}, u32[]{:S(2)}) collective-permute-start(bf16[128,256]{1,0:T(8,128)(2,1)S(1)} %pad_maximum_fusion.2), channel_id=1, source_target_pairs={{0,128},{4,132},{8,136},{12,140},{16,144},{20,148},{24,152},{28,15... | collective-permute-start | bytes 196616 | tf_op jit(solution)/shard_map/ppermute | solution.py:57
  26.7 9.3 %collective-permute-start.7 = (bf16[128,1024]{1,0:T(8,128)(2,1)S(1)}, bf16[128,1024]{1,0:T(8,128)(2,1)S(1)}, u32[]{:S(2)}, u32[]{:S(2)}) collective-permute-start(bf16[128,1024]{1,0:T(8,128)(2,1)S(1)} %slice.80), channel_id=1, source_target_pairs={{0,1},{1,2},{2,3},{3,0},{4,5},{5,6},{6,7},{7,4},{8,9},{9,10},{10,1... | collective-permute-start | bytes 786440 | tf_op jit(solution)/shard_map/ppermute | solution.py:37
  26.8 9.2 %collective-permute-start.8 = (bf16[128,1024]{1,0:T(8,128)(2,1)S(1)}, bf16[128,1024]{1,0:T(8,128)(2,1)S(1)}, u32[]{:S(2)}, u32[]{:S(2)}) collective-permute-start(bf16[128,1024]{1,0:T(8,128)(2,1)S(1)} %slice.81), channel_id=1, source_target_pairs={{0,3},{1,0},{2,1},{3,2},{4,7},{5,4},{6,5},{7,6},{8,11},{9,8},{10,9... | collective-permute-start | bytes 786440 | tf_op jit(solution)/shard_map/ppermute | solution.py:37
  29.6 6.4 %collective-permute-start.6 = (bf16[256,256]{1,0:T(8,128)(2,1)S(1)}, bf16[256,256]{1,0:T(8,128)(2,1)S(1)}, u32[]{:S(2)}, u32[]{:S(2)}) collective-permute-start(bf16[256,256]{1,0:T(8,128)(2,1)S(1)} %constant_dynamic-update-slice_fusion), channel_id=1, source_target_pairs={{0,64},{4,68},{8,72},{12,76},{16,80},{20,84},{24,88},{28,92},{32,9... | collective-permute-start | bytes 393224 | tf_op jit(solution)/shard_map/ppermute | solution.py:57
  36.0 5.6 %collective-permute-start.9 = (bf16[512,256]{1,0:T(8,128)(2,1)S(1)}, bf16[512,256]{1,0:T(8,128)(2,1)S(1)}, u32[]{:S(2)}, u32[]{:S(2)}) collective-permute-start(bf16[512,256]{1,0:T(8,128)(2,1)S(1)} %pad_maximum_fusion.1), channel_id=1, source_target_pairs={{0,32},{4,36},{8,40},{12,44},{16,48},{20,52},{24,56},{28,60},{32,0... | collective-permute-start | bytes 786440 | tf_op jit(solution)/shard_map/ppermute | solution.py:57
  41.7 14.7 %collective-permute-start.13 = (bf16[1024,256]{1,0:T(8,128)(2,1)S(1)}, bf16[1024,256]{1,0:T(8,128)(2,1)S(1)}, u32[]{:S(2)}, u32[]{:S(2)}) collective-permute-start(bf16[1024,256]{1,0:T(8,128)(2,1)S(1)} %pad_maximum_fusion.refs_4_), channel_id=1, source_target_pairs={{0,4},{4,0},{8,12},{12,8},{16,20},{20,16},{24,28},{28,24},{32,36},... | collective-permute-start | bytes 1572872 | tf_op jit(solution)/shard_map/ppermute | solution.py:33
  46.9 9.1 %collective-permute-start.10 = (bf16[2,256,128]{2,1,0:T(8,128)(2,1)S(1)}, bf16[2,256,128]{2,1,0:T(8,128)(2,1)S(1)}, u32[]{:S(2)}, u32[]{:S(2)}) collective-permute-start(bf16[2,256,128]{2,1,0:T(8,128)(2,1)S(1)} %get-tuple-element.61), channel_id=1, source_target_pairs={{0,8},{4,12},{8,16},{12,20},{16,24},{20,28},{24,0},{28,4},{32,40},... | collective-permute-start | bytes 393224 | tf_op jit(solution)/shard_map/ppermute | solution.py:47
  47.3 8.8 %collective-permute-start.11 = (bf16[2,256,128]{2,1,0:T(8,128)(2,1)S(1)}, bf16[2,256,128]{2,1,0:T(8,128)(2,1)S(1)}, u32[]{:S(2)}, u32[]{:S(2)}) collective-permute-start(bf16[2,256,128]{2,1,0:T(8,128)(2,1)S(1)} %get-tuple-element.62), channel_id=1, source_target_pairs={{0,16},{4,20},{8,24},{12,28},{16,0},{20,4},{24,8},{28,12},{32,48},... | collective-permute-start | bytes 393224 | tf_op jit(solution)/shard_map/ppermute | solution.py:47
  47.9 8.5 %collective-permute-start.12 = (bf16[2,256,128]{2,1,0:T(8,128)(2,1)S(1)}, bf16[2,256,128]{2,1,0:T(8,128)(2,1)S(1)}, u32[]{:S(2)}, u32[]{:S(2)}) collective-permute-start(bf16[2,256,128]{2,1,0:T(8,128)(2,1)S(1)} %get-tuple-element.63), channel_id=1, source_target_pairs={{0,24},{4,28},{8,0},{12,4},{16,8},{20,12},{24,16},{28,20},{32,56},... | collective-permute-start | bytes 393224 | tf_op jit(solution)/shard_map/ppermute | solution.py:47
  60.5 2.1 %collective-permute-start.14 = (f32[3,2,8,128]{3,2,1,0:T(8,128)S(1)}, f32[3,2,8,128]{3,2,1,0:T(8,128)S(1)}, u32[]{:S(2)}, u32[]{:S(2)}) collective-permute-start(f32[3,2,8,128]{3,2,1,0:T(8,128)S(1)} %latent_stats.1), channel_id=1, source_target_pairs={{0,4},{4,0},{8,12},{12,8},{16,20},{20,16},{24,28},{28,24},{32,36},... | collective-permute-start | bytes 73736 | tf_op jit(solution)/shard_map/ppermute | solution.py:33
  88.2 3.8 %collective-permute-start.15 = (bf16[1024,256]{1,0:T(8,128)(2,1)S(1)}, bf16[1024,256]{1,0:T(8,128)(2,1)S(1)}, u32[]{:S(2)}, u32[]{:S(2)}) collective-permute-start(bf16[1024,256]{1,0:T(8,128)(2,1)S(1)} %get-tuple-element.67), channel_id=1, source_target_pairs={{0,4},{4,0},{8,12},{12,8},{16,20},{20,16},{24,28},{28,24},{32,36},... | collective-permute-start | bytes 1572872 | tf_op jit(solution)/shard_map/ppermute | solution.py:33
  92.2 13.6 %collective-permute-start.16 = (bf16[512,256]{1,0:T(8,128)(2,1)S(1)}, bf16[512,256]{1,0:T(8,128)(2,1)S(1)}, u32[]{:S(2)}, u32[]{:S(2)}) collective-permute-start(bf16[512,256]{1,0:T(8,128)(2,1)S(1)} %slice.159), channel_id=1, source_target_pairs={{0,32},{4,36},{8,40},{12,44},{16,48},{20,52},{24,56},{28,60},{32,0... | collective-permute-start | bytes 786440 | tf_op jit(solution)/shard_map/ppermute | solution.py:57
  92.6 5.0 %collective-permute-start.17 = (bf16[2,256,128]{2,1,0:T(8,128)(2,1)S(1)}, bf16[2,256,128]{2,1,0:T(8,128)(2,1)S(1)}, u32[]{:S(2)}, u32[]{:S(2)}) collective-permute-start(bf16[2,256,128]{2,1,0:T(8,128)(2,1)S(1)} %get-tuple-element.69), channel_id=1, source_target_pairs={{0,24},{4,28},{8,0},{12,4},{16,8},{20,12},{24,16},{28,20},{32,56},... | collective-permute-start | bytes 393224 | tf_op jit(solution)/shard_map/ppermute | solution.py:47
  94.6 5.4 %collective-permute-start.18 = (bf16[2,256,128]{2,1,0:T(8,128)(2,1)S(1)}, bf16[2,256,128]{2,1,0:T(8,128)(2,1)S(1)}, u32[]{:S(2)}, u32[]{:S(2)}) collective-permute-start(bf16[2,256,128]{2,1,0:T(8,128)(2,1)S(1)} %get-tuple-element.70), channel_id=1, source_target_pairs={{0,16},{4,20},{8,24},{12,28},{16,0},{20,4},{24,8},{28,12},{32,48},... | collective-permute-start | bytes 393224 | tf_op jit(solution)/shard_map/ppermute | solution.py:47
  94.6 9.1 %collective-permute-start.19 = (bf16[2,256,128]{2,1,0:T(8,128)(2,1)S(1)}, bf16[2,256,128]{2,1,0:T(8,128)(2,1)S(1)}, u32[]{:S(2)}, u32[]{:S(2)}) collective-permute-start(bf16[2,256,128]{2,1,0:T(8,128)(2,1)S(1)} %get-tuple-element.71), channel_id=1, source_target_pairs={{0,8},{4,12},{8,16},{12,20},{16,24},{20,28},{24,0},{28,4},{32,40},... | collective-permute-start | bytes 393224 | tf_op jit(solution)/shard_map/ppermute | solution.py:47
  105.9 8.3 %collective-permute-start.20 = (bf16[256,256]{1,0:T(8,128)(2,1)S(1)}, bf16[256,256]{1,0:T(8,128)(2,1)S(1)}, u32[]{:S(2)}, u32[]{:S(2)}) collective-permute-start(bf16[256,256]{1,0:T(8,128)(2,1)S(1)} %slice.160), channel_id=1, source_target_pairs={{0,64},{4,68},{8,72},{12,76},{16,80},{20,84},{24,88},{28,92},{32,9... | collective-permute-start | bytes 393224 | tf_op jit(solution)/shard_map/ppermute | solution.py:57
  106.3 9.8 %collective-permute-start.22 = (bf16[128,1024]{1,0:T(8,128)(2,1)}, bf16[128,1024]{1,0:T(8,128)(2,1)S(1)}, u32[]{:S(2)}, u32[]{:S(2)}) collective-permute-start(bf16[128,1024]{1,0:T(8,128)(2,1)} %get-tuple-element.72), channel_id=1, source_target_pairs={{0,1},{1,2},{2,3},{3,0},{4,5},{5,6},{6,7},{7,4},{8,9},{9,10},{10,1... | collective-permute-start | bytes 786440 | tf_op jit(solution)/shard_map/ppermute | solution.py:37
  106.3 9.8 %collective-permute-start.23 = (bf16[128,1024]{1,0:T(8,128)(2,1)}, bf16[128,1024]{1,0:T(8,128)(2,1)}, u32[]{:S(2)}, u32[]{:S(2)}) collective-permute-start(bf16[128,1024]{1,0:T(8,128)(2,1)} %get-tuple-element.80), channel_id=1, source_target_pairs={{0,3},{1,0},{2,1},{3,2},{4,7},{5,4},{6,5},{7,6},{8,11},{9,8},{10,9... | collective-permute-start | bytes 786440 | tf_op jit(solution)/shard_map/ppermute | solution.py:37
  114.9 7.7 %collective-permute-start.21 = (bf16[128,256]{1,0:T(8,128)(2,1)S(1)}, bf16[128,256]{1,0:T(8,128)(2,1)}, u32[]{:S(2)}, u32[]{:S(2)}) collective-permute-start(bf16[128,256]{1,0:T(8,128)(2,1)S(1)} %slice.161), channel_id=1, source_target_pairs={{0,128},{4,132},{8,136},{12,140},{16,144},{20,148},{24,152},{28,15... | collective-permute-start | bytes 196616 | tf_op jit(solution)/shard_map/ppermute | solution.py:57
  117.2 13.4 %collective-permute-start.27 = (bf16[256,1024]{1,0:T(8,128)(2,1)S(1)}, bf16[256,1024]{1,0:T(8,128)(2,1)S(1)}, u32[]{:S(2)}, u32[]{:S(2)}) collective-permute-start(bf16[256,1024]{1,0:T(8,128)(2,1)S(1)} %get-tuple-element.81), channel_id=1, source_target_pairs={{0,1},{1,2},{2,3},{3,0},{4,5},{5,6},{6,7},{7,4},{8,9},{9,10},{10,1... | collective-permute-start | bytes 1572872 | tf_op jit(solution)/shard_map/ppermute | solution.py:37
  117.2 13.3 %collective-permute-start.28 = (bf16[256,1024]{1,0:T(8,128)(2,1)S(1)}, bf16[256,1024]{1,0:T(8,128)(2,1)S(1)}, u32[]{:S(2)}, u32[]{:S(2)}) collective-permute-start(bf16[256,1024]{1,0:T(8,128)(2,1)S(1)} %get-tuple-element.86), channel_id=1, source_target_pairs={{0,3},{1,0},{2,1},{3,2},{4,7},{5,4},{6,5},{7,6},{8,11},{9,8},{10,9... | collective-permute-start | bytes 1572872 | tf_op jit(solution)/shard_map/ppermute | solution.py:37
  123.6 3.0 %collective-permute-start.24 = (bf16[32,256]{1,0:T(8,128)(2,1)S(1)}, bf16[32,256]{1,0:T(8,128)(2,1)S(1)}, u32[]{:S(2)}, u32[]{:S(2)}) collective-permute-start(bf16[32,256]{1,0:T(8,128)(2,1)S(1)} %get-tuple-element.93), channel_id=1, source_target_pairs={{0,24},{4,28},{8,0},{12,4},{16,8},{20,12},{24,16},{28,20},{32,56},... | collective-permute-start | bytes 49160 | tf_op jit(solution)/shard_map/ppermute | solution.py:47
  123.7 4.2 %collective-permute-start.25 = (bf16[32,256]{1,0:T(8,128)(2,1)S(1)}, bf16[32,256]{1,0:T(8,128)(2,1)S(1)}, u32[]{:S(2)}, u32[]{:S(2)}) collective-permute-start(bf16[32,256]{1,0:T(8,128)(2,1)S(1)} %get-tuple-element.92), channel_id=1, source_target_pairs={{0,16},{4,20},{8,24},{12,28},{16,0},{20,4},{24,8},{28,12},{32,48},... | collective-permute-start | bytes 49160 | tf_op jit(solution)/shard_map/ppermute | solution.py:47
  123.9 5.0 %collective-permute-start.26 = (bf16[32,256]{1,0:T(8,128)(2,1)S(1)}, bf16[32,256]{1,0:T(8,128)(2,1)S(1)}, u32[]{:S(2)}, u32[]{:S(2)}) collective-permute-start(bf16[32,256]{1,0:T(8,128)(2,1)S(1)} %get-tuple-element.91), channel_id=1, source_target_pairs={{0,8},{4,12},{8,16},{12,20},{16,24},{20,28},{24,0},{28,4},{32,40},... | collective-permute-start | bytes 49160 | tf_op jit(solution)/shard_map/ppermute | solution.py:47
  (2 other events, 1.7 us)

commit v3 on v2

--- a/solution.py
+++ b/solution.py
@@ -29,6 +29,10 @@
 Z_GROUPS = [[place(z, x, c) for z in range(NZ)] for x in range(NX) for c in range(NC)]
 
 
+def after(array, *others):
+    return lax.optimization_barrier((array, *others))[0]
+
+
 def swap_cores(array):
     return lax.ppermute(array, "ctx", CORE_SWAP)
 
@@ -80,7 +84,7 @@
     return pl.CostEstimate(flops=0, bytes_accessed=0, transcendentals=0)
 
 
-def load_weights_kernel(*refs):
+def load_weights_kernel(at_ref, *refs):
     sources, targets, sem = refs[:2], refs[2:4], refs[4]
     copies = [pltpu.make_async_copy(*pair, sem.at[n]) for n, pair in enumerate(zip(sources, targets))]
     for copy in copies:
@@ -89,17 +93,17 @@
         copy.wait()
 
 
-def load_weights(wk, wv):
+def load_weights(at, wk, wv):
     return pl.pallas_call(
         load_weights_kernel,
         out_shape=[jax.ShapeDtypeStruct(w.shape, w.dtype) for w in (wk, wv)],
-        in_specs=[pl.BlockSpec(memory_space=pltpu.HBM)] * 2,
+        in_specs=[pl.BlockSpec(memory_space=pltpu.SMEM)] + [pl.BlockSpec(memory_space=pltpu.HBM)] * 2,
         out_specs=[pl.BlockSpec(memory_space=pltpu.VMEM)] * 2,
         scratch_shapes=[pltpu.SemaphoreType.DMA((2,))],
         compiler_params=compiler_params(),
         cost_estimate=cost(0, 4 * wk.size, 0),
         name="load_weights",
-    )(wk, wv)
+    )(at, wk, wv)
 
 
 def project_kernel(steps, first, last, at_ref, *refs):
@@ -178,7 +182,7 @@
 
 
 def stats_kernel(at_ref, *refs):
-    kv_refs, (own_ref, other_ref, lp_ref, out_ref) = refs[:NX], refs[NX:]
+    kv_refs, (own_ref, other_ref, lp_ref, out_ref, expo_ref, grads_ref) = refs[:NX], refs[NX:]
     rows = kv_refs[0].shape[1]
     for half, src in enumerate((own_ref, other_ref)):
         for block in range(src.shape[0] // BLOCK):
@@ -195,6 +199,8 @@
             for n in range(NX):
                 expo = jnp.exp2(scores[n] - peak)
                 grads = lax.dot_general(kv_refs[n][1], go, NT, preferred_element_type=F32)
+                expo_ref[half, block, n] = expo
+                grads_ref[half, block, n] = grads
                 total += jnp.sum(expo, axis=0, keepdims=True)
                 dots += jnp.sum(expo * grads, axis=0, keepdims=True)
             seen = peak > 0.5 * NEG_FILL
@@ -212,9 +218,10 @@
     work = NX * kv[0].shape[1] * 2 * own.shape[0]
     return pl.pallas_call(
         stats_kernel,
-        out_shape=jax.ShapeDtypeStruct((3, 2, own.shape[0] // 128, 128), F32),
+        out_shape=[jax.ShapeDtypeStruct((3, 2, own.shape[0] // 128, 128), F32)]
+        + [jax.ShapeDtypeStruct((2, own.shape[0] // BLOCK, NX, kv[0].shape[1], BLOCK), F32)] * 2,
         in_specs=[pl.BlockSpec(memory_space=pltpu.SMEM)] + [whole] * (NX + 3),
-        out_specs=whole,
+        out_specs=[whole] * 3,
         compiler_params=compiler_params(),
         cost_estimate=cost(4 * work * DH, 2 * 2**20, work),
         name="latent_stats",
@@ -224,7 +231,7 @@
 def backward_kernel(at_ref, *refs):
     kv_refs, refs = refs[:NX], refs[NX:]
     rows = kv_refs[0].shape[1]
-    (own_ref, other_ref, lp_ref, st_ref), refs = refs[:4], refs[4:]
+    (own_ref, other_ref, expo_ref, grads_ref, mine_ref, st_ref), refs = refs[:6], refs[6:]
     dkv_refs, (own_out, other_out, kvt_ref, acc_ref, fin_ref) = refs[:NX], refs[NX:]
     for n in range(NX):
         for kind in range(2):
@@ -239,24 +246,21 @@
         share = jnp.exp2(peaks[n] - top)
         total += share * st_ref[n, 1]
         dots += share * st_ref[n, 2]
-    fin_ref[0] = top
-    fin_ref[1] = jnp.log2(total)
-    fin_ref[2] = dots / total
+    fin_ref[0] = jnp.where(mine_ref[1] > 0.0, jnp.exp2(mine_ref[0] - top), 0.0) / total
+    fin_ref[1] = dots / total
 
     for half, (src, dst) in enumerate(((own_ref, own_out), (other_ref, other_out))):
         for block in range(src.shape[0] // BLOCK):
             at = pl.ds(block * BLOCK, BLOCK)
             q = src[at, :DH]
             go = src[at, DH:]
-            lp = row_of(at_ref, lp_ref, half, block)
-            peak, log_total, dot = (row_of(at_ref, fin_ref, k, half, block) for k in range(3))
+            share, dot = (row_of(at_ref, fin_ref, k, half, block) for k in range(2))
             attended = 0.0
             query_grad = 0.0
             for n in range(NX):
-                scores = masked_scores(first_position(at_ref, n, rows), kv_refs[n][0], q, lp)
-                probs = jnp.exp2((scores - peak) - log_total)
+                probs = expo_ref[half, block, n] * share
                 low = probs.astype(BF16)
-                grads = lax.dot_general(kv_refs[n][1], go, NT, preferred_element_type=F32)
+                grads = grads_ref[half, block, n]
                 score_grad = (probs * (grads - dot) * SCORE_SCALE).astype(BF16)
                 acc_ref[n, 1] += jnp.dot(low, go, preferred_element_type=F32)
                 acc_ref[n, 0] += jnp.dot(score_grad, q, preferred_element_type=F32)
@@ -268,7 +272,7 @@
         dkv_refs[n][...] = acc_ref[n].astype(BF16)
 
 
-def backward(at, kv, own, other, lp, stats):
+def backward(at, kv, own, other, expo, grads, mine, stats):
     whole = pl.BlockSpec(memory_space=pltpu.VMEM)
     rows = kv[0].shape[1]
     work = NX * rows * 2 * own.shape[0]
@@ -276,17 +280,17 @@
         backward_kernel,
         out_shape=[jax.ShapeDtypeStruct(kv[0].shape, BF16)] * NX
         + [jax.ShapeDtypeStruct(own.shape, F32), jax.ShapeDtypeStruct(own.shape, BF16)],
-        in_specs=[pl.BlockSpec(memory_space=pltpu.SMEM)] + [whole] * (NX + 4),
+        in_specs=[pl.BlockSpec(memory_space=pltpu.SMEM)] + [whole] * (NX + 6),
         out_specs=[whole] * (NX + 2),
         scratch_shapes=[
             pltpu.VMEM((NX, 2, DH, rows), BF16),
             pltpu.VMEM((NX, *kv[0].shape), F32),
-            pltpu.VMEM(stats.shape[1:], F32),
+            pltpu.VMEM((2, *stats.shape[2:]), F32),
         ],
         compiler_params=compiler_params(),
-        cost_estimate=cost(12 * work * DH, 5 * 2**20, work),
+        cost_estimate=cost(8 * work * DH, 5 * 2**20, 0),
         name="backward",
-    )(at, *kv, own, other, lp, stats)
+    )(at, *kv, own, other, expo, grads, mine, stats)
     return out[:NX], out[NX], out[NX + 1]
 
 
@@ -377,8 +381,6 @@
 
     rows = context.shape[0]
     ahead, behind = shift_y(context, 1), shift_y(context, -1)
-    weights = load_weights(key_weight, value_weight)
-    (total,) = project(at, *weights, {0: [context]}, None, False)
 
     both = jnp.concatenate(
         [queries.reshape(lat, heads, DH), out_grad.reshape(lat, heads, DH)], axis=2
@@ -386,19 +388,19 @@
     both = jnp.concatenate([both, both])
     by_turn = [lax.dynamic_slice_in_dim(both, x + turn, 1, 0)[0] for turn in range(NX)]
     own = jnp.concatenate([by_turn[0]] + [shift_x(by_turn[n], n) for n in range(1, NX)])
-    own = jnp.concatenate([own, flip_z(own, 4)])
-    own, total, ahead, behind = lax.optimization_barrier((own, total, ahead, behind))
+    got = [flip_z(own, bit) for bit in (4, 2, 6)]
+    own = jnp.concatenate([own, *got])
+    weights = load_weights(after(at, *got), key_weight, value_weight)
+    (total,) = project(at, *weights, {0: [context]}, None, False)
     far_upper, far_lower = shift_y(ahead[: rows // 2], 1), shift_y(behind[rows // 2 :], -1)
-    own = jnp.concatenate([own, flip_z(own, 2)])
     (total,) = project(at, *weights, {3: [ahead], 1: [behind]}, total, False)
-    own, total, far_upper, far_lower = lax.optimization_barrier((own, total, far_upper, far_lower))
+    own = after(own, far_upper, far_lower, total)
     own = jnp.concatenate([own, flip_z(own, 1)])
     kv = project(at, *weights, {2: [far_upper, far_lower]}, total, True)
-    own, kv = lax.optimization_barrier((own, kv))
     kv = [kv[0]] + [shift_x(kv[n], n) for n in range(1, NX)]
-    other = swap_cores(own)
-
-    stats = latent_stats(at, kv, own, other, lp)
+    other = swap_cores(after(own, *kv[1:]))
+
+    stats, expo, prob_grads = latent_stats(at, kv, own, other, lp)
     theirs = swap_cores(stats)[:, ::-1]
     peak = jnp.maximum(stats[0], theirs[0])
     mine_share = jnp.exp2(stats[0] - peak)
@@ -406,7 +408,7 @@
     joined = jnp.stack([peak] + [stats[k] * mine_share + theirs[k] * their_share for k in (1, 2)])
     every = exchange(jnp.broadcast_to(joined[None], (NZ, *joined.shape)), Z_GROUPS)
 
-    dkv, own_part, other_part = backward(at, kv, own, other, lp, every)
+    dkv, own_part, other_part = backward(at, kv, own, other, expo, prob_grads, stats, every)
     received = swap_cores(other_part)
     dkv = [dkv[0]] + [shift_x(dkv[n], -n) for n in range(1, NX)]
 
@@ -421,20 +423,18 @@
     add_upper, add_lower = shift_y(far_upper, 1), shift_y(far_lower, -1)
     part = own_part + received.astype(F32)
     part = halve(part, 1)
-    part, far_upper = lax.optimization_barrier((part, far_upper))
-    part = halve(part, 2)
+    part = halve(after(part, far_upper), 2)
 
     up, down, kept = terms((1, 3, 0), 1, F32)
-    part, up, down, kept = lax.optimization_barrier((part, up, down, kept))
-    part = halve(part, 4)
+    part = halve(after(part, kept), 4)
     up, down = join_terms(up, down, add_upper, add_lower)
     from_below, from_above = shift_y(up, 1), shift_y(down, -1)
-    part, up = lax.optimization_barrier((part, up))
-
+    part = after(part, up)
     part = part.astype(BF16).reshape(NX, lat, 2 * DH)
     part = jnp.stack([part[0]] + [shift_x(part[n], -n) for n in range(1, NX)])
     part = lax.dynamic_slice_in_dim(jnp.concatenate([part, part]), (heads - x) & 3, heads, 0)
-    part, kept = lax.optimization_barrier((part.transpose(1, 0, 2), kept))
+    part = part.transpose(1, 0, 2)
+    kept = after(kept, part)
     attended = part[:, :, :DH].reshape(lat, heads * DH)
     query_grad = part[:, :, DH:].reshape(lat, heads * DH)
 

time: 133 us -> 119 us (0.89)
  Pallas kernels: 25 us -> 20.9 us
  blocking collectives: 16.3 us -> 12.2 us
  waiting for transfers between devices: 36.1 us -> 32.9 us
    pallas_call x1, Pallas kernels: 9.14 us -> 4.36 us  [backward(): pl.pallas_call(backward_kernel, out_shape=[jax.ShapeDtypeStruct(kv[0].sha...]
    ppermute x6 -> x7, waiting for transfers between devices: 14.5 us -> 10.2 us  [flip_z(): return lax.ppermute(array, 'ctx', pairs)]
    all_to_all x1, blocking collectives: 16.3 us -> 12.2 us  [exchange(): lax.all_to_all(array, 'ctx', 0, 0, tiled=True, axis_index_groups=groups)]
    ppermute x3, waiting for transfers between devices: 2.39 us -> 3.92 us  [swap_cores(): return lax.ppermute(array, 'ctx', CORE_SWAP)]
    ppermute x12, waiting for transfers between devices: 19 us -> 17.5 us  [shift_x(): return lax.ppermute(array, 'ctx', pairs)]
    unnamed x21 -> x24, local copies, waits for them, and re-layouts: 5.58 us -> 5.15 us
    ppermute x6 -> x7, starting transfers between devices: 10.3 us -> 10.6 us  [flip_z(): return lax.ppermute(array, 'ctx', pairs)]
  transfers between devices with their start and end apart: 29 -> 30, of which waited for: 16 -> 16; matrix products, arithmetic and copies ran while one was open for 3% -> 4% of each run, Pallas kernels for 8% -> 9%
where the time goes in v3:
time: 119 us
  starting transfers between devices  42.2 us (35%)
  waiting for transfers between devices  32.9 us (28%)
  Pallas kernels  20.9 us (18%)
  blocking collectives  12.2 us (10%)
  local copies, waits for them, and re-layouts  8.21 us (7%)
  other arithmetic  1.41 us (1%)
    ppermute x12, waiting for transfers between devices, shift_x(): return lax.ppermute(array, 'ctx', pairs)  17.5 us
    ppermute x12, starting transfers between devices, shift_x(): return lax.ppermute(array, 'ctx', pairs)  12.4 us
    all_to_all x1, blocking collectives, exchange(): lax.all_to_all(array, 'ctx', 0, 0, tiled=True, axis_index_groups=groups)  12.2 us
    ppermute x8, starting transfers between devices, shift_y(): return lax.ppermute(array, 'tp', [(i, (i + step) % NY) for i in range(NY)])  10.9 us
    ppermute x7, starting transfers between devices, flip_z(): return lax.ppermute(array, 'ctx', pairs)  10.6 us
    ppermute x7, waiting for transfers between devices, flip_z(): return lax.ppermute(array, 'ctx', pairs)  10.2 us
    ppermute x3, starting transfers between devices, swap_cores(): return lax.ppermute(array, 'ctx', CORE_SWAP)  8.22 us
    unnamed x24, local copies, waits for them, and re-layouts  5.15 us
  transfers between devices with their start and end apart: 30, of which 16 were waited for; matrix products, arithmetic and copies ran while one was open for 4% of the time, Pallas kernels for 9%

profile of v3, /device:TPU:1, one launch (start us, length us, event | category | flops | bytes accessed | tf_op | source)
XLA Modules:
  0.0 118.8 jit_solution(12019667685372735610)
XLA Ops:
  0.6 2.2 %collective-permute-start.6 = (bf16[256,1024]{1,0:T(8,128)(2,1)}, bf16[256,1024]{1,0:T(8,128)(2,1)S(1)}, u32[]{:S(2)}, u32[]{:S(2)}) collective-permute-start(bf16[256,1024]{1,0:T(8,128)(2,1)} %refs_2_.1), channel_id=1, source_target_pairs={{0,1},{1,2},{2,3},{3,0},{4,5},{5,6},{6,7},{7,4},{8,9},{9,10},{10,1... | collective-permute-start | bytes 1572872 | tf_op jit(solution)/shard_map/ppermute | solution.py:41
  2.8 1.5 %collective-permute-start.8 = (bf16[256,1024]{1,0:T(8,128)(2,1)}, bf16[256,1024]{1,0:T(8,128)(2,1)S(1)}, u32[]{:S(2)}, u32[]{:S(2)}) collective-permute-start(bf16[256,1024]{1,0:T(8,128)(2,1)} %refs_2_.1), channel_id=1, source_target_pairs={{0,3},{1,0},{2,1},{3,2},{4,7},{5,4},{6,5},{7,6},{8,11},{9,8},{10,9... | collective-permute-start | bytes 1572872 | tf_op jit(solution)/shard_map/ppermute | solution.py:41
  6.5 2.5 %collective-permute-start.1 = (bf16[32,256]{1,0:T(8,128)(2,1)S(1)}, bf16[32,256]{1,0:T(8,128)(2,1)S(1)}, u32[]{:S(2)}, u32[]{:S(2)}) collective-permute-start(bf16[32,256]{1,0:T(8,128)(2,1)S(1)} %get-tuple-element.73), channel_id=1, source_target_pairs={{0,16},{4,20},{8,24},{12,28},{16,0},{20,4},{24,8},{28,12},{32,48},... | collective-permute-start | bytes 49160 | tf_op jit(solution)/shard_map/ppermute | solution.py:51
  11.9 6.1 %collective-permute-start.5 = (bf16[128,256]{1,0:T(8,128)(2,1)S(1)}, bf16[128,256]{1,0:T(8,128)(2,1)S(1)}, u32[]{:S(2)}, u32[]{:S(2)}) collective-permute-start(bf16[128,256]{1,0:T(8,128)(2,1)S(1)} %pad_maximum_fusion), channel_id=1, source_target_pairs={{0,192},{4,196},{8,200},{12,204},{16,208},{20,212},{24,216},{28,22... | collective-permute-start | bytes 196616 | tf_op jit(solution)/shard_map/ppermute | solution.py:61
  20.4 2.7 %collective-permute-start.9 = (bf16[128,1024]{1,0:T(8,128)(2,1)S(1)}, bf16[128,1024]{1,0:T(8,128)(2,1)S(1)}, u32[]{:S(2)}, u32[]{:S(2)}) collective-permute-start(bf16[128,1024]{1,0:T(8,128)(2,1)S(1)} %slice.105), channel_id=1, source_target_pairs={{0,3},{1,0},{2,1},{3,2},{4,7},{5,4},{6,5},{7,6},{8,11},{9,8},{10,9... | collective-permute-start | bytes 786440 | tf_op jit(solution)/shard_map/ppermute | solution.py:41
  23.1 3.8 %collective-permute-done.3 = bf16[128,256]{1,0:T(8,128)(2,1)S(1)} collective-permute-done((bf16[128,256]{1,0:T(8,128)(2,1)S(1)}, bf16[128,256]{1,0:T(8,128)(2,1)S(1)}, u32[]{:S(2)}, u32[]{:S(2)}) %collective-permute-start.3) | collective-permute-done | bytes 65568 | tf_op jit(solution)/shard_map/ppermute | solution.py:61
  26.9 2.2 %copy-done.1 = bf16[4096,512]{1,0:T(8,128)(2,1)S(1)} copy-done((bf16[4096,512]{1,0:T(8,128)(2,1)S(1)}, bf16[4096,512]{1,0:T(8,128)(2,1)}, u32[]{:S(2)}) %copy-start.1) | copy-done | bytes 4194328
  29.1 2.2 %copy-done.2 = bf16[4096,512]{1,0:T(8,128)(2,1)S(1)} copy-done((bf16[4096,512]{1,0:T(8,128)(2,1)S(1)}, bf16[4096,512]{1,0:T(8,128)(2,1)}, u32[]{:S(2)}) %copy-start.2) | copy-done | bytes 4194328
  33.7 1.8 %project.4.refs_4_ = f32[2,256,512]{2,1,0:T(8,128)S(1)} custom-call(s32[4]{0:T(128)S(1)} %pad_add_fusion.at_ref, bf16[4096,512]{1,0:T(8,128)(2,1)S(1)} %get-tuple-element.36.refs_0_.wk_ref, bf16[4096,512]{1,0:T(8,128)(2,1)S(1)} %get-tuple-element.37.refs_1_.wv_ref, bf16[256,1024]{1,0:T(8,128)(2,1)S(1)} %collective-permute-done.6.refs_2_, ...), custom_call_target="tpu_custom_call" | custom-call | tf_op jit(solution)/shard_map/project/pallas_call | solution.py:150
  35.7 1.4 %project.5 = (bf16[2,256,128]{2,1,0:T(8,128)(2,1)S(1)}, bf16[2,256,128]{2,1,0:T(8,128)(2,1)S(1)}, bf16[2,256,128]{2,1,0:T(8,128)(2,1)S(1)}, bf16[2,256,128]{2,1,0:T(8,128)(2,1)S(1)}) custom-call(s32[4]{0:T(128)S(1)} %pad_add_fusion.at_ref, bf16[4096,512]{1,0:T(8,128)(2,1)S(1)} %get-tuple-element.36.refs_0_.wk_ref, ...), custom_call_target="tpu_custom_call" | custom-call | tf_op jit(solution)/shard_map/project/pallas_call | solution.py:150
  37.5 3.3 %collective-permute-start.11 = (bf16[2,256,128]{2,1,0:T(8,128)(2,1)S(1)}, bf16[2,256,128]{2,1,0:T(8,128)(2,1)S(1)}, u32[]{:S(2)}, u32[]{:S(2)}) collective-permute-start(bf16[2,256,128]{2,1,0:T(8,128)(2,1)S(1)} %get-tuple-element.40), channel_id=1, source_target_pairs={{0,16},{4,20},{8,24},{12,28},{16,0},{20,4},{24,8},{28,12},{32,48},... | collective-permute-start | bytes 393224 | tf_op jit(solution)/shard_map/ppermute | solution.py:51
  42.3 2.3 %collective-permute-done.11.refs_2_ = bf16[2,256,128]{2,1,0:T(8,128)(2,1)S(1)} collective-permute-done((bf16[2,256,128]{2,1,0:T(8,128)(2,1)S(1)}, bf16[2,256,128]{2,1,0:T(8,128)(2,1)S(1)}, u32[]{:S(2)}, u32[]{:S(2)}) %collective-permute-start.11) | collective-permute-done | bytes 131104 | tf_op jit(solution)/shard_map/ppermute | solution.py:51
  44.9 5.7 %collective-permute-start.14 = (bf16[1024,256]{1,0:T(8,128)(2,1)S(1)}, bf16[1024,256]{1,0:T(8,128)(2,1)S(1)}, u32[]{:S(2)}, u32[]{:S(2)}) collective-permute-start(bf16[1024,256]{1,0:T(8,128)(2,1)S(1)} %constant_dynamic-update-slice_fusion.7.refs_4_), channel_id=1, source_target_pairs={{0,4},{4,0},{8,12},{12,8},{16,20},{20,16},{24,28},{28,24},{32,36},... | collective-permute-start | bytes 1572872 | tf_op jit(solution)/shard_map/ppermute | solution.py:37
  50.7 1.5 %collective-permute-done.14.refs_5_ = bf16[1024,256]{1,0:T(8,128)(2,1)S(1)} collective-permute-done((bf16[1024,256]{1,0:T(8,128)(2,1)S(1)}, bf16[1024,256]{1,0:T(8,128)(2,1)S(1)}, u32[]{:S(2)}, u32[]{:S(2)}) %collective-permute-start.14) | collective-permute-done | bytes 524320 | tf_op jit(solution)/shard_map/ppermute | solution.py:37
  52.2 4.3 %latent_stats.1 = (f32[3,2,8,128]{3,2,1,0:T(8,128)S(1)}, f32[2,4,4,256,256]{4,3,2,1,0:T(8,128)S(1)}, f32[2,4,4,256,256]{4,3,2,1,0:T(8,128)S(1)}) custom-call(s32[4]{0:T(128)S(1)} %pad_add_fusion.at_ref, bf16[2,256,128]{2,1,0:T(8,128)(2,1)S(1)} %get-tuple-element.38.refs_0_, bf16[2,256,128]{2,1,0:T(8,128)(2,1)S(1)} %collective-permute-done.10.refs_1_, ...), custom_call_target="tpu_custom_call" | custom-call | tf_op jit(solution)/shard_map/latent_stats/pallas_call | solution.py:219
  57.9 12.2 %all_to_all.5.refs_9_ = f32[8,3,2,8,128]{4,3,2,1,0:T(8,128)S(1)} all-to-all(f32[8,3,2,8,128]{4,3,2,1,0:T(8,128)S(1)} %broadcast_in_dim.2), channel_id=1, replica_groups={{0,32,64,96,128,160,192,224},{4,36,68,100,132,164,196,228},{8,40,72,104..., dimensions={0} | all-to-all | bytes 393216 | tf_op jit(solution)/shard_map/all_to_all | solution.py:65
  70.0 4.4 %backward.1 = (bf16[2,256,128]{2,1,0:T(8,128)(2,1)S(1)}, bf16[2,256,128]{2,1,0:T(8,128)(2,1)S(1)}, bf16[2,256,128]{2,1,0:T(8,128)(2,1)S(1)}, bf16[2,256,128]{2,1...) custom-call(s32[4]{0:T(128)S(1)} %pad_add_fusion.at_ref, ...), custom_call_target="tpu_custom_call" | custom-call | tf_op jit(solution)/shard_map/backward/pallas_call | solution.py:279
  74.4 2.0 %collective-permute-start.16 = (bf16[1024,256]{1,0:T(8,128)(2,1)S(1)}, bf16[1024,256]{1,0:T(8,128)(2,1)S(1)}, u32[]{:S(2)}, u32[]{:S(2)}) collective-permute-start(bf16[1024,256]{1,0:T(8,128)(2,1)S(1)} %get-tuple-element.49), channel_id=1, source_target_pairs={{0,4},{4,0},{8,12},{12,8},{16,20},{20,16},{24,28},{28,24},{32,36},... | collective-permute-start | bytes 1572872 | tf_op jit(solution)/shard_map/ppermute | solution.py:37
  76.5 1.5 %collective-permute-done.16 = bf16[1024,256]{1,0:T(8,128)(2,1)S(1)} collective-permute-done((bf16[1024,256]{1,0:T(8,128)(2,1)S(1)}, bf16[1024,256]{1,0:T(8,128)(2,1)S(1)}, u32[]{:S(2)}, u32[]{:S(2)}) %collective-permute-start.16) | collective-permute-done | bytes 524320 | tf_op jit(solution)/shard_map/ppermute | solution.py:37
  78.5 1.8 %collective-permute-start.18 = (bf16[2,256,128]{2,1,0:T(8,128)(2,1)S(1)}, bf16[2,256,128]{2,1,0:T(8,128)(2,1)S(1)}, u32[]{:S(2)}, u32[]{:S(2)}) collective-permute-start(bf16[2,256,128]{2,1,0:T(8,128)(2,1)S(1)} %get-tuple-element.51), channel_id=1, source_target_pairs={{0,24},{4,28},{8,0},{12,4},{16,8},{20,12},{24,16},{28,20},{32,56},... | collective-permute-start | bytes 393224 | tf_op jit(solution)/shard_map/ppermute | solution.py:51
  80.9 2.0 %collective-permute-done.18.refs_1_ = bf16[2,256,128]{2,1,0:T(8,128)(2,1)S(1)} collective-permute-done((bf16[2,256,128]{2,1,0:T(8,128)(2,1)S(1)}, bf16[2,256,128]{2,1,0:T(8,128)(2,1)S(1)}, u32[]{:S(2)}, u32[]{:S(2)}) %collective-permute-start.18) | collective-permute-done | bytes 131104 | tf_op jit(solution)/shard_map/ppermute | solution.py:51
  82.9 2.8 %collective-permute-done.19.refs_2_ = bf16[2,256,128]{2,1,0:T(8,128)(2,1)S(1)} collective-permute-done((bf16[2,256,128]{2,1,0:T(8,128)(2,1)S(1)}, bf16[2,256,128]{2,1,0:T(8,128)(2,1)S(1)}, u32[]{:S(2)}, u32[]{:S(2)}) %collective-permute-start.19) | collective-permute-done | bytes 131104 | tf_op jit(solution)/shard_map/ppermute | solution.py:51
  85.7 3.9 %collective-permute-done.20.refs_3_ = bf16[2,256,128]{2,1,0:T(8,128)(2,1)S(1)} collective-permute-done((bf16[2,256,128]{2,1,0:T(8,128)(2,1)S(1)}, bf16[2,256,128]{2,1,0:T(8,128)(2,1)S(1)}, u32[]{:S(2)}, u32[]{:S(2)}) %collective-permute-start.20) | collective-permute-done | bytes 131104 | tf_op jit(solution)/shard_map/ppermute | solution.py:51
  89.7 2.1 %context_terms.2 = (bf16[128,1024]{1,0:T(8,128)(2,1)}, bf16[128,1024]{1,0:T(8,128)(2,1)}) custom-call(s32[4]{0:T(128)S(1)} %pad_add_fusion.at_ref, bf16[4096,512]{1,0:T(8,128)(2,1)S(1)} %get-tuple-element.36.refs_0_.wk_ref, bf16[4096,512]{1,0:T(8,128)(2,1)S(1)} %get-tuple-element.37.refs_1_.wv_ref, bf16[2,256,128]{2,1,0:T(8,128)(2,1)S(1)} %get-tuple-element.50.refs_0_, ...), custom_call_target="tpu_custom_call" | custom-call | tf_op jit(solution)/shard_map/context_terms/pallas_call | solution.py:317
  92.5 2.6 %collective-permute-start.24 = (bf16[128,1024]{1,0:T(8,128)(2,1)}, bf16[128,1024]{1,0:T(8,128)(2,1)}, u32[]{:S(2)}, u32[]{:S(2)}) collective-permute-start(bf16[128,1024]{1,0:T(8,128)(2,1)} %get-tuple-element.60), channel_id=1, source_target_pairs={{0,3},{1,0},{2,1},{3,2},{4,7},{5,4},{6,5},{7,6},{8,11},{9,8},{10,9... | collective-permute-start | bytes 786440 | tf_op jit(solution)/shard_map/ppermute | solution.py:41
  95.1 2.5 %context_terms.3 = (f32[256,1024]{1,0:T(8,128)S(1)}, f32[256,1024]{1,0:T(8,128)S(1)}, f32[256,1024]{1,0:T(8,128)S(1)}) custom-call(s32[4]{0:T(128)S(1)} %pad_add_fusion.at_ref, bf16[4096,512]{1,0:T(8,128)(2,1)S(1)} %get-tuple-element.36.refs_0_.wk_ref, bf16[4096,512]{1,0:T(8,128)(2,1)S(1)} %get-tuple-element.37.refs_1_.wv_ref, ...), custom_call_target="tpu_custom_call" | custom-call | tf_op jit(solution)/shard_map/context_terms/pallas_call | solution.py:317
  97.6 2.8 %collective-permute-done.21 = bf16[256,256]{1,0:T(8,128)(2,1)S(1)} collective-permute-done((bf16[256,256]{1,0:T(8,128)(2,1)S(1)}, bf16[256,256]{1,0:T(8,128)(2,1)S(1)}, u32[]{:S(2)}, u32[]{:S(2)}) %collective-permute-start.21) | collective-permute-done | bytes 131104 | tf_op jit(solution)/shard_map/ppermute | solution.py:61
  103.3 1.7 %collective-permute-start.29 = (bf16[256,1024]{1,0:T(8,128)(2,1)S(1)}, bf16[256,1024]{1,0:T(8,128)(2,1)S(1)}, u32[]{:S(2)}, u32[]{:S(2)}) collective-permute-start(bf16[256,1024]{1,0:T(8,128)(2,1)S(1)} %get-tuple-element.64), channel_id=1, source_target_pairs={{0,3},{1,0},{2,1},{3,2},{4,7},{5,4},{6,5},{7,6},{8,11},{9,8},{10,9... | collective-permute-start | bytes 1572872 | tf_op jit(solution)/shard_map/ppermute | solution.py:41
  105.0 3.6 %collective-permute-done.22 = bf16[128,256]{1,0:T(8,128)(2,1)} collective-permute-done((bf16[128,256]{1,0:T(8,128)(2,1)S(1)}, bf16[128,256]{1,0:T(8,128)(2,1)}, u32[]{:S(2)}, u32[]{:S(2)}) %collective-permute-start.22) | collective-permute-done | bytes 65568 | tf_op jit(solution)/shard_map/ppermute | solution.py:61
  109.7 1.4 %collective-permute-start.27 = (bf16[32,256]{1,0:T(8,128)(2,1)S(1)}, bf16[32,256]{1,0:T(8,128)(2,1)S(1)}, u32[]{:S(2)}, u32[]{:S(2)}) collective-permute-start(bf16[32,256]{1,0:T(8,128)(2,1)S(1)} %get-tuple-element.69), channel_id=1, source_target_pairs={{0,8},{4,12},{8,16},{12,20},{16,24},{20,28},{24,0},{28,4},{32,40},... | collective-permute-start | bytes 49160 | tf_op jit(solution)/shard_map/ppermute | solution.py:51
  111.1 1.4 %collective-permute-done.25 = bf16[32,256]{1,0:T(8,128)(2,1)S(1)} collective-permute-done((bf16[32,256]{1,0:T(8,128)(2,1)S(1)}, bf16[32,256]{1,0:T(8,128)(2,1)S(1)}, u32[]{:S(2)}, u32[]{:S(2)}) %collective-permute-start.25) | collective-permute-done | bytes 16416 | tf_op jit(solution)/shard_map/ppermute | solution.py:51
  112.6 2.7 %collective-permute-done.26 = bf16[32,256]{1,0:T(8,128)(2,1)S(1)} collective-permute-done((bf16[32,256]{1,0:T(8,128)(2,1)S(1)}, bf16[32,256]{1,0:T(8,128)(2,1)S(1)}, u32[]{:S(2)}, u32[]{:S(2)}) %collective-permute-start.26) | collective-permute-done | bytes 16416 | tf_op jit(solution)/shard_map/ppermute | solution.py:51
  (95 shorter events, 22.7 us)
Async XLA Ops:
  0.6 3.8 %copy-start = (bf16[32,512]{1,0:T(8,128)(2,1)S(1)}, bf16[32,512]{1,0:T(8,128)(2,1)}, u32[]{:S(2)}) copy-start(bf16[32,512]{1,0:T(8,128)(2,1)} %param.9) | copy-start | bytes 98308
  0.6 19.6 %collective-permute-start.6 = (bf16[256,1024]{1,0:T(8,128)(2,1)}, bf16[256,1024]{1,0:T(8,128)(2,1)S(1)}, u32[]{:S(2)}, u32[]{:S(2)}) collective-permute-start(bf16[256,1024]{1,0:T(8,128)(2,1)} %refs_2_.1), channel_id=1, source_target_pairs={{0,1},{1,2},{2,3},{3,0},{4,5},{5,6},{6,7},{7,4},{8,9},{9,10},{10,1... | collective-permute-start | bytes 1572872 | tf_op jit(solution)/shard_map/ppermute | solution.py:41
  2.8 17.5 %collective-permute-start.8 = (bf16[256,1024]{1,0:T(8,128)(2,1)}, bf16[256,1024]{1,0:T(8,128)(2,1)S(1)}, u32[]{:S(2)}, u32[]{:S(2)}) collective-permute-start(bf16[256,1024]{1,0:T(8,128)(2,1)} %refs_2_.1), channel_id=1, source_target_pairs={{0,3},{1,0},{2,1},{3,2},{4,7},{5,4},{6,5},{7,6},{8,11},{9,8},{10,9... | collective-permute-start | bytes 1572872 | tf_op jit(solution)/shard_map/ppermute | solution.py:41
  5.2 6.0 %collective-permute-start = (bf16[32,256]{1,0:T(8,128)(2,1)S(1)}, bf16[32,256]{1,0:T(8,128)(2,1)S(1)}, u32[]{:S(2)}, u32[]{:S(2)}) collective-permute-start(bf16[32,256]{1,0:T(8,128)(2,1)S(1)} %get-tuple-element.72), channel_id=1, source_target_pairs={{0,8},{4,12},{8,16},{12,20},{16,24},{20,28},{24,0},{28,4},{32,40},... | collective-permute-start | bytes 49160 | tf_op jit(solution)/shard_map/ppermute | solution.py:51
  6.5 4.7 %collective-permute-start.1 = (bf16[32,256]{1,0:T(8,128)(2,1)S(1)}, bf16[32,256]{1,0:T(8,128)(2,1)S(1)}, u32[]{:S(2)}, u32[]{:S(2)}) collective-permute-start(bf16[32,256]{1,0:T(8,128)(2,1)S(1)} %get-tuple-element.73), channel_id=1, source_target_pairs={{0,16},{4,20},{8,24},{12,28},{16,0},{20,4},{24,8},{28,12},{32,48},... | collective-permute-start | bytes 49160 | tf_op jit(solution)/shard_map/ppermute | solution.py:51
  9.0 2.9 %collective-permute-start.2 = (bf16[32,256]{1,0:T(8,128)(2,1)S(1)}, bf16[32,256]{1,0:T(8,128)(2,1)S(1)}, u32[]{:S(2)}, u32[]{:S(2)}) collective-permute-start(bf16[32,256]{1,0:T(8,128)(2,1)S(1)} %get-tuple-element.74), channel_id=1, source_target_pairs={{0,24},{4,28},{8,0},{12,4},{16,8},{20,12},{24,16},{28,20},{32,56},... | collective-permute-start | bytes 49160 | tf_op jit(solution)/shard_map/ppermute | solution.py:51
  11.9 15.0 %collective-permute-start.5 = (bf16[128,256]{1,0:T(8,128)(2,1)S(1)}, bf16[128,256]{1,0:T(8,128)(2,1)S(1)}, u32[]{:S(2)}, u32[]{:S(2)}) collective-permute-start(bf16[128,256]{1,0:T(8,128)(2,1)S(1)} %pad_maximum_fusion), channel_id=1, source_target_pairs={{0,192},{4,196},{8,200},{12,204},{16,208},{20,212},{24,216},{28,22... | collective-permute-start | bytes 196616 | tf_op jit(solution)/shard_map/ppermute | solution.py:61
  18.0 8.9 %collective-permute-start.4 = (bf16[128,256]{1,0:T(8,128)(2,1)S(1)}, bf16[128,256]{1,0:T(8,128)(2,1)S(1)}, u32[]{:S(2)}, u32[]{:S(2)}) collective-permute-start(bf16[128,256]{1,0:T(8,128)(2,1)S(1)} %pad_maximum_fusion), channel_id=1, source_target_pairs={{0,64},{4,68},{8,72},{12,76},{16,80},{20,84},{24,88},{28,92},{32,9... | collective-permute-start | bytes 196616 | tf_op jit(solution)/shard_map/ppermute | solution.py:61
  19.2 7.7 %collective-permute-start.3 = (bf16[128,256]{1,0:T(8,128)(2,1)S(1)}, bf16[128,256]{1,0:T(8,128)(2,1)S(1)}, u32[]{:S(2)}, u32[]{:S(2)}) collective-permute-start(bf16[128,256]{1,0:T(8,128)(2,1)S(1)} %pad_maximum_fusion), channel_id=1, source_target_pairs={{0,128},{4,132},{8,136},{12,140},{16,144},{20,148},{24,152},{28,15... | collective-permute-start | bytes 196616 | tf_op jit(solution)/shard_map/ppermute | solution.py:61
  20.2 15.3 %collective-permute-start.7 = (bf16[128,1024]{1,0:T(8,128)(2,1)S(1)}, bf16[128,1024]{1,0:T(8,128)(2,1)S(1)}, u32[]{:S(2)}, u32[]{:S(2)}) collective-permute-start(bf16[128,1024]{1,0:T(8,128)(2,1)S(1)} %slice.104), channel_id=1, source_target_pairs={{0,1},{1,2},{2,3},{3,0},{4,5},{5,6},{6,7},{7,4},{8,9},{9,10},{10,1... | collective-permute-start | bytes 786440 | tf_op jit(solution)/shard_map/ppermute | solution.py:41
  20.4 15.2 %collective-permute-start.9 = (bf16[128,1024]{1,0:T(8,128)(2,1)S(1)}, bf16[128,1024]{1,0:T(8,128)(2,1)S(1)}, u32[]{:S(2)}, u32[]{:S(2)}) collective-permute-start(bf16[128,1024]{1,0:T(8,128)(2,1)S(1)} %slice.105), channel_id=1, source_target_pairs={{0,3},{1,0},{2,1},{3,2},{4,7},{5,4},{6,5},{7,6},{8,11},{9,8},{10,9... | collective-permute-start | bytes 786440 | tf_op jit(solution)/shard_map/ppermute | solution.py:41
  26.9 2.2 %copy-start.1 = (bf16[4096,512]{1,0:T(8,128)(2,1)S(1)}, bf16[4096,512]{1,0:T(8,128)(2,1)}, u32[]{:S(2)}) copy-start(bf16[4096,512]{1,0:T(8,128)(2,1)} %refs_0_.1) | copy-start | bytes 12582916
  35.6 5.3 %collective-permute-start.13 = (bf16[512,256]{1,0:T(8,128)(2,1)S(1)}, bf16[512,256]{1,0:T(8,128)(2,1)S(1)}, u32[]{:S(2)}, u32[]{:S(2)}) collective-permute-start(bf16[512,256]{1,0:T(8,128)(2,1)S(1)} %constant_dynamic-update-slice_fusion), channel_id=1, source_target_pairs={{0,32},{4,36},{8,40},{12,44},{16,48},{20,52},{24,56},{28,60},{32,0... | collective-permute-start | bytes 786440 | tf_op jit(solution)/shard_map/ppermute | solution.py:61
  37.2 5.1 %collective-permute-start.10 = (bf16[2,256,128]{2,1,0:T(8,128)(2,1)S(1)}, bf16[2,256,128]{2,1,0:T(8,128)(2,1)S(1)}, u32[]{:S(2)}, u32[]{:S(2)}) collective-permute-start(bf16[2,256,128]{2,1,0:T(8,128)(2,1)S(1)} %get-tuple-element.39), channel_id=1, source_target_pairs={{0,8},{4,12},{8,16},{12,20},{16,24},{20,28},{24,0},{28,4},{32,40},... | collective-permute-start | bytes 393224 | tf_op jit(solution)/shard_map/ppermute | solution.py:51
  37.5 7.1 %collective-permute-start.11 = (bf16[2,256,128]{2,1,0:T(8,128)(2,1)S(1)}, bf16[2,256,128]{2,1,0:T(8,128)(2,1)S(1)}, u32[]{:S(2)}, u32[]{:S(2)}) collective-permute-start(bf16[2,256,128]{2,1,0:T(8,128)(2,1)S(1)} %get-tuple-element.40), channel_id=1, source_target_pairs={{0,16},{4,20},{8,24},{12,28},{16,0},{20,4},{24,8},{28,12},{32,48},... | collective-permute-start | bytes 393224 | tf_op jit(solution)/shard_map/ppermute | solution.py:51
  40.8 4.1 %collective-permute-start.12 = (bf16[2,256,128]{2,1,0:T(8,128)(2,1)S(1)}, bf16[2,256,128]{2,1,0:T(8,128)(2,1)S(1)}, u32[]{:S(2)}, u32[]{:S(2)}) collective-permute-start(bf16[2,256,128]{2,1,0:T(8,128)(2,1)S(1)} %get-tuple-element.41), channel_id=1, source_target_pairs={{0,24},{4,28},{8,0},{12,4},{16,8},{20,12},{24,16},{28,20},{32,56},... | collective-permute-start | bytes 393224 | tf_op jit(solution)/shard_map/ppermute | solution.py:51
  44.9 7.2 %collective-permute-start.14 = (bf16[1024,256]{1,0:T(8,128)(2,1)S(1)}, bf16[1024,256]{1,0:T(8,128)(2,1)S(1)}, u32[]{:S(2)}, u32[]{:S(2)}) collective-permute-start(bf16[1024,256]{1,0:T(8,128)(2,1)S(1)} %constant_dynamic-update-slice_fusion.7.refs_4_), channel_id=1, source_target_pairs={{0,4},{4,0},{8,12},{12,8},{16,20},{20,16},{24,28},{28,24},{32,36},... | collective-permute-start | bytes 1572872 | tf_op jit(solution)/shard_map/ppermute | solution.py:37
  56.5 1.3 %collective-permute-start.15 = (f32[3,2,8,128]{3,2,1,0:T(8,128)S(1)}, f32[3,2,8,128]{3,2,1,0:T(8,128)S(1)}, u32[]{:S(2)}, u32[]{:S(2)}) collective-permute-start(f32[3,2,8,128]{3,2,1,0:T(8,128)S(1)} %get-tuple-element.47.refs_8_), channel_id=1, source_target_pairs={{0,4},{4,0},{8,12},{12,8},{16,20},{20,16},{24,28},{28,24},{32,36},... | collective-permute-start | bytes 73736 | tf_op jit(solution)/shard_map/ppermute | solution.py:37
  74.4 3.6 %collective-permute-start.16 = (bf16[1024,256]{1,0:T(8,128)(2,1)S(1)}, bf16[1024,256]{1,0:T(8,128)(2,1)S(1)}, u32[]{:S(2)}, u32[]{:S(2)}) collective-permute-start(bf16[1024,256]{1,0:T(8,128)(2,1)S(1)} %get-tuple-element.49), channel_id=1, source_target_pairs={{0,4},{4,0},{8,12},{12,8},{16,20},{20,16},{24,28},{28,24},{32,36},... | collective-permute-start | bytes 1572872 | tf_op jit(solution)/shard_map/ppermute | solution.py:37
  78.2 13.6 %collective-permute-start.17 = (bf16[512,256]{1,0:T(8,128)(2,1)S(1)}, bf16[512,256]{1,0:T(8,128)(2,1)S(1)}, u32[]{:S(2)}, u32[]{:S(2)}) collective-permute-start(bf16[512,256]{1,0:T(8,128)(2,1)S(1)} %slice.156), channel_id=1, source_target_pairs={{0,32},{4,36},{8,40},{12,44},{16,48},{20,52},{24,56},{28,60},{32,0... | collective-permute-start | bytes 786440 | tf_op jit(solution)/shard_map/ppermute | solution.py:61
  78.5 4.4 %collective-permute-start.18 = (bf16[2,256,128]{2,1,0:T(8,128)(2,1)S(1)}, bf16[2,256,128]{2,1,0:T(8,128)(2,1)S(1)}, u32[]{:S(2)}, u32[]{:S(2)}) collective-permute-start(bf16[2,256,128]{2,1,0:T(8,128)(2,1)S(1)} %get-tuple-element.51), channel_id=1, source_target_pairs={{0,24},{4,28},{8,0},{12,4},{16,8},{20,12},{24,16},{28,20},{32,56},... | collective-permute-start | bytes 393224 | tf_op jit(solution)/shard_map/ppermute | solution.py:51
  80.3 5.4 %collective-permute-start.19 = (bf16[2,256,128]{2,1,0:T(8,128)(2,1)S(1)}, bf16[2,256,128]{2,1,0:T(8,128)(2,1)S(1)}, u32[]{:S(2)}, u32[]{:S(2)}) collective-permute-start(bf16[2,256,128]{2,1,0:T(8,128)(2,1)S(1)} %get-tuple-element.52), channel_id=1, source_target_pairs={{0,16},{4,20},{8,24},{12,28},{16,0},{20,4},{24,8},{28,12},{32,48},... | collective-permute-start | bytes 393224 | tf_op jit(solution)/shard_map/ppermute | solution.py:51
  80.4 9.2 %collective-permute-start.20 = (bf16[2,256,128]{2,1,0:T(8,128)(2,1)S(1)}, bf16[2,256,128]{2,1,0:T(8,128)(2,1)S(1)}, u32[]{:S(2)}, u32[]{:S(2)}) collective-permute-start(bf16[2,256,128]{2,1,0:T(8,128)(2,1)S(1)} %get-tuple-element.53), channel_id=1, source_target_pairs={{0,8},{4,12},{8,16},{12,20},{16,24},{20,28},{24,0},{28,4},{32,40},... | collective-permute-start | bytes 393224 | tf_op jit(solution)/shard_map/ppermute | solution.py:51
  91.9 8.5 %collective-permute-start.21 = (bf16[256,256]{1,0:T(8,128)(2,1)S(1)}, bf16[256,256]{1,0:T(8,128)(2,1)S(1)}, u32[]{:S(2)}, u32[]{:S(2)}) collective-permute-start(bf16[256,256]{1,0:T(8,128)(2,1)S(1)} %slice.157), channel_id=1, source_target_pairs={{0,64},{4,68},{8,72},{12,76},{16,80},{20,84},{24,88},{28,92},{32,9... | collective-permute-start | bytes 393224 | tf_op jit(solution)/shard_map/ppermute | solution.py:61
  92.5 9.8 %collective-permute-start.23 = (bf16[128,1024]{1,0:T(8,128)(2,1)}, bf16[128,1024]{1,0:T(8,128)(2,1)S(1)}, u32[]{:S(2)}, u32[]{:S(2)}) collective-permute-start(bf16[128,1024]{1,0:T(8,128)(2,1)} %get-tuple-element.54), channel_id=1, source_target_pairs={{0,1},{1,2},{2,3},{3,0},{4,5},{5,6},{6,7},{7,4},{8,9},{9,10},{10,1... | collective-permute-start | bytes 786440 | tf_op jit(solution)/shard_map/ppermute | solution.py:41
  92.5 9.7 %collective-permute-start.24 = (bf16[128,1024]{1,0:T(8,128)(2,1)}, bf16[128,1024]{1,0:T(8,128)(2,1)}, u32[]{:S(2)}, u32[]{:S(2)}) collective-permute-start(bf16[128,1024]{1,0:T(8,128)(2,1)} %get-tuple-element.60), channel_id=1, source_target_pairs={{0,3},{1,0},{2,1},{3,2},{4,7},{5,4},{6,5},{7,6},{8,11},{9,8},{10,9... | collective-permute-start | bytes 786440 | tf_op jit(solution)/shard_map/ppermute | solution.py:41
  101.1 7.5 %collective-permute-start.22 = (bf16[128,256]{1,0:T(8,128)(2,1)S(1)}, bf16[128,256]{1,0:T(8,128)(2,1)}, u32[]{:S(2)}, u32[]{:S(2)}) collective-permute-start(bf16[128,256]{1,0:T(8,128)(2,1)S(1)} %slice.158), channel_id=1, source_target_pairs={{0,128},{4,132},{8,136},{12,140},{16,144},{20,148},{24,152},{28,15... | collective-permute-start | bytes 196616 | tf_op jit(solution)/shard_map/ppermute | solution.py:61
  103.3 13.3 %collective-permute-start.29 = (bf16[256,1024]{1,0:T(8,128)(2,1)S(1)}, bf16[256,1024]{1,0:T(8,128)(2,1)S(1)}, u32[]{:S(2)}, u32[]{:S(2)}) collective-permute-start(bf16[256,1024]{1,0:T(8,128)(2,1)S(1)} %get-tuple-element.64), channel_id=1, source_target_pairs={{0,3},{1,0},{2,1},{3,2},{4,7},{5,4},{6,5},{7,6},{8,11},{9,8},{10,9... | collective-permute-start | bytes 1572872 | tf_op jit(solution)/shard_map/ppermute | solution.py:41
  105.0 12.8 %collective-permute-start.28 = (bf16[256,1024]{1,0:T(8,128)(2,1)S(1)}, bf16[256,1024]{1,0:T(8,128)(2,1)S(1)}, u32[]{:S(2)}, u32[]{:S(2)}) collective-permute-start(bf16[256,1024]{1,0:T(8,128)(2,1)S(1)} %get-tuple-element.61), channel_id=1, source_target_pairs={{0,1},{1,2},{2,3},{3,0},{4,5},{5,6},{6,7},{7,4},{8,9},{9,10},{10,1... | collective-permute-start | bytes 1572872 | tf_op jit(solution)/shard_map/ppermute | solution.py:41
  109.6 3.0 %collective-permute-start.25 = (bf16[32,256]{1,0:T(8,128)(2,1)S(1)}, bf16[32,256]{1,0:T(8,128)(2,1)S(1)}, u32[]{:S(2)}, u32[]{:S(2)}) collective-permute-start(bf16[32,256]{1,0:T(8,128)(2,1)S(1)} %get-tuple-element.71), channel_id=1, source_target_pairs={{0,24},{4,28},{8,0},{12,4},{16,8},{20,12},{24,16},{28,20},{32,56},... | collective-permute-start | bytes 49160 | tf_op jit(solution)/shard_map/ppermute | solution.py:51
  109.7 5.5 %collective-permute-start.27 = (bf16[32,256]{1,0:T(8,128)(2,1)S(1)}, bf16[32,256]{1,0:T(8,128)(2,1)S(1)}, u32[]{:S(2)}, u32[]{:S(2)}) collective-permute-start(bf16[32,256]{1,0:T(8,128)(2,1)S(1)} %get-tuple-element.69), channel_id=1, source_target_pairs={{0,8},{4,12},{8,16},{12,20},{16,24},{20,28},{24,0},{28,4},{32,40},... | collective-permute-start | bytes 49160 | tf_op jit(solution)/shard_map/ppermute | solution.py:51
  111.1 4.1 %collective-permute-start.26 = (bf16[32,256]{1,0:T(8,128)(2,1)S(1)}, bf16[32,256]{1,0:T(8,128)(2,1)S(1)}, u32[]{:S(2)}, u32[]{:S(2)}) collective-permute-start(bf16[32,256]{1,0:T(8,128)(2,1)S(1)} %get-tuple-element.70), channel_id=1, source_target_pairs={{0,16},{4,20},{8,24},{12,28},{16,0},{20,4},{24,8},{28,12},{32,48},... | collective-permute-start | bytes 49160 | tf_op jit(solution)/shard_map/ppermute | solution.py:51
  (3 other events, 4.0 us)

commit v4 on v3

--- a/solution.py
+++ b/solution.py
@@ -13,7 +13,7 @@
 NEG_FILL = -1e30
 SCORE_SCALE = 1.0 / math.sqrt(DH)
 LOG2_SCALE = SCORE_SCALE * math.log2(math.e)
-VMEM_LIMIT = 16 * 1024 * 1024
+VMEM_LIMIT = 8 * 1024 * 1024
 F32 = jnp.float32
 BF16 = jnp.bfloat16
 NT = (((1,), (1,)), ((), ()))
@@ -365,6 +365,27 @@
     )(kept, up, down)
 
 
+def place_heads_kernel(at_ref, *refs):
+    pieces, outs = refs[:NX], refs[NX:]
+    for turn, piece in enumerate(pieces):
+        for kind, out in enumerate(outs):
+            out[:, head_columns(at_ref, turn, NX)] = piece[:, kind * DH : (kind + 1) * DH]
+
+
+def place_heads(at, pieces):
+    whole = pl.BlockSpec(memory_space=pltpu.VMEM)
+    shape = jax.ShapeDtypeStruct((pieces[0].shape[0], NX * DH), BF16)
+    return pl.pallas_call(
+        place_heads_kernel,
+        out_shape=[shape, shape],
+        in_specs=[pl.BlockSpec(memory_space=pltpu.SMEM)] + [whole] * NX,
+        out_specs=[whole] * 2,
+        compiler_params=compiler_params(),
+        cost_estimate=cost(0, 2**17, 0),
+        name="place_heads",
+    )(at, *pieces)
+
+
 def shards(context, key_weight, value_weight, queries, latent_pos, out_grad):
     lat = queries.shape[0]
     heads = key_weight.shape[1] // DH
@@ -431,12 +452,9 @@
     from_below, from_above = shift_y(up, 1), shift_y(down, -1)
     part = after(part, up)
     part = part.astype(BF16).reshape(NX, lat, 2 * DH)
-    part = jnp.stack([part[0]] + [shift_x(part[n], -n) for n in range(1, NX)])
-    part = lax.dynamic_slice_in_dim(jnp.concatenate([part, part]), (heads - x) & 3, heads, 0)
-    part = part.transpose(1, 0, 2)
-    kept = after(kept, part)
-    attended = part[:, :, :DH].reshape(lat, heads * DH)
-    query_grad = part[:, :, DH:].reshape(lat, heads * DH)
+    pieces = [part[0]] + [shift_x(part[n], -n) for n in range(1, NX)]
+    attended, query_grad = place_heads(at, pieces)
+    kept = after(kept, attended)
 
     return (attended, finish(kept, from_below, from_above), query_grad)
 

time: 119 us -> 117 us (0.983)
  local copies, waits for them, and re-layouts: 8.21 us -> 6.22 us
  waiting for transfers between devices: 32.9 us -> 34.3 us
    ppermute x12, waiting for transfers between devices: 17.5 us -> 15.6 us  [shift_x(): return lax.ppermute(array, 'ctx', pairs)]
    ppermute x7, waiting for transfers between devices: 10.2 us -> 12.1 us  [flip_z(): return lax.ppermute(array, 'ctx', pairs)]
    ppermute x8, waiting for transfers between devices: 1.27 us -> 2.64 us  [shift_y(): return lax.ppermute(array, 'tp', [(i, (i + step) % NY) for i in range(NY)])]
    ppermute x8, starting transfers between devices: 10.9 us -> 9.58 us  [shift_y(): return lax.ppermute(array, 'tp', [(i, (i + step) % NY) for i in range(NY)])]
    reshape x2 -> x0, local copies, waits for them, and re-layouts: 1.24 us -> none  [the longest x1 0.62 us: shards(): query_grad = part[:, :, DH:].reshape(lat, heads * DH)]
    ppermute x12, starting transfers between devices: 12.4 us -> 13.6 us  [shift_x(): return lax.ppermute(array, 'ctx', pairs)]
    unnamed x24 -> x14, local copies, waits for them, and re-layouts: 5.15 us -> 4.42 us
  transfers between devices with their start and end apart: 30 -> 30, of which waited for: 16 -> 18; matrix products, arithmetic and copies ran while one was open for 4% -> 2% of each run, Pallas kernels for 9% -> 9%
where the time goes in v4:
time: 117 us
  starting transfers between devices  42 us (36%)
  waiting for transfers between devices  34.3 us (29%)
  Pallas kernels  20.6 us (18%)
  blocking collectives  12.2 us (10%)
  local copies, waits for them, and re-layouts  6.22 us (5%)
    ppermute x12, waiting for transfers between devices, shift_x(): return lax.ppermute(array, 'ctx', pairs)  15.6 us
    ppermute x12, starting transfers between devices, shift_x(): return lax.ppermute(array, 'ctx', pairs)  13.6 us
    all_to_all x1, blocking collectives, exchange(): lax.all_to_all(array, 'ctx', 0, 0, tiled=True, axis_index_groups=groups)  12.2 us
    ppermute x7, waiting for transfers between devices, flip_z(): return lax.ppermute(array, 'ctx', pairs)  12.1 us
    ppermute x7, starting transfers between devices, flip_z(): return lax.ppermute(array, 'ctx', pairs)  10.6 us
    ppermute x8, starting transfers between devices, shift_y(): return lax.ppermute(array, 'tp', [(i, (i + step) % NY) for i in range(NY)])  9.58 us
    ppermute x3, starting transfers between devices, swap_cores(): return lax.ppermute(array, 'ctx', CORE_SWAP)  8.22 us
    pallas_call x1, Pallas kernels, backward(): pl.pallas_call(backward_kernel, out_shape=[jax.ShapeDtypeStruct(kv[0].sha...  4.53 us
  transfers between devices with their start and end apart: 30, of which 18 were waited for; matrix products, arithmetic and copies ran while one was open for 2% of the time, Pallas kernels for 9%

profile of v4, /device:TPU:1, one launch (start us, length us, event | category | flops | bytes accessed | tf_op | source)
XLA Modules:
  0.0 116.8 jit_solution(1542481514731988784)
XLA Ops:
  0.6 2.2 %collective-permute-start.6 = (bf16[256,1024]{1,0:T(8,128)(2,1)}, bf16[256,1024]{1,0:T(8,128)(2,1)S(1)}, u32[]{:S(2)}, u32[]{:S(2)}) collective-permute-start(bf16[256,1024]{1,0:T(8,128)(2,1)} %refs_2_.1), channel_id=1, source_target_pairs={{0,1},{1,2},{2,3},{3,0},{4,5},{5,6},{6,7},{7,4},{8,9},{9,10},{10,1... | collective-permute-start | bytes 1572872 | tf_op jit(solution)/shard_map/ppermute | solution.py:41
  2.8 1.5 %collective-permute-start.8 = (bf16[256,1024]{1,0:T(8,128)(2,1)}, bf16[256,1024]{1,0:T(8,128)(2,1)S(1)}, u32[]{:S(2)}, u32[]{:S(2)}) collective-permute-start(bf16[256,1024]{1,0:T(8,128)(2,1)} %refs_2_.1), channel_id=1, source_target_pairs={{0,3},{1,0},{2,1},{3,2},{4,7},{5,4},{6,5},{7,6},{8,11},{9,8},{10,9... | collective-permute-start | bytes 1572872 | tf_op jit(solution)/shard_map/ppermute | solution.py:41
  6.5 2.5 %collective-permute-start.1 = (bf16[32,256]{1,0:T(8,128)(2,1)S(1)}, bf16[32,256]{1,0:T(8,128)(2,1)S(1)}, u32[]{:S(2)}, u32[]{:S(2)}) collective-permute-start(bf16[32,256]{1,0:T(8,128)(2,1)S(1)} %get-tuple-element.76), channel_id=1, source_target_pairs={{0,16},{4,20},{8,24},{12,28},{16,0},{20,4},{24,8},{28,12},{32,48},... | collective-permute-start | bytes 49160 | tf_op jit(solution)/shard_map/ppermute | solution.py:51
  11.9 6.1 %collective-permute-start.5 = (bf16[128,256]{1,0:T(8,128)(2,1)S(1)}, bf16[128,256]{1,0:T(8,128)(2,1)S(1)}, u32[]{:S(2)}, u32[]{:S(2)}) collective-permute-start(bf16[128,256]{1,0:T(8,128)(2,1)S(1)} %pad_maximum_fusion), channel_id=1, source_target_pairs={{0,192},{4,196},{8,200},{12,204},{16,208},{20,212},{24,216},{28,22... | collective-permute-start | bytes 196616 | tf_op jit(solution)/shard_map/ppermute | solution.py:61
  20.4 2.7 %collective-permute-start.9 = (bf16[128,1024]{1,0:T(8,128)(2,1)S(1)}, bf16[128,1024]{1,0:T(8,128)(2,1)S(1)}, u32[]{:S(2)}, u32[]{:S(2)}) collective-permute-start(bf16[128,1024]{1,0:T(8,128)(2,1)S(1)} %slice.94), channel_id=1, source_target_pairs={{0,3},{1,0},{2,1},{3,2},{4,7},{5,4},{6,5},{7,6},{8,11},{9,8},{10,9... | collective-permute-start | bytes 786440 | tf_op jit(solution)/shard_map/ppermute | solution.py:41
  23.1 3.8 %collective-permute-done.3 = bf16[128,256]{1,0:T(8,128)(2,1)S(1)} collective-permute-done((bf16[128,256]{1,0:T(8,128)(2,1)S(1)}, bf16[128,256]{1,0:T(8,128)(2,1)S(1)}, u32[]{:S(2)}, u32[]{:S(2)}) %collective-permute-start.3) | collective-permute-done | bytes 65568 | tf_op jit(solution)/shard_map/ppermute | solution.py:61
  26.9 2.2 %copy-done.1 = bf16[4096,512]{1,0:T(8,128)(2,1)S(1)} copy-done((bf16[4096,512]{1,0:T(8,128)(2,1)S(1)}, bf16[4096,512]{1,0:T(8,128)(2,1)}, u32[]{:S(2)}) %copy-start.1) | copy-done | bytes 4194328
  29.1 2.2 %copy-done.2 = bf16[4096,512]{1,0:T(8,128)(2,1)S(1)} copy-done((bf16[4096,512]{1,0:T(8,128)(2,1)S(1)}, bf16[4096,512]{1,0:T(8,128)(2,1)}, u32[]{:S(2)}) %copy-start.2) | copy-done | bytes 4194328
  33.7 1.8 %project.4.refs_4_ = f32[2,256,512]{2,1,0:T(8,128)S(1)} custom-call(s32[4]{0:T(128)S(1)} %pad_add_fusion.at_ref, bf16[4096,512]{1,0:T(8,128)(2,1)S(1)} %get-tuple-element.38.refs_0_.wk_ref, bf16[4096,512]{1,0:T(8,128)(2,1)S(1)} %get-tuple-element.39.refs_1_.wv_ref, bf16[256,1024]{1,0:T(8,128)(2,1)S(1)} %collective-permute-done.6.refs_2_, ...), custom_call_target="tpu_custom_call" | custom-call | tf_op jit(solution)/shard_map/project/pallas_call | solution.py:150
  35.7 1.4 %project.5 = (bf16[2,256,128]{2,1,0:T(8,128)(2,1)S(1)}, bf16[2,256,128]{2,1,0:T(8,128)(2,1)S(1)}, bf16[2,256,128]{2,1,0:T(8,128)(2,1)S(1)}, bf16[2,256,128]{2,1,0:T(8,128)(2,1)S(1)}) custom-call(s32[4]{0:T(128)S(1)} %pad_add_fusion.at_ref, bf16[4096,512]{1,0:T(8,128)(2,1)S(1)} %get-tuple-element.38.refs_0_.wk_ref, ...), custom_call_target="tpu_custom_call" | custom-call | tf_op jit(solution)/shard_map/project/pallas_call | solution.py:150
  37.5 3.3 %collective-permute-start.11 = (bf16[2,256,128]{2,1,0:T(8,128)(2,1)S(1)}, bf16[2,256,128]{2,1,0:T(8,128)(2,1)S(1)}, u32[]{:S(2)}, u32[]{:S(2)}) collective-permute-start(bf16[2,256,128]{2,1,0:T(8,128)(2,1)S(1)} %get-tuple-element.42), channel_id=1, source_target_pairs={{0,16},{4,20},{8,24},{12,28},{16,0},{20,4},{24,8},{28,12},{32,48},... | collective-permute-start | bytes 393224 | tf_op jit(solution)/shard_map/ppermute | solution.py:51
  40.9 1.4 %collective-permute-done.10.refs_1_ = bf16[2,256,128]{2,1,0:T(8,128)(2,1)S(1)} collective-permute-done((bf16[2,256,128]{2,1,0:T(8,128)(2,1)S(1)}, bf16[2,256,128]{2,1,0:T(8,128)(2,1)S(1)}, u32[]{:S(2)}, u32[]{:S(2)}) %collective-permute-start.10) | collective-permute-done | bytes 131104 | tf_op jit(solution)/shard_map/ppermute | solution.py:51
  42.3 2.3 %collective-permute-done.11.refs_2_ = bf16[2,256,128]{2,1,0:T(8,128)(2,1)S(1)} collective-permute-done((bf16[2,256,128]{2,1,0:T(8,128)(2,1)S(1)}, bf16[2,256,128]{2,1,0:T(8,128)(2,1)S(1)}, u32[]{:S(2)}, u32[]{:S(2)}) %collective-permute-start.11) | collective-permute-done | bytes 131104 | tf_op jit(solution)/shard_map/ppermute | solution.py:51
  44.9 5.7 %collective-permute-start.14 = (bf16[1024,256]{1,0:T(8,128)(2,1)S(1)}, bf16[1024,256]{1,0:T(8,128)(2,1)S(1)}, u32[]{:S(2)}, u32[]{:S(2)}) collective-permute-start(bf16[1024,256]{1,0:T(8,128)(2,1)S(1)} %constant_dynamic-update-slice_fusion.7.refs_4_), channel_id=1, source_target_pairs={{0,4},{4,0},{8,12},{12,8},{16,20},{20,16},{24,28},{28,24},{32,36},... | collective-permute-start | bytes 1572872 | tf_op jit(solution)/shard_map/ppermute | solution.py:37
  50.7 1.5 %collective-permute-done.14.refs_5_ = bf16[1024,256]{1,0:T(8,128)(2,1)S(1)} collective-permute-done((bf16[1024,256]{1,0:T(8,128)(2,1)S(1)}, bf16[1024,256]{1,0:T(8,128)(2,1)S(1)}, u32[]{:S(2)}, u32[]{:S(2)}) %collective-permute-start.14) | collective-permute-done | bytes 524320 | tf_op jit(solution)/shard_map/ppermute | solution.py:37
  52.2 4.4 %latent_stats.1 = (f32[3,2,8,128]{3,2,1,0:T(8,128)S(1)}, f32[2,4,4,256,256]{4,3,2,1,0:T(8,128)S(1)}, f32[2,4,4,256,256]{4,3,2,1,0:T(8,128)S(1)}) custom-call(s32[4]{0:T(128)S(1)} %pad_add_fusion.at_ref, bf16[2,256,128]{2,1,0:T(8,128)(2,1)S(1)} %get-tuple-element.40.refs_0_, bf16[2,256,128]{2,1,0:T(8,128)(2,1)S(1)} %collective-permute-done.10.refs_1_, ...), custom_call_target="tpu_custom_call" | custom-call | tf_op jit(solution)/shard_map/latent_stats/pallas_call | solution.py:219
  57.9 12.2 %all_to_all.5.refs_9_ = f32[8,3,2,8,128]{4,3,2,1,0:T(8,128)S(1)} all-to-all(f32[8,3,2,8,128]{4,3,2,1,0:T(8,128)S(1)} %broadcast_in_dim.2), channel_id=1, replica_groups={{0,32,64,96,128,160,192,224},{4,36,68,100,132,164,196,228},{8,40,72,104..., dimensions={0} | all-to-all | bytes 393216 | tf_op jit(solution)/shard_map/all_to_all | solution.py:65
  70.1 4.5 %backward.1 = (bf16[2,256,128]{2,1,0:T(8,128)(2,1)S(1)}, bf16[2,256,128]{2,1,0:T(8,128)(2,1)S(1)}, bf16[2,256,128]{2,1,0:T(8,128)(2,1)S(1)}, bf16[2,256,128]{2,1...) custom-call(s32[4]{0:T(128)S(1)} %pad_add_fusion.at_ref, ...), custom_call_target="tpu_custom_call" | custom-call | tf_op jit(solution)/shard_map/backward/pallas_call | solution.py:279
  74.6 2.0 %collective-permute-start.16 = (bf16[1024,256]{1,0:T(8,128)(2,1)S(1)}, bf16[1024,256]{1,0:T(8,128)(2,1)S(1)}, u32[]{:S(2)}, u32[]{:S(2)}) collective-permute-start(bf16[1024,256]{1,0:T(8,128)(2,1)S(1)} %get-tuple-element.51), channel_id=1, source_target_pairs={{0,4},{4,0},{8,12},{12,8},{16,20},{20,16},{24,28},{28,24},{32,36},... | collective-permute-start | bytes 1572872 | tf_op jit(solution)/shard_map/ppermute | solution.py:37
  76.7 1.5 %collective-permute-done.16 = bf16[1024,256]{1,0:T(8,128)(2,1)S(1)} collective-permute-done((bf16[1024,256]{1,0:T(8,128)(2,1)S(1)}, bf16[1024,256]{1,0:T(8,128)(2,1)S(1)}, u32[]{:S(2)}, u32[]{:S(2)}) %collective-permute-start.16) | collective-permute-done | bytes 524320 | tf_op jit(solution)/shard_map/ppermute | solution.py:37
  78.8 1.8 %collective-permute-start.18 = (bf16[2,256,128]{2,1,0:T(8,128)(2,1)S(1)}, bf16[2,256,128]{2,1,0:T(8,128)(2,1)S(1)}, u32[]{:S(2)}, u32[]{:S(2)}) collective-permute-start(bf16[2,256,128]{2,1,0:T(8,128)(2,1)S(1)} %get-tuple-element.53), channel_id=1, source_target_pairs={{0,24},{4,28},{8,0},{12,4},{16,8},{20,12},{24,16},{28,20},{32,56},... | collective-permute-start | bytes 393224 | tf_op jit(solution)/shard_map/ppermute | solution.py:51
  81.1 2.1 %collective-permute-done.18.refs_1_ = bf16[2,256,128]{2,1,0:T(8,128)(2,1)S(1)} collective-permute-done((bf16[2,256,128]{2,1,0:T(8,128)(2,1)S(1)}, bf16[2,256,128]{2,1,0:T(8,128)(2,1)S(1)}, u32[]{:S(2)}, u32[]{:S(2)}) %collective-permute-start.18) | collective-permute-done | bytes 131104 | tf_op jit(solution)/shard_map/ppermute | solution.py:51
  83.2 2.8 %collective-permute-done.19.refs_2_ = bf16[2,256,128]{2,1,0:T(8,128)(2,1)S(1)} collective-permute-done((bf16[2,256,128]{2,1,0:T(8,128)(2,1)S(1)}, bf16[2,256,128]{2,1,0:T(8,128)(2,1)S(1)}, u32[]{:S(2)}, u32[]{:S(2)}) %collective-permute-start.19) | collective-permute-done | bytes 131104 | tf_op jit(solution)/shard_map/ppermute | solution.py:51
  86.0 3.9 %collective-permute-done.20.refs_3_ = bf16[2,256,128]{2,1,0:T(8,128)(2,1)S(1)} collective-permute-done((bf16[2,256,128]{2,1,0:T(8,128)(2,1)S(1)}, bf16[2,256,128]{2,1,0:T(8,128)(2,1)S(1)}, u32[]{:S(2)}, u32[]{:S(2)}) %collective-permute-start.20) | collective-permute-done | bytes 131104 | tf_op jit(solution)/shard_map/ppermute | solution.py:51
  91.9 1.5 %collective-permute-start.24 = (bf16[128,1024]{1,0:T(8,128)(2,1)S(1)}, bf16[128,1024]{1,0:T(8,128)(2,1)S(1)}, u32[]{:S(2)}, u32[]{:S(2)}) collective-permute-start(bf16[128,1024]{1,0:T(8,128)(2,1)S(1)} %get-tuple-element.62), channel_id=1, source_target_pairs={{0,3},{1,0},{2,1},{3,2},{4,7},{5,4},{6,5},{7,6},{8,11},{9,8},{10,9... | collective-permute-start | bytes 786440 | tf_op jit(solution)/shard_map/ppermute | solution.py:41
  93.4 2.5 %context_terms.3 = (f32[256,1024]{1,0:T(8,128)S(1)}, f32[256,1024]{1,0:T(8,128)S(1)}, f32[256,1024]{1,0:T(8,128)S(1)}) custom-call(s32[4]{0:T(128)S(1)} %pad_add_fusion.at_ref, bf16[4096,512]{1,0:T(8,128)(2,1)S(1)} %get-tuple-element.38.refs_0_.wk_ref, bf16[4096,512]{1,0:T(8,128)(2,1)S(1)} %get-tuple-element.39.refs_1_.wv_ref, ...), custom_call_target="tpu_custom_call" | custom-call | tf_op jit(solution)/shard_map/context_terms/pallas_call | solution.py:317
  95.9 4.0 %collective-permute-done.21 = bf16[256,256]{1,0:T(8,128)(2,1)S(1)} collective-permute-done((bf16[256,256]{1,0:T(8,128)(2,1)S(1)}, bf16[256,256]{1,0:T(8,128)(2,1)S(1)}, u32[]{:S(2)}, u32[]{:S(2)}) %collective-permute-start.21) | collective-permute-done | bytes 131104 | tf_op jit(solution)/shard_map/ppermute | solution.py:61
  101.4 1.4 %collective-permute-start.29 = (bf16[256,1024]{1,0:T(8,128)(2,1)S(1)}, bf16[256,1024]{1,0:T(8,128)(2,1)S(1)}, u32[]{:S(2)}, u32[]{:S(2)}) collective-permute-start(bf16[256,1024]{1,0:T(8,128)(2,1)S(1)} %get-tuple-element.67), channel_id=1, source_target_pairs={{0,3},{1,0},{2,1},{3,2},{4,7},{5,4},{6,5},{7,6},{8,11},{9,8},{10,9... | collective-permute-start | bytes 1572872 | tf_op jit(solution)/shard_map/ppermute | solution.py:41
  102.9 4.3 %collective-permute-done.22 = bf16[128,256]{1,0:T(8,128)(2,1)S(1)} collective-permute-done((bf16[128,256]{1,0:T(8,128)(2,1)S(1)}, bf16[128,256]{1,0:T(8,128)(2,1)S(1)}, u32[]{:S(2)}, u32[]{:S(2)}) %collective-permute-start.22) | collective-permute-done | bytes 65568 | tf_op jit(solution)/shard_map/ppermute | solution.py:61
  107.4 2.6 %collective-permute-start.25 = (bf16[32,256]{1,0:T(8,128)(2,1)S(1)}, bf16[32,256]{1,0:T(8,128)(2,1)S(1)}, u32[]{:S(2)}, u32[]{:S(2)}) collective-permute-start(bf16[32,256]{1,0:T(8,128)(2,1)S(1)} %get-tuple-element.73), channel_id=1, source_target_pairs={{0,24},{4,28},{8,0},{12,4},{16,8},{20,12},{24,16},{28,20},{32,56},... | collective-permute-start | bytes 49160 | tf_op jit(solution)/shard_map/ppermute | solution.py:51
  110.0 1.4 %collective-permute-done.27.refs_3_ = bf16[32,256]{1,0:T(8,128)(2,1)S(1)} collective-permute-done((bf16[32,256]{1,0:T(8,128)(2,1)S(1)}, bf16[32,256]{1,0:T(8,128)(2,1)S(1)}, u32[]{:S(2)}, u32[]{:S(2)}) %collective-permute-start.27) | collective-permute-done | bytes 16416 | tf_op jit(solution)/shard_map/ppermute | solution.py:51
  113.3 2.5 %collective-permute-done.28.up_ref = bf16[256,1024]{1,0:T(8,128)(2,1)S(1)} collective-permute-done((bf16[256,1024]{1,0:T(8,128)(2,1)S(1)}, bf16[256,1024]{1,0:T(8,128)(2,1)S(1)}, u32[]{:S(2)}, u32[]{:S(2)}) %collective-permute-start.28) | collective-permute-done | bytes 524320 | tf_op jit(solution)/shard_map/ppermute | solution.py:41
  (82 shorter events, 19.8 us)
Async XLA Ops:
  0.6 3.8 %copy-start = (bf16[32,512]{1,0:T(8,128)(2,1)S(1)}, bf16[32,512]{1,0:T(8,128)(2,1)}, u32[]{:S(2)}) copy-start(bf16[32,512]{1,0:T(8,128)(2,1)} %param.9) | copy-start | bytes 98308
  0.6 19.6 %collective-permute-start.6 = (bf16[256,1024]{1,0:T(8,128)(2,1)}, bf16[256,1024]{1,0:T(8,128)(2,1)S(1)}, u32[]{:S(2)}, u32[]{:S(2)}) collective-permute-start(bf16[256,1024]{1,0:T(8,128)(2,1)} %refs_2_.1), channel_id=1, source_target_pairs={{0,1},{1,2},{2,3},{3,0},{4,5},{5,6},{6,7},{7,4},{8,9},{9,10},{10,1... | collective-permute-start | bytes 1572872 | tf_op jit(solution)/shard_map/ppermute | solution.py:41
  2.8 17.5 %collective-permute-start.8 = (bf16[256,1024]{1,0:T(8,128)(2,1)}, bf16[256,1024]{1,0:T(8,128)(2,1)S(1)}, u32[]{:S(2)}, u32[]{:S(2)}) collective-permute-start(bf16[256,1024]{1,0:T(8,128)(2,1)} %refs_2_.1), channel_id=1, source_target_pairs={{0,3},{1,0},{2,1},{3,2},{4,7},{5,4},{6,5},{7,6},{8,11},{9,8},{10,9... | collective-permute-start | bytes 1572872 | tf_op jit(solution)/shard_map/ppermute | solution.py:41
  5.2 6.0 %collective-permute-start = (bf16[32,256]{1,0:T(8,128)(2,1)S(1)}, bf16[32,256]{1,0:T(8,128)(2,1)S(1)}, u32[]{:S(2)}, u32[]{:S(2)}) collective-permute-start(bf16[32,256]{1,0:T(8,128)(2,1)S(1)} %get-tuple-element.75), channel_id=1, source_target_pairs={{0,8},{4,12},{8,16},{12,20},{16,24},{20,28},{24,0},{28,4},{32,40},... | collective-permute-start | bytes 49160 | tf_op jit(solution)/shard_map/ppermute | solution.py:51
  6.5 4.7 %collective-permute-start.1 = (bf16[32,256]{1,0:T(8,128)(2,1)S(1)}, bf16[32,256]{1,0:T(8,128)(2,1)S(1)}, u32[]{:S(2)}, u32[]{:S(2)}) collective-permute-start(bf16[32,256]{1,0:T(8,128)(2,1)S(1)} %get-tuple-element.76), channel_id=1, source_target_pairs={{0,16},{4,20},{8,24},{12,28},{16,0},{20,4},{24,8},{28,12},{32,48},... | collective-permute-start | bytes 49160 | tf_op jit(solution)/shard_map/ppermute | solution.py:51
  9.0 2.9 %collective-permute-start.2 = (bf16[32,256]{1,0:T(8,128)(2,1)S(1)}, bf16[32,256]{1,0:T(8,128)(2,1)S(1)}, u32[]{:S(2)}, u32[]{:S(2)}) collective-permute-start(bf16[32,256]{1,0:T(8,128)(2,1)S(1)} %get-tuple-element.77), channel_id=1, source_target_pairs={{0,24},{4,28},{8,0},{12,4},{16,8},{20,12},{24,16},{28,20},{32,56},... | collective-permute-start | bytes 49160 | tf_op jit(solution)/shard_map/ppermute | solution.py:51
  11.9 15.0 %collective-permute-start.5 = (bf16[128,256]{1,0:T(8,128)(2,1)S(1)}, bf16[128,256]{1,0:T(8,128)(2,1)S(1)}, u32[]{:S(2)}, u32[]{:S(2)}) collective-permute-start(bf16[128,256]{1,0:T(8,128)(2,1)S(1)} %pad_maximum_fusion), channel_id=1, source_target_pairs={{0,192},{4,196},{8,200},{12,204},{16,208},{20,212},{24,216},{28,22... | collective-permute-start | bytes 196616 | tf_op jit(solution)/shard_map/ppermute | solution.py:61
  18.0 8.9 %collective-permute-start.4 = (bf16[128,256]{1,0:T(8,128)(2,1)S(1)}, bf16[128,256]{1,0:T(8,128)(2,1)S(1)}, u32[]{:S(2)}, u32[]{:S(2)}) collective-permute-start(bf16[128,256]{1,0:T(8,128)(2,1)S(1)} %pad_maximum_fusion), channel_id=1, source_target_pairs={{0,64},{4,68},{8,72},{12,76},{16,80},{20,84},{24,88},{28,92},{32,9... | collective-permute-start | bytes 196616 | tf_op jit(solution)/shard_map/ppermute | solution.py:61
  19.2 7.7 %collective-permute-start.3 = (bf16[128,256]{1,0:T(8,128)(2,1)S(1)}, bf16[128,256]{1,0:T(8,128)(2,1)S(1)}, u32[]{:S(2)}, u32[]{:S(2)}) collective-permute-start(bf16[128,256]{1,0:T(8,128)(2,1)S(1)} %pad_maximum_fusion), channel_id=1, source_target_pairs={{0,128},{4,132},{8,136},{12,140},{16,144},{20,148},{24,152},{28,15... | collective-permute-start | bytes 196616 | tf_op jit(solution)/shard_map/ppermute | solution.py:61
  20.2 15.3 %collective-permute-start.7 = (bf16[128,1024]{1,0:T(8,128)(2,1)S(1)}, bf16[128,1024]{1,0:T(8,128)(2,1)S(1)}, u32[]{:S(2)}, u32[]{:S(2)}) collective-permute-start(bf16[128,1024]{1,0:T(8,128)(2,1)S(1)} %slice.93), channel_id=1, source_target_pairs={{0,1},{1,2},{2,3},{3,0},{4,5},{5,6},{6,7},{7,4},{8,9},{9,10},{10,1... | collective-permute-start | bytes 786440 | tf_op jit(solution)/shard_map/ppermute | solution.py:41
  20.4 15.2 %collective-permute-start.9 = (bf16[128,1024]{1,0:T(8,128)(2,1)S(1)}, bf16[128,1024]{1,0:T(8,128)(2,1)S(1)}, u32[]{:S(2)}, u32[]{:S(2)}) collective-permute-start(bf16[128,1024]{1,0:T(8,128)(2,1)S(1)} %slice.94), channel_id=1, source_target_pairs={{0,3},{1,0},{2,1},{3,2},{4,7},{5,4},{6,5},{7,6},{8,11},{9,8},{10,9... | collective-permute-start | bytes 786440 | tf_op jit(solution)/shard_map/ppermute | solution.py:41
  26.9 2.2 %copy-start.1 = (bf16[4096,512]{1,0:T(8,128)(2,1)S(1)}, bf16[4096,512]{1,0:T(8,128)(2,1)}, u32[]{:S(2)}) copy-start(bf16[4096,512]{1,0:T(8,128)(2,1)} %refs_0_.1) | copy-start | bytes 12582916
  35.6 5.3 %collective-permute-start.13 = (bf16[512,256]{1,0:T(8,128)(2,1)S(1)}, bf16[512,256]{1,0:T(8,128)(2,1)S(1)}, u32[]{:S(2)}, u32[]{:S(2)}) collective-permute-start(bf16[512,256]{1,0:T(8,128)(2,1)S(1)} %constant_dynamic-update-slice_fusion), channel_id=1, source_target_pairs={{0,32},{4,36},{8,40},{12,44},{16,48},{20,52},{24,56},{28,60},{32,0... | collective-permute-start | bytes 786440 | tf_op jit(solution)/shard_map/ppermute | solution.py:61
  37.2 5.1 %collective-permute-start.10 = (bf16[2,256,128]{2,1,0:T(8,128)(2,1)S(1)}, bf16[2,256,128]{2,1,0:T(8,128)(2,1)S(1)}, u32[]{:S(2)}, u32[]{:S(2)}) collective-permute-start(bf16[2,256,128]{2,1,0:T(8,128)(2,1)S(1)} %get-tuple-element.41), channel_id=1, source_target_pairs={{0,8},{4,12},{8,16},{12,20},{16,24},{20,28},{24,0},{28,4},{32,40},... | collective-permute-start | bytes 393224 | tf_op jit(solution)/shard_map/ppermute | solution.py:51
  37.5 7.1 %collective-permute-start.11 = (bf16[2,256,128]{2,1,0:T(8,128)(2,1)S(1)}, bf16[2,256,128]{2,1,0:T(8,128)(2,1)S(1)}, u32[]{:S(2)}, u32[]{:S(2)}) collective-permute-start(bf16[2,256,128]{2,1,0:T(8,128)(2,1)S(1)} %get-tuple-element.42), channel_id=1, source_target_pairs={{0,16},{4,20},{8,24},{12,28},{16,0},{20,4},{24,8},{28,12},{32,48},... | collective-permute-start | bytes 393224 | tf_op jit(solution)/shard_map/ppermute | solution.py:51
  40.8 4.1 %collective-permute-start.12 = (bf16[2,256,128]{2,1,0:T(8,128)(2,1)S(1)}, bf16[2,256,128]{2,1,0:T(8,128)(2,1)S(1)}, u32[]{:S(2)}, u32[]{:S(2)}) collective-permute-start(bf16[2,256,128]{2,1,0:T(8,128)(2,1)S(1)} %get-tuple-element.43), channel_id=1, source_target_pairs={{0,24},{4,28},{8,0},{12,4},{16,8},{20,12},{24,16},{28,20},{32,56},... | collective-permute-start | bytes 393224 | tf_op jit(solution)/shard_map/ppermute | solution.py:51
  44.9 7.2 %collective-permute-start.14 = (bf16[1024,256]{1,0:T(8,128)(2,1)S(1)}, bf16[1024,256]{1,0:T(8,128)(2,1)S(1)}, u32[]{:S(2)}, u32[]{:S(2)}) collective-permute-start(bf16[1024,256]{1,0:T(8,128)(2,1)S(1)} %constant_dynamic-update-slice_fusion.7.refs_4_), channel_id=1, source_target_pairs={{0,4},{4,0},{8,12},{12,8},{16,20},{20,16},{24,28},{28,24},{32,36},... | collective-permute-start | bytes 1572872 | tf_op jit(solution)/shard_map/ppermute | solution.py:37
  56.6 1.3 %collective-permute-start.15 = (f32[3,2,8,128]{3,2,1,0:T(8,128)S(1)}, f32[3,2,8,128]{3,2,1,0:T(8,128)S(1)}, u32[]{:S(2)}, u32[]{:S(2)}) collective-permute-start(f32[3,2,8,128]{3,2,1,0:T(8,128)S(1)} %get-tuple-element.49.refs_8_), channel_id=1, source_target_pairs={{0,4},{4,0},{8,12},{12,8},{16,20},{20,16},{24,28},{28,24},{32,36},... | collective-permute-start | bytes 73736 | tf_op jit(solution)/shard_map/ppermute | solution.py:37
  74.6 3.6 %collective-permute-start.16 = (bf16[1024,256]{1,0:T(8,128)(2,1)S(1)}, bf16[1024,256]{1,0:T(8,128)(2,1)S(1)}, u32[]{:S(2)}, u32[]{:S(2)}) collective-permute-start(bf16[1024,256]{1,0:T(8,128)(2,1)S(1)} %get-tuple-element.51), channel_id=1, source_target_pairs={{0,4},{4,0},{8,12},{12,8},{16,20},{20,16},{24,28},{28,24},{32,36},... | collective-permute-start | bytes 1572872 | tf_op jit(solution)/shard_map/ppermute | solution.py:37
  78.4 12.8 %collective-permute-start.17 = (bf16[512,256]{1,0:T(8,128)(2,1)S(1)}, bf16[512,256]{1,0:T(8,128)(2,1)S(1)}, u32[]{:S(2)}, u32[]{:S(2)}) collective-permute-start(bf16[512,256]{1,0:T(8,128)(2,1)S(1)} %slice.136), channel_id=1, source_target_pairs={{0,32},{4,36},{8,40},{12,44},{16,48},{20,52},{24,56},{28,60},{32,0... | collective-permute-start | bytes 786440 | tf_op jit(solution)/shard_map/ppermute | solution.py:61
  78.8 4.4 %collective-permute-start.18 = (bf16[2,256,128]{2,1,0:T(8,128)(2,1)S(1)}, bf16[2,256,128]{2,1,0:T(8,128)(2,1)S(1)}, u32[]{:S(2)}, u32[]{:S(2)}) collective-permute-start(bf16[2,256,128]{2,1,0:T(8,128)(2,1)S(1)} %get-tuple-element.53), channel_id=1, source_target_pairs={{0,24},{4,28},{8,0},{12,4},{16,8},{20,12},{24,16},{28,20},{32,56},... | collective-permute-start | bytes 393224 | tf_op jit(solution)/shard_map/ppermute | solution.py:51
  80.5 5.4 %collective-permute-start.19 = (bf16[2,256,128]{2,1,0:T(8,128)(2,1)S(1)}, bf16[2,256,128]{2,1,0:T(8,128)(2,1)S(1)}, u32[]{:S(2)}, u32[]{:S(2)}) collective-permute-start(bf16[2,256,128]{2,1,0:T(8,128)(2,1)S(1)} %get-tuple-element.54), channel_id=1, source_target_pairs={{0,16},{4,20},{8,24},{12,28},{16,0},{20,4},{24,8},{28,12},{32,48},... | collective-permute-start | bytes 393224 | tf_op jit(solution)/shard_map/ppermute | solution.py:51
  80.7 9.3 %collective-permute-start.20 = (bf16[2,256,128]{2,1,0:T(8,128)(2,1)S(1)}, bf16[2,256,128]{2,1,0:T(8,128)(2,1)S(1)}, u32[]{:S(2)}, u32[]{:S(2)}) collective-permute-start(bf16[2,256,128]{2,1,0:T(8,128)(2,1)S(1)} %get-tuple-element.55), channel_id=1, source_target_pairs={{0,8},{4,12},{8,16},{12,20},{16,24},{20,28},{24,0},{28,4},{32,40},... | collective-permute-start | bytes 393224 | tf_op jit(solution)/shard_map/ppermute | solution.py:51
  91.4 8.5 %collective-permute-start.21 = (bf16[256,256]{1,0:T(8,128)(2,1)S(1)}, bf16[256,256]{1,0:T(8,128)(2,1)S(1)}, u32[]{:S(2)}, u32[]{:S(2)}) collective-permute-start(bf16[256,256]{1,0:T(8,128)(2,1)S(1)} %slice.137), channel_id=1, source_target_pairs={{0,64},{4,68},{8,72},{12,76},{16,80},{20,84},{24,88},{28,92},{32,9... | collective-permute-start | bytes 393224 | tf_op jit(solution)/shard_map/ppermute | solution.py:61
  91.9 9.1 %collective-permute-start.24 = (bf16[128,1024]{1,0:T(8,128)(2,1)S(1)}, bf16[128,1024]{1,0:T(8,128)(2,1)S(1)}, u32[]{:S(2)}, u32[]{:S(2)}) collective-permute-start(bf16[128,1024]{1,0:T(8,128)(2,1)S(1)} %get-tuple-element.62), channel_id=1, source_target_pairs={{0,3},{1,0},{2,1},{3,2},{4,7},{5,4},{6,5},{7,6},{8,11},{9,8},{10,9... | collective-permute-start | bytes 786440 | tf_op jit(solution)/shard_map/ppermute | solution.py:41
  93.4 7.7 %collective-permute-start.23 = (bf16[128,1024]{1,0:T(8,128)(2,1)S(1)}, bf16[128,1024]{1,0:T(8,128)(2,1)S(1)}, u32[]{:S(2)}, u32[]{:S(2)}) collective-permute-start(bf16[128,1024]{1,0:T(8,128)(2,1)S(1)} %get-tuple-element.56), channel_id=1, source_target_pairs={{0,1},{1,2},{2,3},{3,0},{4,5},{5,6},{6,7},{7,4},{8,9},{9,10},{10,1... | collective-permute-start | bytes 786440 | tf_op jit(solution)/shard_map/ppermute | solution.py:41
  99.9 7.3 %collective-permute-start.22 = (bf16[128,256]{1,0:T(8,128)(2,1)S(1)}, bf16[128,256]{1,0:T(8,128)(2,1)S(1)}, u32[]{:S(2)}, u32[]{:S(2)}) collective-permute-start(bf16[128,256]{1,0:T(8,128)(2,1)S(1)} %slice.138), channel_id=1, source_target_pairs={{0,128},{4,132},{8,136},{12,140},{16,144},{20,148},{24,152},{28,15... | collective-permute-start | bytes 196616 | tf_op jit(solution)/shard_map/ppermute | solution.py:61
  101.4 12.0 %collective-permute-start.29 = (bf16[256,1024]{1,0:T(8,128)(2,1)S(1)}, bf16[256,1024]{1,0:T(8,128)(2,1)S(1)}, u32[]{:S(2)}, u32[]{:S(2)}) collective-permute-start(bf16[256,1024]{1,0:T(8,128)(2,1)S(1)} %get-tuple-element.67), channel_id=1, source_target_pairs={{0,3},{1,0},{2,1},{3,2},{4,7},{5,4},{6,5},{7,6},{8,11},{9,8},{10,9... | collective-permute-start | bytes 1572872 | tf_op jit(solution)/shard_map/ppermute | solution.py:41
  102.8 13.0 %collective-permute-start.28 = (bf16[256,1024]{1,0:T(8,128)(2,1)S(1)}, bf16[256,1024]{1,0:T(8,128)(2,1)S(1)}, u32[]{:S(2)}, u32[]{:S(2)}) collective-permute-start(bf16[256,1024]{1,0:T(8,128)(2,1)S(1)} %get-tuple-element.63), channel_id=1, source_target_pairs={{0,1},{1,2},{2,3},{3,0},{4,5},{5,6},{6,7},{7,4},{8,9},{9,10},{10,1... | collective-permute-start | bytes 1572872 | tf_op jit(solution)/shard_map/ppermute | solution.py:41
  107.2 4.2 %collective-permute-start.27 = (bf16[32,256]{1,0:T(8,128)(2,1)S(1)}, bf16[32,256]{1,0:T(8,128)(2,1)S(1)}, u32[]{:S(2)}, u32[]{:S(2)}) collective-permute-start(bf16[32,256]{1,0:T(8,128)(2,1)S(1)} %get-tuple-element.71), channel_id=1, source_target_pairs={{0,8},{4,12},{8,16},{12,20},{16,24},{20,28},{24,0},{28,4},{32,40},... | collective-permute-start | bytes 49160 | tf_op jit(solution)/shard_map/ppermute | solution.py:51
  107.3 4.2 %collective-permute-start.26 = (bf16[32,256]{1,0:T(8,128)(2,1)S(1)}, bf16[32,256]{1,0:T(8,128)(2,1)S(1)}, u32[]{:S(2)}, u32[]{:S(2)}) collective-permute-start(bf16[32,256]{1,0:T(8,128)(2,1)S(1)} %get-tuple-element.72), channel_id=1, source_target_pairs={{0,16},{4,20},{8,24},{12,28},{16,0},{20,4},{24,8},{28,12},{32,48},... | collective-permute-start | bytes 49160 | tf_op jit(solution)/shard_map/ppermute | solution.py:51
  107.4 4.7 %collective-permute-start.25 = (bf16[32,256]{1,0:T(8,128)(2,1)S(1)}, bf16[32,256]{1,0:T(8,128)(2,1)S(1)}, u32[]{:S(2)}, u32[]{:S(2)}) collective-permute-start(bf16[32,256]{1,0:T(8,128)(2,1)S(1)} %get-tuple-element.73), channel_id=1, source_target_pairs={{0,24},{4,28},{8,0},{12,4},{16,8},{20,12},{24,16},{28,20},{32,56},... | collective-permute-start | bytes 49160 | tf_op jit(solution)/shard_map/ppermute | solution.py:51
  (2 other events, 3.3 us)

commit v5 on v4

--- a/solution.py
+++ b/solution.py
@@ -412,9 +412,9 @@
     got = [flip_z(own, bit) for bit in (4, 2, 6)]
     own = jnp.concatenate([own, *got])
     weights = load_weights(after(at, *got), key_weight, value_weight)
-    (total,) = project(at, *weights, {0: [context]}, None, False)
     far_upper, far_lower = shift_y(ahead[: rows // 2], 1), shift_y(behind[rows // 2 :], -1)
-    (total,) = project(at, *weights, {3: [ahead], 1: [behind]}, total, False)
+    pieces = {0: [context], 3: [ahead], 1: [behind]}
+    (total,) = project(at, *weights, pieces, None, False)
     own = after(own, far_upper, far_lower, total)
     own = jnp.concatenate([own, flip_z(own, 1)])
     kv = project(at, *weights, {2: [far_upper, far_lower]}, total, True)

time: 117 us -> 116 us (level)
    pallas_call x3 -> x2, Pallas kernels: 4.5 us -> 3.78 us  [project(): pl.pallas_call(functools.partial(project_kernel, steps, first, last), out...]
where the time goes in v5:
time: 116 us
  starting transfers between devices  42.1 us (36%)
  waiting for transfers between devices  34.2 us (29%)
  Pallas kernels  19.9 us (17%)
  blocking collectives  12.2 us (11%)
  local copies, waits for them, and re-layouts  6.22 us (5%)
    ppermute x12, waiting for transfers between devices, shift_x(): return lax.ppermute(array, 'ctx', pairs)  15.6 us
    ppermute x12, starting transfers between devices, shift_x(): return lax.ppermute(array, 'ctx', pairs)  13.6 us
    all_to_all x1, blocking collectives, exchange(): lax.all_to_all(array, 'ctx', 0, 0, tiled=True, axis_index_groups=groups)  12.2 us
    ppermute x7, waiting for transfers between devices, flip_z(): return lax.ppermute(array, 'ctx', pairs)  12 us
    ppermute x7, starting transfers between devices, flip_z(): return lax.ppermute(array, 'ctx', pairs)  10.6 us
    ppermute x8, starting transfers between devices, shift_y(): return lax.ppermute(array, 'tp', [(i, (i + step) % NY) for i in range(NY)])  9.6 us
    ppermute x3, starting transfers between devices, swap_cores(): return lax.ppermute(array, 'ctx', CORE_SWAP)  8.23 us
    pallas_call x1, Pallas kernels, backward(): pl.pallas_call(backward_kernel, out_shape=[jax.ShapeDtypeStruct(kv[0].sha...  4.53 us
  transfers between devices with their start and end apart: 30, of which 18 were waited for; matrix products, arithmetic and copies ran while one was open for 2% of the time, Pallas kernels for 9%

profile of v5, /device:TPU:1, one launch (start us, length us, event | category | flops | bytes accessed | tf_op | source)
XLA Modules:
  0.0 116.1 jit_solution(10293469985589189754)
XLA Ops:
  0.6 2.2 %collective-permute-start.6 = (bf16[256,1024]{1,0:T(8,128)(2,1)}, bf16[256,1024]{1,0:T(8,128)(2,1)S(1)}, u32[]{:S(2)}, u32[]{:S(2)}) collective-permute-start(bf16[256,1024]{1,0:T(8,128)(2,1)} %refs_2_.1), channel_id=1, source_target_pairs={{0,1},{1,2},{2,3},{3,0},{4,5},{5,6},{6,7},{7,4},{8,9},{9,10},{10,1... | collective-permute-start | bytes 1572872 | tf_op jit(solution)/shard_map/ppermute | solution.py:41
  2.8 1.5 %collective-permute-start.8 = (bf16[256,1024]{1,0:T(8,128)(2,1)}, bf16[256,1024]{1,0:T(8,128)(2,1)S(1)}, u32[]{:S(2)}, u32[]{:S(2)}) collective-permute-start(bf16[256,1024]{1,0:T(8,128)(2,1)} %refs_2_.1), channel_id=1, source_target_pairs={{0,3},{1,0},{2,1},{3,2},{4,7},{5,4},{6,5},{7,6},{8,11},{9,8},{10,9... | collective-permute-start | bytes 1572872 | tf_op jit(solution)/shard_map/ppermute | solution.py:41
  6.5 2.5 %collective-permute-start.1 = (bf16[32,256]{1,0:T(8,128)(2,1)S(1)}, bf16[32,256]{1,0:T(8,128)(2,1)S(1)}, u32[]{:S(2)}, u32[]{:S(2)}) collective-permute-start(bf16[32,256]{1,0:T(8,128)(2,1)S(1)} %get-tuple-element.76), channel_id=1, source_target_pairs={{0,16},{4,20},{8,24},{12,28},{16,0},{20,4},{24,8},{28,12},{32,48},... | collective-permute-start | bytes 49160 | tf_op jit(solution)/shard_map/ppermute | solution.py:51
  11.9 6.1 %collective-permute-start.5 = (bf16[128,256]{1,0:T(8,128)(2,1)S(1)}, bf16[128,256]{1,0:T(8,128)(2,1)S(1)}, u32[]{:S(2)}, u32[]{:S(2)}) collective-permute-start(bf16[128,256]{1,0:T(8,128)(2,1)S(1)} %pad_maximum_fusion), channel_id=1, source_target_pairs={{0,192},{4,196},{8,200},{12,204},{16,208},{20,212},{24,216},{28,22... | collective-permute-start | bytes 196616 | tf_op jit(solution)/shard_map/ppermute | solution.py:61
  20.4 2.7 %collective-permute-start.9 = (bf16[128,1024]{1,0:T(8,128)(2,1)S(1)}, bf16[128,1024]{1,0:T(8,128)(2,1)S(1)}, u32[]{:S(2)}, u32[]{:S(2)}) collective-permute-start(bf16[128,1024]{1,0:T(8,128)(2,1)S(1)} %slice.94), channel_id=1, source_target_pairs={{0,3},{1,0},{2,1},{3,2},{4,7},{5,4},{6,5},{7,6},{8,11},{9,8},{10,9... | collective-permute-start | bytes 786440 | tf_op jit(solution)/shard_map/ppermute | solution.py:41
  23.1 3.8 %collective-permute-done.3 = bf16[128,256]{1,0:T(8,128)(2,1)S(1)} collective-permute-done((bf16[128,256]{1,0:T(8,128)(2,1)S(1)}, bf16[128,256]{1,0:T(8,128)(2,1)S(1)}, u32[]{:S(2)}, u32[]{:S(2)}) %collective-permute-start.3) | collective-permute-done | bytes 65568 | tf_op jit(solution)/shard_map/ppermute | solution.py:61
  26.9 2.2 %copy-done.1 = bf16[4096,512]{1,0:T(8,128)(2,1)S(1)} copy-done((bf16[4096,512]{1,0:T(8,128)(2,1)S(1)}, bf16[4096,512]{1,0:T(8,128)(2,1)}, u32[]{:S(2)}) %copy-start.1) | copy-done | bytes 4194328
  29.1 2.2 %copy-done.2 = bf16[4096,512]{1,0:T(8,128)(2,1)S(1)} copy-done((bf16[4096,512]{1,0:T(8,128)(2,1)S(1)}, bf16[4096,512]{1,0:T(8,128)(2,1)}, u32[]{:S(2)}) %copy-start.2) | copy-done | bytes 4194328
  32.5 2.4 %project.2.refs_4_ = f32[2,256,512]{2,1,0:T(8,128)S(1)} custom-call(s32[4]{0:T(128)S(1)} %pad_add_fusion.at_ref, bf16[4096,512]{1,0:T(8,128)(2,1)S(1)} %get-tuple-element.38.refs_0_.wk_ref, bf16[4096,512]{1,0:T(8,128)(2,1)S(1)} %get-tuple-element.39.refs_1_.wv_ref, bf16[256,1024]{1,0:T(8,128)(2,1)S(1)} %copy-done.3, ...), custom_call_target="tpu_custom_call" | custom-call | tf_op jit(solution)/shard_map/project/pallas_call | solution.py:150
  35.0 1.4 %project.3 = (bf16[2,256,128]{2,1,0:T(8,128)(2,1)S(1)}, bf16[2,256,128]{2,1,0:T(8,128)(2,1)S(1)}, bf16[2,256,128]{2,1,0:T(8,128)(2,1)S(1)}, bf16[2,256,128]{2,1,0:T(8,128)(2,1)S(1)}) custom-call(s32[4]{0:T(128)S(1)} %pad_add_fusion.at_ref, bf16[4096,512]{1,0:T(8,128)(2,1)S(1)} %get-tuple-element.38.refs_0_.wk_ref, ...), custom_call_target="tpu_custom_call" | custom-call | tf_op jit(solution)/shard_map/project/pallas_call | solution.py:150
  36.8 3.3 %collective-permute-start.11 = (bf16[2,256,128]{2,1,0:T(8,128)(2,1)S(1)}, bf16[2,256,128]{2,1,0:T(8,128)(2,1)S(1)}, u32[]{:S(2)}, u32[]{:S(2)}) collective-permute-start(bf16[2,256,128]{2,1,0:T(8,128)(2,1)S(1)} %get-tuple-element.42), channel_id=1, source_target_pairs={{0,16},{4,20},{8,24},{12,28},{16,0},{20,4},{24,8},{28,12},{32,48},... | collective-permute-start | bytes 393224 | tf_op jit(solution)/shard_map/ppermute | solution.py:51
  40.2 1.4 %collective-permute-done.10.refs_1_ = bf16[2,256,128]{2,1,0:T(8,128)(2,1)S(1)} collective-permute-done((bf16[2,256,128]{2,1,0:T(8,128)(2,1)S(1)}, bf16[2,256,128]{2,1,0:T(8,128)(2,1)S(1)}, u32[]{:S(2)}, u32[]{:S(2)}) %collective-permute-start.10) | collective-permute-done | bytes 131104 | tf_op jit(solution)/shard_map/ppermute | solution.py:51
  41.6 2.3 %collective-permute-done.11.refs_2_ = bf16[2,256,128]{2,1,0:T(8,128)(2,1)S(1)} collective-permute-done((bf16[2,256,128]{2,1,0:T(8,128)(2,1)S(1)}, bf16[2,256,128]{2,1,0:T(8,128)(2,1)S(1)}, u32[]{:S(2)}, u32[]{:S(2)}) %collective-permute-start.11) | collective-permute-done | bytes 131104 | tf_op jit(solution)/shard_map/ppermute | solution.py:51
  44.2 5.7 %collective-permute-start.14 = (bf16[1024,256]{1,0:T(8,128)(2,1)S(1)}, bf16[1024,256]{1,0:T(8,128)(2,1)S(1)}, u32[]{:S(2)}, u32[]{:S(2)}) collective-permute-start(bf16[1024,256]{1,0:T(8,128)(2,1)S(1)} %constant_dynamic-update-slice_fusion.7.refs_4_), channel_id=1, source_target_pairs={{0,4},{4,0},{8,12},{12,8},{16,20},{20,16},{24,28},{28,24},{32,36},... | collective-permute-start | bytes 1572872 | tf_op jit(solution)/shard_map/ppermute | solution.py:37
  49.9 1.5 %collective-permute-done.14.refs_5_ = bf16[1024,256]{1,0:T(8,128)(2,1)S(1)} collective-permute-done((bf16[1024,256]{1,0:T(8,128)(2,1)S(1)}, bf16[1024,256]{1,0:T(8,128)(2,1)S(1)}, u32[]{:S(2)}, u32[]{:S(2)}) %collective-permute-start.14) | collective-permute-done | bytes 524320 | tf_op jit(solution)/shard_map/ppermute | solution.py:37
  51.5 4.4 %latent_stats.1 = (f32[3,2,8,128]{3,2,1,0:T(8,128)S(1)}, f32[2,4,4,256,256]{4,3,2,1,0:T(8,128)S(1)}, f32[2,4,4,256,256]{4,3,2,1,0:T(8,128)S(1)}) custom-call(s32[4]{0:T(128)S(1)} %pad_add_fusion.at_ref, bf16[2,256,128]{2,1,0:T(8,128)(2,1)S(1)} %get-tuple-element.40.refs_0_, bf16[2,256,128]{2,1,0:T(8,128)(2,1)S(1)} %collective-permute-done.10.refs_1_, ...), custom_call_target="tpu_custom_call" | custom-call | tf_op jit(solution)/shard_map/latent_stats/pallas_call | solution.py:219
  57.2 12.2 %all_to_all.5.refs_9_ = f32[8,3,2,8,128]{4,3,2,1,0:T(8,128)S(1)} all-to-all(f32[8,3,2,8,128]{4,3,2,1,0:T(8,128)S(1)} %broadcast_in_dim.2), channel_id=1, replica_groups={{0,32,64,96,128,160,192,224},{4,36,68,100,132,164,196,228},{8,40,72,104..., dimensions={0} | all-to-all | bytes 393216 | tf_op jit(solution)/shard_map/all_to_all | solution.py:65
  69.4 4.5 %backward.1 = (bf16[2,256,128]{2,1,0:T(8,128)(2,1)S(1)}, bf16[2,256,128]{2,1,0:T(8,128)(2,1)S(1)}, bf16[2,256,128]{2,1,0:T(8,128)(2,1)S(1)}, bf16[2,256,128]{2,1...) custom-call(s32[4]{0:T(128)S(1)} %pad_add_fusion.at_ref, ...), custom_call_target="tpu_custom_call" | custom-call | tf_op jit(solution)/shard_map/backward/pallas_call | solution.py:279
  73.9 2.0 %collective-permute-start.16 = (bf16[1024,256]{1,0:T(8,128)(2,1)S(1)}, bf16[1024,256]{1,0:T(8,128)(2,1)S(1)}, u32[]{:S(2)}, u32[]{:S(2)}) collective-permute-start(bf16[1024,256]{1,0:T(8,128)(2,1)S(1)} %get-tuple-element.51), channel_id=1, source_target_pairs={{0,4},{4,0},{8,12},{12,8},{16,20},{20,16},{24,28},{28,24},{32,36},... | collective-permute-start | bytes 1572872 | tf_op jit(solution)/shard_map/ppermute | solution.py:37
  76.0 1.5 %collective-permute-done.16 = bf16[1024,256]{1,0:T(8,128)(2,1)S(1)} collective-permute-done((bf16[1024,256]{1,0:T(8,128)(2,1)S(1)}, bf16[1024,256]{1,0:T(8,128)(2,1)S(1)}, u32[]{:S(2)}, u32[]{:S(2)}) %collective-permute-start.16) | collective-permute-done | bytes 524320 | tf_op jit(solution)/shard_map/ppermute | solution.py:37
  78.1 1.8 %collective-permute-start.18 = (bf16[2,256,128]{2,1,0:T(8,128)(2,1)S(1)}, bf16[2,256,128]{2,1,0:T(8,128)(2,1)S(1)}, u32[]{:S(2)}, u32[]{:S(2)}) collective-permute-start(bf16[2,256,128]{2,1,0:T(8,128)(2,1)S(1)} %get-tuple-element.53), channel_id=1, source_target_pairs={{0,24},{4,28},{8,0},{12,4},{16,8},{20,12},{24,16},{28,20},{32,56},... | collective-permute-start | bytes 393224 | tf_op jit(solution)/shard_map/ppermute | solution.py:51
  80.4 2.0 %collective-permute-done.18.refs_1_ = bf16[2,256,128]{2,1,0:T(8,128)(2,1)S(1)} collective-permute-done((bf16[2,256,128]{2,1,0:T(8,128)(2,1)S(1)}, bf16[2,256,128]{2,1,0:T(8,128)(2,1)S(1)}, u32[]{:S(2)}, u32[]{:S(2)}) %collective-permute-start.18) | collective-permute-done | bytes 131104 | tf_op jit(solution)/shard_map/ppermute | solution.py:51
  82.5 2.8 %collective-permute-done.19.refs_2_ = bf16[2,256,128]{2,1,0:T(8,128)(2,1)S(1)} collective-permute-done((bf16[2,256,128]{2,1,0:T(8,128)(2,1)S(1)}, bf16[2,256,128]{2,1,0:T(8,128)(2,1)S(1)}, u32[]{:S(2)}, u32[]{:S(2)}) %collective-permute-start.19) | collective-permute-done | bytes 131104 | tf_op jit(solution)/shard_map/ppermute | solution.py:51
  85.2 3.9 %collective-permute-done.20.refs_3_ = bf16[2,256,128]{2,1,0:T(8,128)(2,1)S(1)} collective-permute-done((bf16[2,256,128]{2,1,0:T(8,128)(2,1)S(1)}, bf16[2,256,128]{2,1,0:T(8,128)(2,1)S(1)}, u32[]{:S(2)}, u32[]{:S(2)}) %collective-permute-start.20) | collective-permute-done | bytes 131104 | tf_op jit(solution)/shard_map/ppermute | solution.py:51
  91.2 1.5 %collective-permute-start.24 = (bf16[128,1024]{1,0:T(8,128)(2,1)S(1)}, bf16[128,1024]{1,0:T(8,128)(2,1)S(1)}, u32[]{:S(2)}, u32[]{:S(2)}) collective-permute-start(bf16[128,1024]{1,0:T(8,128)(2,1)S(1)} %get-tuple-element.62), channel_id=1, source_target_pairs={{0,3},{1,0},{2,1},{3,2},{4,7},{5,4},{6,5},{7,6},{8,11},{9,8},{10,9... | collective-permute-start | bytes 786440 | tf_op jit(solution)/shard_map/ppermute | solution.py:41
  92.7 2.5 %context_terms.3 = (f32[256,1024]{1,0:T(8,128)S(1)}, f32[256,1024]{1,0:T(8,128)S(1)}, f32[256,1024]{1,0:T(8,128)S(1)}) custom-call(s32[4]{0:T(128)S(1)} %pad_add_fusion.at_ref, bf16[4096,512]{1,0:T(8,128)(2,1)S(1)} %get-tuple-element.38.refs_0_.wk_ref, bf16[4096,512]{1,0:T(8,128)(2,1)S(1)} %get-tuple-element.39.refs_1_.wv_ref, ...), custom_call_target="tpu_custom_call" | custom-call | tf_op jit(solution)/shard_map/context_terms/pallas_call | solution.py:317
  95.2 3.9 %collective-permute-done.21 = bf16[256,256]{1,0:T(8,128)(2,1)S(1)} collective-permute-done((bf16[256,256]{1,0:T(8,128)(2,1)S(1)}, bf16[256,256]{1,0:T(8,128)(2,1)S(1)}, u32[]{:S(2)}, u32[]{:S(2)}) %collective-permute-start.21) | collective-permute-done | bytes 131104 | tf_op jit(solution)/shard_map/ppermute | solution.py:61
  100.6 1.4 %collective-permute-start.29 = (bf16[256,1024]{1,0:T(8,128)(2,1)S(1)}, bf16[256,1024]{1,0:T(8,128)(2,1)S(1)}, u32[]{:S(2)}, u32[]{:S(2)}) collective-permute-start(bf16[256,1024]{1,0:T(8,128)(2,1)S(1)} %get-tuple-element.67), channel_id=1, source_target_pairs={{0,3},{1,0},{2,1},{3,2},{4,7},{5,4},{6,5},{7,6},{8,11},{9,8},{10,9... | collective-permute-start | bytes 1572872 | tf_op jit(solution)/shard_map/ppermute | solution.py:41
  102.2 4.2 %collective-permute-done.22 = bf16[128,256]{1,0:T(8,128)(2,1)S(1)} collective-permute-done((bf16[128,256]{1,0:T(8,128)(2,1)S(1)}, bf16[128,256]{1,0:T(8,128)(2,1)S(1)}, u32[]{:S(2)}, u32[]{:S(2)}) %collective-permute-start.22) | collective-permute-done | bytes 65568 | tf_op jit(solution)/shard_map/ppermute | solution.py:61
  106.6 2.6 %collective-permute-start.25 = (bf16[32,256]{1,0:T(8,128)(2,1)S(1)}, bf16[32,256]{1,0:T(8,128)(2,1)S(1)}, u32[]{:S(2)}, u32[]{:S(2)}) collective-permute-start(bf16[32,256]{1,0:T(8,128)(2,1)S(1)} %get-tuple-element.73), channel_id=1, source_target_pairs={{0,24},{4,28},{8,0},{12,4},{16,8},{20,12},{24,16},{28,20},{32,56},... | collective-permute-start | bytes 49160 | tf_op jit(solution)/shard_map/ppermute | solution.py:51
  109.2 1.4 %collective-permute-done.27.refs_3_ = bf16[32,256]{1,0:T(8,128)(2,1)S(1)} collective-permute-done((bf16[32,256]{1,0:T(8,128)(2,1)S(1)}, bf16[32,256]{1,0:T(8,128)(2,1)S(1)}, u32[]{:S(2)}, u32[]{:S(2)}) %collective-permute-start.27) | collective-permute-done | bytes 16416 | tf_op jit(solution)/shard_map/ppermute | solution.py:51
  112.6 2.5 %collective-permute-done.28.up_ref = bf16[256,1024]{1,0:T(8,128)(2,1)S(1)} collective-permute-done((bf16[256,1024]{1,0:T(8,128)(2,1)S(1)}, bf16[256,1024]{1,0:T(8,128)(2,1)S(1)}, u32[]{:S(2)}, u32[]{:S(2)}) %collective-permute-start.28) | collective-permute-done | bytes 524320 | tf_op jit(solution)/shard_map/ppermute | solution.py:41
  (81 shorter events, 18.6 us)
Async XLA Ops:
  0.6 3.8 %copy-start = (bf16[32,512]{1,0:T(8,128)(2,1)S(1)}, bf16[32,512]{1,0:T(8,128)(2,1)}, u32[]{:S(2)}) copy-start(bf16[32,512]{1,0:T(8,128)(2,1)} %param.9) | copy-start | bytes 98308
  0.6 19.6 %collective-permute-start.6 = (bf16[256,1024]{1,0:T(8,128)(2,1)}, bf16[256,1024]{1,0:T(8,128)(2,1)S(1)}, u32[]{:S(2)}, u32[]{:S(2)}) collective-permute-start(bf16[256,1024]{1,0:T(8,128)(2,1)} %refs_2_.1), channel_id=1, source_target_pairs={{0,1},{1,2},{2,3},{3,0},{4,5},{5,6},{6,7},{7,4},{8,9},{9,10},{10,1... | collective-permute-start | bytes 1572872 | tf_op jit(solution)/shard_map/ppermute | solution.py:41
  2.8 17.5 %collective-permute-start.8 = (bf16[256,1024]{1,0:T(8,128)(2,1)}, bf16[256,1024]{1,0:T(8,128)(2,1)S(1)}, u32[]{:S(2)}, u32[]{:S(2)}) collective-permute-start(bf16[256,1024]{1,0:T(8,128)(2,1)} %refs_2_.1), channel_id=1, source_target_pairs={{0,3},{1,0},{2,1},{3,2},{4,7},{5,4},{6,5},{7,6},{8,11},{9,8},{10,9... | collective-permute-start | bytes 1572872 | tf_op jit(solution)/shard_map/ppermute | solution.py:41
  5.2 6.0 %collective-permute-start = (bf16[32,256]{1,0:T(8,128)(2,1)S(1)}, bf16[32,256]{1,0:T(8,128)(2,1)S(1)}, u32[]{:S(2)}, u32[]{:S(2)}) collective-permute-start(bf16[32,256]{1,0:T(8,128)(2,1)S(1)} %get-tuple-element.75), channel_id=1, source_target_pairs={{0,8},{4,12},{8,16},{12,20},{16,24},{20,28},{24,0},{28,4},{32,40},... | collective-permute-start | bytes 49160 | tf_op jit(solution)/shard_map/ppermute | solution.py:51
  6.5 4.7 %collective-permute-start.1 = (bf16[32,256]{1,0:T(8,128)(2,1)S(1)}, bf16[32,256]{1,0:T(8,128)(2,1)S(1)}, u32[]{:S(2)}, u32[]{:S(2)}) collective-permute-start(bf16[32,256]{1,0:T(8,128)(2,1)S(1)} %get-tuple-element.76), channel_id=1, source_target_pairs={{0,16},{4,20},{8,24},{12,28},{16,0},{20,4},{24,8},{28,12},{32,48},... | collective-permute-start | bytes 49160 | tf_op jit(solution)/shard_map/ppermute | solution.py:51
  9.0 2.9 %collective-permute-start.2 = (bf16[32,256]{1,0:T(8,128)(2,1)S(1)}, bf16[32,256]{1,0:T(8,128)(2,1)S(1)}, u32[]{:S(2)}, u32[]{:S(2)}) collective-permute-start(bf16[32,256]{1,0:T(8,128)(2,1)S(1)} %get-tuple-element.77), channel_id=1, source_target_pairs={{0,24},{4,28},{8,0},{12,4},{16,8},{20,12},{24,16},{28,20},{32,56},... | collective-permute-start | bytes 49160 | tf_op jit(solution)/shard_map/ppermute | solution.py:51
  11.9 15.0 %collective-permute-start.5 = (bf16[128,256]{1,0:T(8,128)(2,1)S(1)}, bf16[128,256]{1,0:T(8,128)(2,1)S(1)}, u32[]{:S(2)}, u32[]{:S(2)}) collective-permute-start(bf16[128,256]{1,0:T(8,128)(2,1)S(1)} %pad_maximum_fusion), channel_id=1, source_target_pairs={{0,192},{4,196},{8,200},{12,204},{16,208},{20,212},{24,216},{28,22... | collective-permute-start | bytes 196616 | tf_op jit(solution)/shard_map/ppermute | solution.py:61
  18.0 8.9 %collective-permute-start.4 = (bf16[128,256]{1,0:T(8,128)(2,1)S(1)}, bf16[128,256]{1,0:T(8,128)(2,1)S(1)}, u32[]{:S(2)}, u32[]{:S(2)}) collective-permute-start(bf16[128,256]{1,0:T(8,128)(2,1)S(1)} %pad_maximum_fusion), channel_id=1, source_target_pairs={{0,64},{4,68},{8,72},{12,76},{16,80},{20,84},{24,88},{28,92},{32,9... | collective-permute-start | bytes 196616 | tf_op jit(solution)/shard_map/ppermute | solution.py:61
  19.2 7.7 %collective-permute-start.3 = (bf16[128,256]{1,0:T(8,128)(2,1)S(1)}, bf16[128,256]{1,0:T(8,128)(2,1)S(1)}, u32[]{:S(2)}, u32[]{:S(2)}) collective-permute-start(bf16[128,256]{1,0:T(8,128)(2,1)S(1)} %pad_maximum_fusion), channel_id=1, source_target_pairs={{0,128},{4,132},{8,136},{12,140},{16,144},{20,148},{24,152},{28,15... | collective-permute-start | bytes 196616 | tf_op jit(solution)/shard_map/ppermute | solution.py:61
  20.2 14.6 %collective-permute-start.7 = (bf16[128,1024]{1,0:T(8,128)(2,1)S(1)}, bf16[128,1024]{1,0:T(8,128)(2,1)S(1)}, u32[]{:S(2)}, u32[]{:S(2)}) collective-permute-start(bf16[128,1024]{1,0:T(8,128)(2,1)S(1)} %slice.93), channel_id=1, source_target_pairs={{0,1},{1,2},{2,3},{3,0},{4,5},{5,6},{6,7},{7,4},{8,9},{9,10},{10,1... | collective-permute-start | bytes 786440 | tf_op jit(solution)/shard_map/ppermute | solution.py:41
  20.4 14.5 %collective-permute-start.9 = (bf16[128,1024]{1,0:T(8,128)(2,1)S(1)}, bf16[128,1024]{1,0:T(8,128)(2,1)S(1)}, u32[]{:S(2)}, u32[]{:S(2)}) collective-permute-start(bf16[128,1024]{1,0:T(8,128)(2,1)S(1)} %slice.94), channel_id=1, source_target_pairs={{0,3},{1,0},{2,1},{3,2},{4,7},{5,4},{6,5},{7,6},{8,11},{9,8},{10,9... | collective-permute-start | bytes 786440 | tf_op jit(solution)/shard_map/ppermute | solution.py:41
  26.9 2.2 %copy-start.1 = (bf16[4096,512]{1,0:T(8,128)(2,1)S(1)}, bf16[4096,512]{1,0:T(8,128)(2,1)}, u32[]{:S(2)}) copy-start(bf16[4096,512]{1,0:T(8,128)(2,1)} %refs_0_.1) | copy-start | bytes 12582916
  34.8 5.3 %collective-permute-start.13 = (bf16[512,256]{1,0:T(8,128)(2,1)S(1)}, bf16[512,256]{1,0:T(8,128)(2,1)S(1)}, u32[]{:S(2)}, u32[]{:S(2)}) collective-permute-start(bf16[512,256]{1,0:T(8,128)(2,1)S(1)} %constant_dynamic-update-slice_fusion), channel_id=1, source_target_pairs={{0,32},{4,36},{8,40},{12,44},{16,48},{20,52},{24,56},{28,60},{32,0... | collective-permute-start | bytes 786440 | tf_op jit(solution)/shard_map/ppermute | solution.py:61
  36.4 5.1 %collective-permute-start.10 = (bf16[2,256,128]{2,1,0:T(8,128)(2,1)S(1)}, bf16[2,256,128]{2,1,0:T(8,128)(2,1)S(1)}, u32[]{:S(2)}, u32[]{:S(2)}) collective-permute-start(bf16[2,256,128]{2,1,0:T(8,128)(2,1)S(1)} %get-tuple-element.41), channel_id=1, source_target_pairs={{0,8},{4,12},{8,16},{12,20},{16,24},{20,28},{24,0},{28,4},{32,40},... | collective-permute-start | bytes 393224 | tf_op jit(solution)/shard_map/ppermute | solution.py:51
  36.8 7.1 %collective-permute-start.11 = (bf16[2,256,128]{2,1,0:T(8,128)(2,1)S(1)}, bf16[2,256,128]{2,1,0:T(8,128)(2,1)S(1)}, u32[]{:S(2)}, u32[]{:S(2)}) collective-permute-start(bf16[2,256,128]{2,1,0:T(8,128)(2,1)S(1)} %get-tuple-element.42), channel_id=1, source_target_pairs={{0,16},{4,20},{8,24},{12,28},{16,0},{20,4},{24,8},{28,12},{32,48},... | collective-permute-start | bytes 393224 | tf_op jit(solution)/shard_map/ppermute | solution.py:51
  40.1 4.1 %collective-permute-start.12 = (bf16[2,256,128]{2,1,0:T(8,128)(2,1)S(1)}, bf16[2,256,128]{2,1,0:T(8,128)(2,1)S(1)}, u32[]{:S(2)}, u32[]{:S(2)}) collective-permute-start(bf16[2,256,128]{2,1,0:T(8,128)(2,1)S(1)} %get-tuple-element.43), channel_id=1, source_target_pairs={{0,24},{4,28},{8,0},{12,4},{16,8},{20,12},{24,16},{28,20},{32,56},... | collective-permute-start | bytes 393224 | tf_op jit(solution)/shard_map/ppermute | solution.py:51
  44.2 7.2 %collective-permute-start.14 = (bf16[1024,256]{1,0:T(8,128)(2,1)S(1)}, bf16[1024,256]{1,0:T(8,128)(2,1)S(1)}, u32[]{:S(2)}, u32[]{:S(2)}) collective-permute-start(bf16[1024,256]{1,0:T(8,128)(2,1)S(1)} %constant_dynamic-update-slice_fusion.7.refs_4_), channel_id=1, source_target_pairs={{0,4},{4,0},{8,12},{12,8},{16,20},{20,16},{24,28},{28,24},{32,36},... | collective-permute-start | bytes 1572872 | tf_op jit(solution)/shard_map/ppermute | solution.py:37
  55.8 1.3 %collective-permute-start.15 = (f32[3,2,8,128]{3,2,1,0:T(8,128)S(1)}, f32[3,2,8,128]{3,2,1,0:T(8,128)S(1)}, u32[]{:S(2)}, u32[]{:S(2)}) collective-permute-start(f32[3,2,8,128]{3,2,1,0:T(8,128)S(1)} %get-tuple-element.49.refs_8_), channel_id=1, source_target_pairs={{0,4},{4,0},{8,12},{12,8},{16,20},{20,16},{24,28},{28,24},{32,36},... | collective-permute-start | bytes 73736 | tf_op jit(solution)/shard_map/ppermute | solution.py:37
  73.9 3.6 %collective-permute-start.16 = (bf16[1024,256]{1,0:T(8,128)(2,1)S(1)}, bf16[1024,256]{1,0:T(8,128)(2,1)S(1)}, u32[]{:S(2)}, u32[]{:S(2)}) collective-permute-start(bf16[1024,256]{1,0:T(8,128)(2,1)S(1)} %get-tuple-element.51), channel_id=1, source_target_pairs={{0,4},{4,0},{8,12},{12,8},{16,20},{20,16},{24,28},{28,24},{32,36},... | collective-permute-start | bytes 1572872 | tf_op jit(solution)/shard_map/ppermute | solution.py:37
  77.7 12.8 %collective-permute-start.17 = (bf16[512,256]{1,0:T(8,128)(2,1)S(1)}, bf16[512,256]{1,0:T(8,128)(2,1)S(1)}, u32[]{:S(2)}, u32[]{:S(2)}) collective-permute-start(bf16[512,256]{1,0:T(8,128)(2,1)S(1)} %slice.136), channel_id=1, source_target_pairs={{0,32},{4,36},{8,40},{12,44},{16,48},{20,52},{24,56},{28,60},{32,0... | collective-permute-start | bytes 786440 | tf_op jit(solution)/shard_map/ppermute | solution.py:61
  78.1 4.4 %collective-permute-start.18 = (bf16[2,256,128]{2,1,0:T(8,128)(2,1)S(1)}, bf16[2,256,128]{2,1,0:T(8,128)(2,1)S(1)}, u32[]{:S(2)}, u32[]{:S(2)}) collective-permute-start(bf16[2,256,128]{2,1,0:T(8,128)(2,1)S(1)} %get-tuple-element.53), channel_id=1, source_target_pairs={{0,24},{4,28},{8,0},{12,4},{16,8},{20,12},{24,16},{28,20},{32,56},... | collective-permute-start | bytes 393224 | tf_op jit(solution)/shard_map/ppermute | solution.py:51
  79.8 5.4 %collective-permute-start.19 = (bf16[2,256,128]{2,1,0:T(8,128)(2,1)S(1)}, bf16[2,256,128]{2,1,0:T(8,128)(2,1)S(1)}, u32[]{:S(2)}, u32[]{:S(2)}) collective-permute-start(bf16[2,256,128]{2,1,0:T(8,128)(2,1)S(1)} %get-tuple-element.54), channel_id=1, source_target_pairs={{0,16},{4,20},{8,24},{12,28},{16,0},{20,4},{24,8},{28,12},{32,48},... | collective-permute-start | bytes 393224 | tf_op jit(solution)/shard_map/ppermute | solution.py:51
  79.9 9.2 %collective-permute-start.20 = (bf16[2,256,128]{2,1,0:T(8,128)(2,1)S(1)}, bf16[2,256,128]{2,1,0:T(8,128)(2,1)S(1)}, u32[]{:S(2)}, u32[]{:S(2)}) collective-permute-start(bf16[2,256,128]{2,1,0:T(8,128)(2,1)S(1)} %get-tuple-element.55), channel_id=1, source_target_pairs={{0,8},{4,12},{8,16},{12,20},{16,24},{20,28},{24,0},{28,4},{32,40},... | collective-permute-start | bytes 393224 | tf_op jit(solution)/shard_map/ppermute | solution.py:51
  90.6 8.5 %collective-permute-start.21 = (bf16[256,256]{1,0:T(8,128)(2,1)S(1)}, bf16[256,256]{1,0:T(8,128)(2,1)S(1)}, u32[]{:S(2)}, u32[]{:S(2)}) collective-permute-start(bf16[256,256]{1,0:T(8,128)(2,1)S(1)} %slice.137), channel_id=1, source_target_pairs={{0,64},{4,68},{8,72},{12,76},{16,80},{20,84},{24,88},{28,92},{32,9... | collective-permute-start | bytes 393224 | tf_op jit(solution)/shard_map/ppermute | solution.py:61
  91.2 9.1 %collective-permute-start.24 = (bf16[128,1024]{1,0:T(8,128)(2,1)S(1)}, bf16[128,1024]{1,0:T(8,128)(2,1)S(1)}, u32[]{:S(2)}, u32[]{:S(2)}) collective-permute-start(bf16[128,1024]{1,0:T(8,128)(2,1)S(1)} %get-tuple-element.62), channel_id=1, source_target_pairs={{0,3},{1,0},{2,1},{3,2},{4,7},{5,4},{6,5},{7,6},{8,11},{9,8},{10,9... | collective-permute-start | bytes 786440 | tf_op jit(solution)/shard_map/ppermute | solution.py:41
  92.7 7.7 %collective-permute-start.23 = (bf16[128,1024]{1,0:T(8,128)(2,1)S(1)}, bf16[128,1024]{1,0:T(8,128)(2,1)S(1)}, u32[]{:S(2)}, u32[]{:S(2)}) collective-permute-start(bf16[128,1024]{1,0:T(8,128)(2,1)S(1)} %get-tuple-element.56), channel_id=1, source_target_pairs={{0,1},{1,2},{2,3},{3,0},{4,5},{5,6},{6,7},{7,4},{8,9},{9,10},{10,1... | collective-permute-start | bytes 786440 | tf_op jit(solution)/shard_map/ppermute | solution.py:41
  99.2 7.3 %collective-permute-start.22 = (bf16[128,256]{1,0:T(8,128)(2,1)S(1)}, bf16[128,256]{1,0:T(8,128)(2,1)S(1)}, u32[]{:S(2)}, u32[]{:S(2)}) collective-permute-start(bf16[128,256]{1,0:T(8,128)(2,1)S(1)} %slice.138), channel_id=1, source_target_pairs={{0,128},{4,132},{8,136},{12,140},{16,144},{20,148},{24,152},{28,15... | collective-permute-start | bytes 196616 | tf_op jit(solution)/shard_map/ppermute | solution.py:61
  100.6 11.9 %collective-permute-start.29 = (bf16[256,1024]{1,0:T(8,128)(2,1)S(1)}, bf16[256,1024]{1,0:T(8,128)(2,1)S(1)}, u32[]{:S(2)}, u32[]{:S(2)}) collective-permute-start(bf16[256,1024]{1,0:T(8,128)(2,1)S(1)} %get-tuple-element.67), channel_id=1, source_target_pairs={{0,3},{1,0},{2,1},{3,2},{4,7},{5,4},{6,5},{7,6},{8,11},{9,8},{10,9... | collective-permute-start | bytes 1572872 | tf_op jit(solution)/shard_map/ppermute | solution.py:41
  102.0 13.0 %collective-permute-start.28 = (bf16[256,1024]{1,0:T(8,128)(2,1)S(1)}, bf16[256,1024]{1,0:T(8,128)(2,1)S(1)}, u32[]{:S(2)}, u32[]{:S(2)}) collective-permute-start(bf16[256,1024]{1,0:T(8,128)(2,1)S(1)} %get-tuple-element.63), channel_id=1, source_target_pairs={{0,1},{1,2},{2,3},{3,0},{4,5},{5,6},{6,7},{7,4},{8,9},{9,10},{10,1... | collective-permute-start | bytes 1572872 | tf_op jit(solution)/shard_map/ppermute | solution.py:41
  106.4 4.2 %collective-permute-start.27 = (bf16[32,256]{1,0:T(8,128)(2,1)S(1)}, bf16[32,256]{1,0:T(8,128)(2,1)S(1)}, u32[]{:S(2)}, u32[]{:S(2)}) collective-permute-start(bf16[32,256]{1,0:T(8,128)(2,1)S(1)} %get-tuple-element.71), channel_id=1, source_target_pairs={{0,8},{4,12},{8,16},{12,20},{16,24},{20,28},{24,0},{28,4},{32,40},... | collective-permute-start | bytes 49160 | tf_op jit(solution)/shard_map/ppermute | solution.py:51
  106.5 4.2 %collective-permute-start.26 = (bf16[32,256]{1,0:T(8,128)(2,1)S(1)}, bf16[32,256]{1,0:T(8,128)(2,1)S(1)}, u32[]{:S(2)}, u32[]{:S(2)}) collective-permute-start(bf16[32,256]{1,0:T(8,128)(2,1)S(1)} %get-tuple-element.72), channel_id=1, source_target_pairs={{0,16},{4,20},{8,24},{12,28},{16,0},{20,4},{24,8},{28,12},{32,48},... | collective-permute-start | bytes 49160 | tf_op jit(solution)/shard_map/ppermute | solution.py:51
  106.6 4.7 %collective-permute-start.25 = (bf16[32,256]{1,0:T(8,128)(2,1)S(1)}, bf16[32,256]{1,0:T(8,128)(2,1)S(1)}, u32[]{:S(2)}, u32[]{:S(2)}) collective-permute-start(bf16[32,256]{1,0:T(8,128)(2,1)S(1)} %get-tuple-element.73), channel_id=1, source_target_pairs={{0,24},{4,28},{8,0},{12,4},{16,8},{20,12},{24,16},{28,20},{32,56},... | collective-permute-start | bytes 49160 | tf_op jit(solution)/shard_map/ppermute | solution.py:51
  (2 other events, 3.3 us)
